TPU v7x, 32 devices: a whole 2x2x4 slice. The times are simulated.
32 devices in a mesh: dp: 4 (over z), chan: 8 (over y, x, core).
Axes of the slice: x: 2, y: 2, z: 4, core: 2. Of those that a mesh axis runs over, the one named last changes fastest.
Arguments:
- tokens: bfloat16 [3, 8192, 512], P(None, ('dp', 'chan')), may hold values from -6 to 6
- cotangent: bfloat16 [3, 8192, 512], P(None, ('dp', 'chan')), may hold values from -6 to 6
- lengths: int32 [3, 4], P(None, 'dp'), may hold values from 1024 to 2048, as said below
- norm_gain: bfloat16 [512], P(('dp', 'chan')), may hold values from 0.5 to 1.5
- log_step: float32 [512], P('chan'), may hold values from -6.9 to -2.3
- log_decay: float32 [512, 32], P('chan', 'dp'), may hold values from -1.5 to 0.5
- frequency: float32 [512, 32], P('chan', 'dp'), may hold values from 0 to 100
- readout_real: float32 [512, 32], P('chan', 'dp'), may hold values from -4 to 4
- readout_imaginary: float32 [512, 32], P('chan', 'dp'), may hold values from -4 to 4
- skip_gain: float32 [512], P('chan'), may hold values from -4 to 4
- out_weight: bfloat16 [512, 1024], P(('dp', 'chan')), may hold values from -0.25 to 0.25
- out_bias: bfloat16 [1024], P(('dp', 'chan')), may hold values from -3 to 3
- ffn_gain: bfloat16 [512], P(('dp', 'chan')), may hold values from 0.5 to 1.5
- in_weight: bfloat16 [512, 2048], P(('dp', 'chan')), may hold values from -0.25 to 0.25
- in_bias: bfloat16 [2048], P(('dp', 'chan')), may hold values from -3 to 3
- back_weight: bfloat16 [2048, 512], P(('dp', 'chan')), may hold values from -0.125 to 0.125
Outputs:
- block_out: bfloat16 [3, 8192, 512], P(None, ('dp', 'chan'))
- grad_tokens: bfloat16 [3, 8192, 512], P(None, ('dp', 'chan'))
- grad_norm_gain: float32 [512], P(('dp', 'chan'))
- grad_log_step: float32 [512], P('chan')
- grad_log_decay: float32 [512, 32], P('chan', 'dp')
- grad_frequency: float32 [512, 32], P('chan', 'dp')
- grad_readout_real: float32 [512, 32], P('chan', 'dp')
- grad_readout_imaginary: float32 [512, 32], P('chan', 'dp')
- grad_skip_gain: float32 [512], P('chan')
- grad_out_weight: float32 [512, 1024], P(('dp', 'chan'))
- grad_out_bias: float32 [1024], P(('dp', 'chan'))
- grad_ffn_gain: float32 [512], P(('dp', 'chan'))
- grad_in_weight: float32 [512, 2048], P(('dp', 'chan'))
- grad_in_bias: float32 [2048], P(('dp', 'chan'))
- grad_back_weight: float32 [2048, 512], P(('dp', 'chan'))
Inputs may be any that keep to these rules, and one draw needn't show every extreme that they name: `lengths`: each entry is 2048 divided by a power of two; in every group some micro-batch has length 2048.
All inputs are finite; a program needn't handle non-finite values.
Results may differ from a plain program's by a relative error of at most 0.0088.
Values may be sent and summed in bfloat16 or wider, within the bound.
A program may use at most 320 MiB of HBM per device.

v0:
```python
import jax
import jax.numpy as jnp
from jax import lax
from jax.sharding import PartitionSpec as P


def layer_norm(values, gain_vector):
    average = jnp.mean(values, axis=-1, keepdims=True)
    centred = values - average
    spread = jnp.mean(centred * centred, axis=-1, keepdims=True)
    return centred * lax.rsqrt(spread + 1e-05) * gain_vector


def exact_gelu(values):
    return jax.nn.gelu(values, approximate=False)


def gate_mix(project):
    features = project.shape[1] // 2
    return project[:, :features] * jax.nn.sigmoid(project[:, features:])


def matmul(former, latter):
    return jnp.dot(former, latter, preferred_element_type=jnp.float32)


def outer_sum(former, latter):
    return lax.dot_general(
        former, latter, (((0,), (0,)), ((), ())), preferred_element_type=jnp.float32
    )


def back_product(former, latter):
    return lax.dot_general(
        former, latter, (((1,), (1,)), ((), ())), preferred_element_type=jnp.float32
    )


def add_up(running, addition):
    if running is None:
        return addition
    return tuple((former + latter for former, latter in zip(running, addition)))


def mode_powers(damping, rotation, offsets):
    shaped = offsets[..., None, None]
    magnitude = jnp.exp(shaped * damping)
    return (magnitude * jnp.cos(shaped * rotation), magnitude * jnp.sin(shaped * rotation))


def lower_toeplitz(kernel):
    block_size, channels = kernel.shape
    zero_part = jnp.zeros((block_size, channels), kernel.dtype)
    row_base = jnp.concatenate([kernel[0:1], zero_part, kernel[1:][::-1]], axis=0)
    tiled = jnp.broadcast_to(row_base[None], (block_size, 2 * block_size, channels))
    flat = tiled.reshape(2 * block_size * block_size, channels)[: block_size * (2 * block_size - 1)]
    return flat.reshape(block_size, 2 * block_size - 1, channels)[:, :block_size]


def state_mix(
    inputs, length, log_step, log_decay, frequency, readout_real, readout_imaginary, skip_gain
):
    positions, channels = inputs.shape
    block_size = min(256, positions)
    blocks = positions // block_size
    highest = lax.Precision.HIGHEST
    step_size = jnp.exp(log_step)[:, None]
    real_rate = -jnp.exp(log_decay)
    damping = step_size * real_rate
    rotation = step_size * frequency
    shrink = jnp.exp(damping)
    above_real = shrink * jnp.cos(rotation) - 1.0
    above_imag = shrink * jnp.sin(rotation)
    modulus = real_rate * real_rate + frequency * frequency
    ratio_real = (above_real * real_rate + above_imag * frequency) / modulus
    ratio_imag = (above_imag * real_rate - above_real * frequency) / modulus
    weight_real = readout_real * ratio_real - readout_imaginary * ratio_imag
    weight_imag = readout_real * ratio_imag + readout_imaginary * ratio_real
    offsets = jnp.arange(block_size + 1).astype(jnp.float32)
    power_real, power_imag = mode_powers(damping, rotation, offsets)
    kernel = 2.0 * (
        jnp.sum(power_real[:block_size] * weight_real, axis=-1)
        - jnp.sum(power_imag[:block_size] * weight_imag, axis=-1)
    )
    places = jnp.arange(block_size)
    distance = places[:, None] - places[None, :]
    inside = (distance >= 0) & (places[:, None] // length == places[None, :] // length)
    toeplitz = jnp.where(inside[:, :, None], lower_toeplitz(kernel), 0.0)
    shaped = inputs.reshape(blocks, block_size, channels)
    within = jnp.einsum("tsc,bsc->btc", toeplitz, shaped, precision=highest)
    reverse_real = power_real[:block_size][::-1]
    reverse_imag = power_imag[:block_size][::-1]
    state_real = jnp.einsum("bsc,scn->bcn", shaped, reverse_real, precision=highest)
    state_imag = jnp.einsum("bsc,scn->bcn", shaped, reverse_imag, precision=highest)
    block_ids = jnp.arange(blocks)
    sequence = block_ids * block_size // length
    block_gap = block_ids[:, None] - 1 - block_ids[None, :]
    linked = (block_gap >= 0) & (sequence[:, None] == sequence[None, :])
    hop_real, hop_imag = mode_powers(
        damping, rotation, (jnp.maximum(block_gap, 0) * block_size).astype(jnp.float32)
    )
    hop_real = jnp.where(linked[:, :, None, None], hop_real, 0.0)
    hop_imag = jnp.where(linked[:, :, None, None], hop_imag, 0.0)
    carry_real = jnp.einsum("ijcn,jcn->icn", hop_real, state_real, precision=highest) - jnp.einsum(
        "ijcn,jcn->icn", hop_imag, state_imag, precision=highest
    )
    carry_imag = jnp.einsum("ijcn,jcn->icn", hop_real, state_imag, precision=highest) + jnp.einsum(
        "ijcn,jcn->icn", hop_imag, state_real, precision=highest
    )
    read_real = power_real[1:] * weight_real - power_imag[1:] * weight_imag
    read_imag = power_real[1:] * weight_imag + power_imag[1:] * weight_real
    across = 2.0 * (
        jnp.einsum("tcn,icn->itc", read_real, carry_real, precision=highest)
        - jnp.einsum("tcn,icn->itc", read_imag, carry_imag, precision=highest)
    )
    return (within + across).reshape(positions, channels) + skip_gain * inputs


def on_device(
    tokens,
    cotangent,
    lengths,
    norm_gain,
    log_step,
    log_decay,
    frequency,
    readout_real,
    readout_imaginary,
    skip_gain,
    out_weight,
    out_bias,
    ffn_gain,
    in_weight,
    in_bias,
    back_weight,
):
    dense_total = None
    mode_total = None
    outputs = []
    input_grads = []
    for micro_batch in range(tokens.shape[0]):
        dense_set = (
            lax.all_gather(out_weight, ("dp", "chan"), axis=0, tiled=True),
            lax.all_gather(out_bias, ("dp", "chan"), axis=0, tiled=True),
            lax.all_gather(norm_gain, ("dp", "chan"), axis=0, tiled=True),
            lax.all_gather(ffn_gain, ("dp", "chan"), axis=0, tiled=True),
            lax.all_gather(in_weight, ("dp", "chan"), axis=0, tiled=True),
            lax.all_gather(in_bias, ("dp", "chan"), axis=0, tiled=True),
            lax.all_gather(back_weight, ("dp", "chan"), axis=0, tiled=True),
        )
        mode_set = (
            lax.all_gather(log_decay, "dp", axis=1, tiled=True),
            lax.all_gather(frequency, "dp", axis=1, tiled=True),
            lax.all_gather(readout_real, "dp", axis=1, tiled=True),
            lax.all_gather(readout_imaginary, "dp", axis=1, tiled=True),
        )
        w_out, b_out, gain_one, gain_two, w_in, b_in, w_back = dense_set
        decay_full, frequency_full, real_full, imag_full = mode_set
        row_block = tokens[micro_batch].astype(jnp.float32)
        normed, norm_pull = jax.vjp(layer_norm, row_block, gain_one.astype(jnp.float32))
        channel_in = lax.all_to_all(
            normed.astype(jnp.bfloat16), "chan", split_axis=1, concat_axis=0, tiled=True
        )
        group_length = lengths[micro_batch, 0]

        def local_mix(
            values, step_part, decay_part, frequency_part, real_part, imag_part, skip_part
        ):
            return exact_gelu(
                state_mix(
                    values,
                    group_length,
                    step_part,
                    decay_part,
                    frequency_part,
                    real_part,
                    imag_part,
                    skip_part,
                )
            )

        activated, mix_pull = jax.vjp(
            local_mix,
            channel_in.astype(jnp.float32),
            log_step,
            decay_full,
            frequency_full,
            real_full,
            imag_full,
            skip_gain,
        )
        act_rows = lax.all_to_all(
            activated.astype(jnp.bfloat16), "chan", split_axis=0, concat_axis=1, tiled=True
        )
        project = matmul(act_rows, w_out) + b_out.astype(jnp.float32)
        gated, gate_pull = jax.vjp(gate_mix, project)
        middle = row_block + gated
        second_float, second_pull = jax.vjp(layer_norm, middle, gain_two.astype(jnp.float32))
        second = second_float.astype(jnp.bfloat16)
        before = matmul(second, w_in) + b_in.astype(jnp.float32)
        hidden_float, hidden_pull = jax.vjp(exact_gelu, before)
        hidden = hidden_float.astype(jnp.bfloat16)
        outputs.append((middle + matmul(hidden, w_back)).astype(jnp.bfloat16))
        upstream = cotangent[micro_batch]
        grad_back = outer_sum(hidden, upstream)
        grad_before = hidden_pull(back_product(upstream, w_back))[0].astype(jnp.bfloat16)
        grad_in = outer_sum(second, grad_before)
        grad_in_bias = jnp.sum(grad_before.astype(jnp.float32), axis=0)
        grad_middle, grad_gain_two = second_pull(back_product(grad_before, w_in))
        grad_middle = grad_middle + upstream.astype(jnp.float32)
        grad_project = gate_pull(grad_middle)[0].astype(jnp.bfloat16)
        grad_out = outer_sum(act_rows, grad_project)
        grad_out_bias = jnp.sum(grad_project.astype(jnp.float32), axis=0)
        grad_act = back_product(grad_project, w_out).astype(jnp.bfloat16)
        channel_grad = lax.all_to_all(grad_act, "chan", split_axis=1, concat_axis=0, tiled=True)
        mode_grads = mix_pull(channel_grad.astype(jnp.float32))
        row_grad = lax.all_to_all(
            mode_grads[0].astype(jnp.bfloat16), "chan", split_axis=0, concat_axis=1, tiled=True
        )
        grad_rows_part, grad_gain_one = norm_pull(row_grad.astype(jnp.float32))
        input_grads.append((grad_rows_part + grad_middle).astype(jnp.bfloat16))
        dense_local = (
            grad_out,
            grad_out_bias,
            grad_gain_one,
            grad_gain_two,
            grad_in,
            grad_in_bias,
            grad_back,
        )
        mode_local = (
            mode_grads[2],
            mode_grads[3],
            mode_grads[4],
            mode_grads[5],
            mode_grads[1],
            mode_grads[6],
        )
        dense_total = add_up(
            dense_total,
            (
                lax.psum_scatter(dense_local[0], ("dp", "chan"), scatter_dimension=0, tiled=True),
                lax.psum_scatter(dense_local[1], ("dp", "chan"), scatter_dimension=0, tiled=True),
                lax.psum_scatter(dense_local[2], ("dp", "chan"), scatter_dimension=0, tiled=True),
                lax.psum_scatter(dense_local[3], ("dp", "chan"), scatter_dimension=0, tiled=True),
                lax.psum_scatter(dense_local[4], ("dp", "chan"), scatter_dimension=0, tiled=True),
                lax.psum_scatter(dense_local[5], ("dp", "chan"), scatter_dimension=0, tiled=True),
                lax.psum_scatter(dense_local[6], ("dp", "chan"), scatter_dimension=0, tiled=True),
            ),
        )
        summed = lax.psum(
            (
                mode_local[0],
                mode_local[1],
                mode_local[2],
                mode_local[3],
                mode_local[4],
                mode_local[5],
            ),
            "dp",
        )
        quarter = log_decay.shape[1]
        first_mode = lax.axis_index("dp") * quarter
        sliced = tuple(
            (lax.dynamic_slice_in_dim(member, first_mode, quarter, 1) for member in summed[:4])
        )
        mode_total = add_up(mode_total, sliced + (summed[4], summed[5]))
    return (
        jnp.stack(outputs),
        jnp.stack(input_grads),
        dense_total[2],
        mode_total[4],
        mode_total[0],
        mode_total[1],
        mode_total[2],
        mode_total[3],
        mode_total[5],
        dense_total[0],
        dense_total[1],
        dense_total[3],
        dense_total[4],
        dense_total[5],
        dense_total[6],
    )


def solution(mesh):
    placed = (
        P(None, ("dp", "chan"), None),
        P(None, ("dp", "chan"), None),
        P(None, "dp"),
        P(("dp", "chan")),
        P("chan"),
        P("chan", "dp"),
        P("chan", "dp"),
        P("chan", "dp"),
        P("chan", "dp"),
        P("chan"),
        P(("dp", "chan"), None),
        P(("dp", "chan")),
        P(("dp", "chan")),
        P(("dp", "chan"), None),
        P(("dp", "chan")),
        P(("dp", "chan"), None),
    )
    return jax.shard_map(
        on_device,
        mesh=mesh,
        in_specs=placed,
        out_specs=(
            P(None, ("dp", "chan"), None),
            P(None, ("dp", "chan"), None),
            P(("dp", "chan")),
            P("chan"),
            P("chan", "dp"),
            P("chan", "dp"),
            P("chan", "dp"),
            P("chan", "dp"),
            P("chan"),
            P(("dp", "chan"), None),
            P(("dp", "chan")),
            P(("dp", "chan")),
            P(("dp", "chan"), None),
            P(("dp", "chan")),
            P(("dp", "chan"), None),
        ),
        check_vma=False,
    )
```

profile of v0, /device:TPU:0, one launch (start us, length us, event | category | flops | bytes accessed | tf_op | source)
XLA Modules:
  0.0 1166.5 jit_solution(5383290621581542497)
XLA Ops:
  10.5 42.1 %all-reduce.49 = (bf16[512]{0:T(512)(128)(2,1)S(1)}, bf16[1024]{0:T(1024)(128)(2,1)}, bf16[2048]{0:T(1024)(128)(2,1)}, bf16[512]{0:T(512)(128)(2,1)}) all-reduce(bf16[512]{0:T(512)(128)(2,1)S(1)} %dynamic-update-slice, bf16[1024]{0:T(1024)(128)(2,1)S(1)} %dynamic-update-slice.1, ...), channel_id=1, replica_groups=mesh['dp'=4,'chan'=8] {'dp','chan'}, use_global_device_ids=true, to_apply=%add.39 | all-reduce | flops 4096 | bytes 16384
  60.8 13.1 %all_gather.24 = f32[64,32]{0,1:T(8,128)S(1)} all-gather(f32[64,8]{0,1:T(8,128)S(1)} %copy-done.256), channel_id=1, replica_groups=mesh['dp'=4,'chan'=8] {'dp'}, dimensions={1}, use_global_device_ids=true | all-gather | bytes 10240 | tf_op jit(solution)/shard_map/all_gather | solution.py:153
  76.2 13.2 %all_gather.26 = f32[64,32]{0,1:T(8,128)S(1)} all-gather(f32[64,8]{0,1:T(8,128)S(1)} %copy-done.257), channel_id=1, replica_groups=mesh['dp'=4,'chan'=8] {'dp'}, dimensions={1}, use_global_device_ids=true | all-gather | bytes 10240 | tf_op jit(solution)/shard_map/all_gather | solution.py:155
  89.4 13.1 %all_gather.25 = f32[64,32]{0,1:T(8,128)S(1)} all-gather(f32[64,8]{0,1:T(8,128)S(1)} %copy-done.258), channel_id=1, replica_groups=mesh['dp'=4,'chan'=8] {'dp'}, dimensions={1}, use_global_device_ids=true | all-gather | bytes 10240 | tf_op jit(solution)/shard_map/all_gather | solution.py:154
  102.5 13.5 %all_gather.23 = f32[64,32]{0,1:T(8,128)S(1)} all-gather(f32[64,8]{0,1:T(8,128)S(1)} %copy-done.259), channel_id=1, replica_groups=mesh['dp'=4,'chan'=8] {'dp'}, dimensions={1}, use_global_device_ids=true | all-gather | bytes 10240 | tf_op jit(solution)/shard_map/all_gather | solution.py:152
  117.7 11.6 fusion.43
  129.5 4.8 multiply_add_fusion
  143.1 4.3 broadcast_in_dim.138
  147.4 21.5 %copy.557 = f32[8,8,256,512]{3,1,2,0:T(8,128)} copy(f32[8,8,256,512]{3,2,1,0:T(8,128)S(1)} %bitcast.708) | data formatting | bytes 67108864
  168.9 22.6 %slice.142 = f32[130816,64]{0,1:T(8,128)} slice(f32[131072,64]{0,1:T(8,128)} %bitcast.711), slice={[0:130816], [0:64]} | slice | bytes 66977792 | tf_op jit(solution)/shard_map/jvp()/slice | solution.py:56
  191.5 45.5 %reshape.1079 = f32[256,511,64]{1,0,2:T(8,128)} reshape(f32[130816,64]{0,1:T(8,128)} %slice.142) | data formatting | bytes 66977792 | tf_op jit(solution)/shard_map/jvp()/reshape | solution.py:57
  239.7 4.6 rev.44
  244.5 4.2 all-to-all-start.2
  273.5 8.1 multiply_reduce_fusion.31
  305.5 12.4 %fusion.6 = f32[64,8,256]{2,1,0:T(8,128)S(1)} fusion(f32[256,511,64]{1,0,2:T(8,128)} %reshape.1079, pred[256,256]{1,0:T(8,128)(4,1)S(1)} %fusion.379, bf16[256,8,64]{0,2,1:T(8,128)(2,1)S(1)} %all-to-all-done.2), kind=kOutput, calls=%fused_computation.12 | convolution fusion | flops 406847488 | bytes 17629184 | tf_op jit(solution)/shard_map/jvp(tsc,bsc->btc)/dot_general | solution.py:90
  320.8 12.4 %fusion.2 = f32[64,8,256]{2,1,0:T(8,128)S(1)} fusion(f32[256,511,64]{1,0,2:T(8,128)} %reshape.1079, pred[256,256]{1,0:T(8,128)(4,1)S(1)} %copy-done.145, bf16[256,8,64]{0,2,1:T(8,128)(2,1)S(1)} %all-to-all-done.4), kind=kOutput, calls=%fused_computation.8 | convolution fusion | flops 406847488 | bytes 17629184 | tf_op jit(solution)/shard_map/jvp(tsc,bsc->btc)/dot_general | solution.py:90
  334.4 12.2 %fusion.10 = f32[64,8,256]{2,1,0:T(8,128)S(1)} fusion(f32[256,511,64]{1,0,2:T(8,128)} %reshape.1079, pred[256,256]{1,0:T(8,128)(4,1)S(1)} %fusion.380, bf16[256,8,64]{0,2,1:T(8,128)(2,1)S(1)} %all-to-all-done), kind=kOutput, calls=%fused_computation.16 | convolution fusion | flops 406847488 | bytes 17629184 | tf_op jit(solution)/shard_map/jvp(tsc,bsc->btc)/dot_general | solution.py:90
  346.8 6.2 multiply_convert_fusion.10
  371.1 4.5 all-to-all-done.3
  382.1 4.5 all-to-all-done.5
  391.4 8.8 multiply_convert_fusion
  400.2 7.0 multiply_convert_fusion.1
  407.2 7.3 multiply_convert_fusion.2
  417.6 4.3 convert_reduce_fusion
  478.4 4.1 all-to-all-start.10
  483.2 6.5 all-to-all-done.10
  495.8 5.1 all-to-all-done.6
  501.7 6.1 fusion.215
  507.8 13.6 %fusion = f32[64,8,256]{2,1,0:T(8,128)} fusion(f32[64,8,256]{2,1,0:T(8,128)S(1)} %get-tuple-element.313, f32[256,511,64]{1,0,2:T(8,128)} %reshape.1079, pred[256,256]{1,0:T(8,128)(4,1)S(1)} %copy-done.145), kind=kOutput, calls=%fused_computation.6 | convolution fusion | flops 406847488 | bytes 17891328 | tf_op jit(solution)/shard_map/transpose(jvp(tsc,bsc->btc))/dot_general | solution.py:90
  568.8 6.6 fusion.147
  575.4 8.3 multiply_reduce_fusion.12
  593.9 4.9 fusion.188
  600.8 4.4 all-to-all-start.11
  612.1 7.3 select_bitcast_fusion.1
  619.4 12.6 %pad.147 = f32[256,511,64]{1,0,2:T(8,128)} pad(f32[256,256,64]{1,0,2:T(8,128)S(1)} %select_bitcast_fusion.1, f32[]{:T(128)} %constant.67.clone.1), padding=0_0x0_255x0_0 | pad | bytes 50266116 | tf_op jit(solution)/shard_map/transpose(jvp())/pad | solution.py:57
  631.9 30.5 %reshape.1082 = f32[130816,64]{0,1:T(8,128)} reshape(f32[256,511,64]{1,0,2:T(8,128)} %pad.147) | data formatting | bytes 66977792 | tf_op jit(solution)/shard_map/transpose(jvp())/reshape | solution.py:57
  662.4 12.0 %pad.148 = f32[131072,64]{0,1:T(8,128)S(1)} pad(f32[130816,64]{0,1:T(8,128)} %reshape.1082, f32[]{:T(128)} %constant.67.clone.1), padding=0_256x0_0 | pad | bytes 67043332 | tf_op jit(solution)/shard_map/transpose(jvp())/pad | solution.py:56
  674.4 21.7 %copy.559 = f32[8,8,256,512]{3,2,1,0:T(8,128)} copy(f32[8,8,256,512]{3,1,2,0:T(8,128)S(1)} %bitcast.709) | data formatting | bytes 67108864
  696.1 12.3 %bitcast_reduce_fusion.1 = f32[512,64]{0,1:T(8,128)S(1)} fusion(f32[8,8,256,512]{3,2,1,0:T(8,128)} %copy.559), kind=kLoop, calls=%fused_computation.1 | loop fusion | flops 8355840 | bytes 33685504 | tf_op jit(solution)/shard_map/transpose(jvp())/reduce_sum | solution.py:55
  709.5 7.3 select_bitcast_fusion
  716.8 12.6 %pad.159 = f32[256,511,64]{1,0,2:T(8,128)} pad(f32[256,256,64]{1,0,2:T(8,128)S(1)} %select_bitcast_fusion, f32[]{:T(128)} %constant.67.clone.1), padding=0_0x0_255x0_0 | pad | bytes 50266116 | tf_op jit(solution)/shard_map/transpose(jvp())/pad | solution.py:57
  729.3 30.9 %reshape.1084 = f32[130816,64]{0,1:T(8,128)} reshape(f32[256,511,64]{1,0,2:T(8,128)} %pad.159) | data formatting | bytes 66977792 | tf_op jit(solution)/shard_map/transpose(jvp())/reshape | solution.py:57
  760.2 12.0 %pad.160 = f32[131072,64]{0,1:T(8,128)S(1)} pad(f32[130816,64]{0,1:T(8,128)} %reshape.1084, f32[]{:T(128)} %constant.67.clone.1), padding=0_256x0_0 | pad | bytes 67043332 | tf_op jit(solution)/shard_map/transpose(jvp())/pad | solution.py:56
  772.2 21.5 %copy.560 = f32[8,8,256,512]{3,2,1,0:T(8,128)} copy(f32[8,8,256,512]{3,1,2,0:T(8,128)S(1)} %bitcast.710) | data formatting | bytes 67108864
  793.8 12.4 %bitcast_reduce_fusion = f32[512,64]{0,1:T(8,128)S(1)} fusion(f32[8,8,256,512]{3,2,1,0:T(8,128)} %copy.560), kind=kLoop, calls=%fused_computation | loop fusion | flops 8355840 | bytes 33685504 | tf_op jit(solution)/shard_map/transpose(jvp())/reduce_sum | solution.py:55
  807.1 7.3 select_bitcast_fusion.2
  814.5 12.6 %pad.135 = f32[256,511,64]{1,0,2:T(8,128)} pad(f32[256,256,64]{1,0,2:T(8,128)S(1)} %select_bitcast_fusion.2, f32[]{:T(128)} %constant.67.clone.1), padding=0_0x0_255x0_0 | pad | bytes 50266116 | tf_op jit(solution)/shard_map/transpose(jvp())/pad | solution.py:57
  827.0 30.4 %reshape.1080 = f32[130816,64]{0,1:T(8,128)} reshape(f32[256,511,64]{1,0,2:T(8,128)} %pad.135) | data formatting | bytes 66977792 | tf_op jit(solution)/shard_map/transpose(jvp())/reshape | solution.py:57
  857.4 11.9 %pad.136 = f32[131072,64]{0,1:T(8,128)S(1)} pad(f32[130816,64]{0,1:T(8,128)} %reshape.1080, f32[]{:T(128)} %constant.67.clone.1), padding=0_256x0_0 | pad | bytes 67043332 | tf_op jit(solution)/shard_map/transpose(jvp())/pad | solution.py:56
  869.3 21.7 %copy.558 = f32[8,8,256,512]{3,2,1,0:T(8,128)} copy(f32[8,8,256,512]{3,1,2,0:T(8,128)S(1)} %bitcast.707) | data formatting | bytes 67108864
  891.0 12.2 %bitcast_reduce_fusion.2 = f32[512,64]{0,1:T(8,128)S(1)} fusion(f32[8,8,256,512]{3,2,1,0:T(8,128)} %copy.558), kind=kLoop, calls=%fused_computation.2 | loop fusion | flops 8355840 | bytes 33685504 | tf_op jit(solution)/shard_map/transpose(jvp())/reduce_sum | solution.py:55
  910.2 4.3 rev.53
  915.6 21.6 %fusion.78 = (f32[64,32]{1,0:T(8,128)}, f32[64,32]{1,0:T(8,128)}, f32[64,32]{1,0:T(8,128)}, f32[64,32]{1,0:T(8,128)}, f32[64,32]{1,0:T(8,128)}, /*index=5*/f32[6...) fusion(f32[257,64,32]{0,2,1:T(8,128)} %copy-done.13, ...), kind=kOutput, calls=%fused_computation.122 | convolution fusion | flops 80457728 | bytes 57835520 | tf_op jit(solution)/shard_map/transpose(jvp(tcn,icn->itc))/dot_general | solution.py:114
  937.3 19.0 %fusion.61 = (f32[64,32]{1,0:T(8,128)S(1)}, f32[64,32]{1,0:T(8,128)}, f32[64,32]{1,0:T(8,128)}) fusion(f32[64,32]{1,0:T(8,128)S(1)} %copy-done.175, f32[64,32]{1,0:T(8,128)S(1)} %copy-done.178, f32[257]{0:T(512)S(1)} %copy-done.223, f32[256,64,32]{0,2,1:T(8,128)} %get-tuple-element.281, f32[256,64,32]{0,2,1:T(8,128)S(1)} %copy-done.46, ...), kind=kLoop, calls=%fused_computation.71 | loop fusion | flops 12099584 | bytes 16819204 | tf_op jit(solution)/shard_map/transpose(jvp())/reduce_sum | solution.py:47
  964.9 4.2 rev.50
  971.6 4.2 rev.47
  979.1 4.2 rev.45
  983.4 23.1 %fusion.55 = (f32[64,32]{1,0:T(8,128)}, f32[64,32]{1,0:T(8,128)S(1)}, f32[64,32]{1,0:T(8,128)S(1)}, f32[64,32]{1,0:T(8,128)S(1)}, f32[64,32]{1,0:T(8,128)S(1)}, /*index=5*/f32[64,32]{1,0:T(8,128)}) fusion(f32[64,32]{1,0:T(8,128)S(1)} %copy-done.176, f32[64,32]{1,0:T(8,128)S(1)} %copy-done.179, f32[257]{0:T(512)S(1)} %copy-done.223, ...), kind=kLoop, calls=%fused_computation.65 | loop fusion | flops 23146496 | bytes 33620996 | tf_op jit(solution)/shard_map/transpose(jvp())/reduce_sum | solution.py:47
  1035.7 7.1 fusion.141
  1047.9 12.7 %fusion.4 = f32[64,8,256]{2,1,0:T(8,128)S(1)} fusion(f32[64,8,256]{2,1,0:T(8,128)S(1)} %copy-done.15, f32[256,511,64]{1,0,2:T(8,128)} %reshape.1079, pred[256,256]{1,0:T(8,128)(4,1)S(1)} %copy-done.141), kind=kOutput, calls=%fused_computation.10 | convolution fusion | flops 406847488 | bytes 17891328 | tf_op jit(solution)/shard_map/transpose(jvp(tsc,bsc->btc))/dot_general | solution.py:90
  1061.8 12.2 %fusion.8 = f32[64,8,256]{2,1,0:T(8,128)S(1)} fusion(f32[64,8,256]{2,1,0:T(8,128)S(1)} %copy-done.18, f32[256,511,64]{1,0,2:T(8,128)} %reshape.1079, pred[256,256]{1,0:T(8,128)(4,1)S(1)} %copy-done.144), kind=kOutput, calls=%fused_computation.14 | convolution fusion | flops 406847488 | bytes 17891328 | tf_op jit(solution)/shard_map/transpose(jvp(tsc,bsc->btc))/dot_general | solution.py:90
  1080.9 18.9 %all-reduce.48 = (f32[64]{0:T(128)}, f32[64,32]{0,1:T(8,128)S(1)}, f32[64,32]{0,1:T(8,128)S(1)}, f32[64,32]{0,1:T(8,128)S(1)}, f32[64,32]{0,1:T(8,128)S(1)}, /*index=5*/f32[64]{0:T(128)}) all-reduce(f32[64]{0:T(128)S(1)} %add_multiply_fusion, f32[64,32]{0,1:T(8,128)S(1)} %copy-done.213, ...), channel_id=1, replica_groups=mesh['dp'=4,'chan'=8] {'dp'}, use_global_device_ids=true, to_apply=%region_47.48 | all-reduce | flops 8320 | bytes 66560 | tf_op jit(solution)/shard_map/psum | solution.py:251
  1100.4 4.2 all-to-all-start.7
  1115.5 37.8 %all-reduce.47 = (f32[512]{0:T(512)S(1)}, f32[1024]{0:T(1024)S(1)}, f32[512]{0:T(512)S(1)}, f32[2048]{0:T(1024)S(1)}) all-reduce(f32[512]{0:T(512)S(1)} %add_add_fusion.29, f32[1024]{0:T(1024)S(1)} %copy-done.236, f32[512]{0:T(512)S(1)} %copy-done.254, f32[2048]{0:T(1024)S(1)} %copy-done.224), channel_id=16, replica_groups=mesh['dp'=4,'chan'=8] {'dp','chan'}, use_global_device_ids=true, to_apply=%region_27.28.clone | all-reduce | flops 4096 | bytes 32768
  (855 shorter events, 322.6 us)
Async XLA Ops:
  7.2 360.9 %all-gather.4.cloned.1.call-start = ((), (), s32[]{:S(2)}) async-start(), calls=%async_computation.15 | async-start | bytes 1081344 | tf_op jit(solution)/shard_map/all_gather | solution.py:143
  9.3 44.3 %copy-start.8 = (bf16[3,256,512]{2,1,0:T(8,128)(2,1)S(1)}, bf16[3,256,512]{2,1,0:T(8,128)(2,1)}, u32[]{:S(2)}) copy-start(bf16[3,256,512]{2,1,0:T(8,128)(2,1)} %param.16) | copy-start | bytes 2359300
  9.5 46.5 %copy-start.66 = (f32[1,256,512]{1,2,0:T(8,128)}, f32[1,256,512]{1,2,0:T(8,128)S(1)}, u32[]{:S(2)}) copy-start(f32[1,256,512]{1,2,0:T(8,128)S(1)} %copy.269) | copy-start | bytes 1572868
  53.9 35.5 %copy-start.258 = (f32[64,8]{0,1:T(8,128)S(1)}, f32[64,8]{0,1:T(8,128)}, u32[]{:S(2)}) copy-start(f32[64,8]{0,1:T(8,128)} %param.23) | copy-start | bytes 6148
  53.9 48.7 %copy-start.259 = (f32[64,8]{0,1:T(8,128)S(1)}, f32[64,8]{0,1:T(8,128)}, u32[]{:S(2)}) copy-start(f32[64,8]{0,1:T(8,128)} %param.21) | copy-start | bytes 6148
  54.4 74.9 %copy-start.246 = (f32[256]{0:T(256)}, f32[256]{0:T(256)S(1)}, u32[]{:S(2)}) copy-start(f32[256]{0:T(256)S(1)} %get-tuple-element.88) | copy-start | bytes 3076
  54.9 74.4 %copy-start.226 = (f32[256]{0:T(256)}, f32[256]{0:T(256)S(1)}, u32[]{:S(2)}) copy-start(f32[256]{0:T(256)S(1)} %fusion.464) | copy-start | bytes 3076
  54.9 74.4 %copy-start.230 = (f32[256]{0:T(256)}, f32[256]{0:T(256)S(1)}, u32[]{:S(2)}) copy-start(f32[256]{0:T(256)S(1)} %fusion.466) | copy-start | bytes 3076
  54.9 74.4 %copy-start.228 = (f32[256]{0:T(256)}, f32[256]{0:T(256)S(1)}, u32[]{:S(2)}) copy-start(f32[256]{0:T(256)S(1)} %fusion.462) | copy-start | bytes 3076
  56.1 188.4 %all-to-all-start = ((bf16[256,8,64]{0,2,1:T(8,128)(2,1)}), bf16[256,8,64]{0,2,1:T(8,128)(2,1)S(1)}, u32[]{:S(2)}, u32[]{:S(2)}) async-start(bf16[256,8,64]{0,2,1:T(8,128)(2,1)} %get-tuple-element.295), calls=%async_computation | async-start | bytes 524288 | tf_op jit(solution)/shard_map/all_to_all | solution.py:161
  60.1 331.3 %all-gather.6.cloned.1.call-start = ((), (), s32[]{:S(2)}) async-start(), calls=%async_computation.16 | async-start | bytes 2162688 | tf_op jit(solution)/shard_map/all_gather | solution.py:147
  74.0 55.4 %copy-start.148 = (f32[64,32]{0,1:T(8,128)}, f32[64,32]{0,1:T(8,128)S(1)}, u32[]{:S(2)}) copy-start(f32[64,32]{0,1:T(8,128)S(1)} %all_gather.24) | copy-start | bytes 24580
  74.0 42.7 %copy-start.232 = (f32[64]{0:T(128)}, f32[64]{0:T(128)S(1)}, u32[]{:S(2)}) copy-start(f32[64]{0:T(128)S(1)} %exp.16) | copy-start | bytes 772
  74.6 54.8 %copy-start.155 = (f32[64,32]{0,1:T(8,128)}, f32[64,32]{0,1:T(8,128)S(1)}, u32[]{:S(2)}) copy-start(f32[64,32]{0,1:T(8,128)S(1)} %get-tuple-element.235) | copy-start | bytes 24580
  75.4 54.0 %copy-start.174 = (f32[64,32]{1,0:T(8,128)}, f32[64,32]{1,0:T(8,128)S(1)}, u32[]{:S(2)}) copy-start(f32[64,32]{1,0:T(8,128)S(1)} %copy.261) | copy-start | bytes 24580
  76.2 53.2 %copy-start.157 = (f32[64,32]{0,1:T(8,128)}, f32[64,32]{0,1:T(8,128)S(1)}, u32[]{:S(2)}) copy-start(f32[64,32]{0,1:T(8,128)S(1)} %cos.7) | copy-start | bytes 24580
  76.2 53.1 %copy-start.222 = (f32[257]{0:T(512)}, f32[257]{0:T(512)S(1)}, u32[]{:S(2)}) copy-start(f32[257]{0:T(512)S(1)} %iota_convert_fusion) | copy-start | bytes 3088
  89.4 40.0 %copy-start.186 = (f32[64,32]{0,1:T(8,128)}, f32[64,32]{0,1:T(8,128)S(1)}, u32[]{:S(2)}) copy-start(f32[64,32]{0,1:T(8,128)S(1)} %all_gather.26) | copy-start | bytes 24580
  139.9 165.6 %copy-start.139 = (pred[256,256]{1,0:T(8,128)(4,1)}, pred[256,256]{1,0:T(8,128)(4,1)S(1)}, u32[]{:S(2)}) copy-start(pred[256,256]{1,0:T(8,128)(4,1)S(1)} %fusion.379) | copy-start | bytes 196612
  139.9 435.5 %copy-start.207 = (f32[8,8]{1,0:T(8,128)}, f32[8,8]{1,0:T(8,128)S(1)}, u32[]{:S(2)}) copy-start(f32[8,8]{1,0:T(8,128)S(1)} %multiply_convert_fusion.12) | copy-start | bytes 772
  142.3 131.2 %copy-start.239 = (pred[8,8]{1,0:T(8,128)(4,1)}, pred[8,8]{1,0:T(8,128)(4,1)S(1)}, u32[]{:S(2)}) copy-start(pred[8,8]{1,0:T(8,128)(4,1)S(1)} %get-tuple-element.320) | copy-start | bytes 196
  142.3 433.1 %copy-start.234 = (pred[8,8]{1,0:T(8,128)(4,1)}, pred[8,8]{1,0:T(8,128)(4,1)S(1)}, u32[]{:S(2)}) copy-start(pred[8,8]{1,0:T(8,128)(4,1)S(1)} %get-tuple-element.319) | copy-start | bytes 196
  142.3 433.1 %copy-start.235 = (pred[8,8]{1,0:T(8,128)(4,1)}, pred[8,8]{1,0:T(8,128)(4,1)S(1)}, u32[]{:S(2)}) copy-start(pred[8,8]{1,0:T(8,128)(4,1)S(1)} %get-tuple-element.321) | copy-start | bytes 196
  239.7 359.1 %copy-start = (f32[256,64,32]{0,2,1:T(8,128)}, f32[256,64,32]{0,2,1:T(8,128)S(1)}, u32[]{:S(2)}) copy-start(f32[256,64,32]{0,2,1:T(8,128)S(1)} %rev.43) | copy-start | bytes 6291460
  244.5 89.9 %copy-start.142 = (pred[256,256]{1,0:T(8,128)(4,1)}, pred[256,256]{1,0:T(8,128)(4,1)S(1)}, u32[]{:S(2)}) copy-start(pred[256,256]{1,0:T(8,128)(4,1)S(1)} %fusion.380) | copy-start | bytes 196612
  244.5 349.3 %copy-start.19 = (bf16[256,8,64]{0,2,1:T(8,128)(2,1)}, bf16[256,8,64]{0,2,1:T(8,128)(2,1)S(1)}, u32[]{:S(2)}) copy-start(bf16[256,8,64]{0,2,1:T(8,128)(2,1)S(1)} %all-to-all-done) | copy-start | bytes 786436
  244.5 11.1 all-to-all-start.2
  255.6 91.1 %copy-start.21 = (bf16[256,8,64]{0,2,1:T(8,128)(2,1)}, bf16[256,8,64]{0,2,1:T(8,128)(2,1)S(1)}, u32[]{:S(2)}) copy-start(bf16[256,8,64]{0,2,1:T(8,128)(2,1)S(1)} %all-to-all-done.2) | copy-start | bytes 786436
  255.6 10.3 all-to-all-start.4
  265.9 80.8 %copy-start.25 = (bf16[256,8,64]{0,2,1:T(8,128)(2,1)}, bf16[256,8,64]{0,2,1:T(8,128)(2,1)S(1)}, u32[]{:S(2)}) copy-start(bf16[256,8,64]{0,2,1:T(8,128)(2,1)S(1)} %all-to-all-done.4) | copy-start | bytes 786436
  353.8 10.3 all-to-all-start.1
  357.2 60.5 %all-gather.8.cloned.1.call-start = ((), (), s32[]{:S(2)}) async-start(), calls=%async_computation.17 | async-start | bytes 2162688 | tf_op jit(solution)/shard_map/all_gather | solution.py:149
  364.1 11.5 all-to-all-start.3
  375.5 11.0 all-to-all-start.5
  379.6 779.8 %reduce-scatter.4.cloned.1.call-start = ((), (), s32[]{:S(2)}) async-start(), calls=%async_computation.18 | async-start | bytes 2162688 | tf_op jit(solution)/shard_map/reduce_scatter | solution.py:242
  440.1 719.3 %reduce-scatter.6.cloned.1.call-start = ((), (), s32[]{:S(2)}) async-start(), calls=%async_computation.19 | async-start | bytes 4325376 | tf_op jit(solution)/shard_map/reduce_scatter | solution.py:246
  452.3 26.1 %all-to-all-start.8 = ((bf16[256,8,64]{0,2,1:T(8,128)(2,1)}), bf16[256,8,64]{0,2,1:T(8,128)(2,1)}, u32[]{:S(2)}, u32[]{:S(2)}) async-start(bf16[256,8,64]{0,2,1:T(8,128)(2,1)} %bitcast.724), calls=%async_computation.8 | async-start | bytes 524288 | tf_op jit(solution)/shard_map/all_to_all | solution.py:215
  456.3 703.1 %reduce-scatter.8.cloned.1.call-start = ((), (), s32[]{:S(2)}) async-start(), calls=%async_computation.20 | async-start | bytes 4325376 | tf_op jit(solution)/shard_map/reduce_scatter | solution.py:248
  478.4 11.3 all-to-all-start.10
  489.7 11.3 all-to-all-start.6
  507.8 29.8 %copy-start.16 = (f32[64,8,256]{2,1,0:T(8,128)}, f32[64,8,256]{2,1,0:T(8,128)S(1)}, u32[]{:S(2)}) copy-start(f32[64,8,256]{2,1,0:T(8,128)S(1)} %get-tuple-element.314) | copy-start | bytes 1572868
  507.8 104.3 %copy-start.14 = (f32[64,8,256]{2,1,0:T(8,128)}, f32[64,8,256]{2,1,0:T(8,128)S(1)}, u32[]{:S(2)}) copy-start(f32[64,8,256]{2,1,0:T(8,128)S(1)} %get-tuple-element.312) | copy-start | bytes 1572868
  554.9 28.8 %copy-start.138 = (f32[64,32,8]{0,1,2:T(8,128)}, f32[64,32,8]{0,1,2:T(8,128)S(1)}, u32[]{:S(2)}) copy-start(f32[64,32,8]{0,1,2:T(8,128)S(1)} %copy.539) | copy-start | bytes 196612
  600.8 476.0 %all-to-all-start.11 = ((bf16[8,256,64]{1,2,0:T(8,128)(2,1)}), bf16[8,256,64]{1,2,0:T(8,128)(2,1)}, u32[]{:S(2)}, u32[]{:S(2)}) async-start(bf16[8,256,64]{1,2,0:T(8,128)(2,1)} %copy.291), calls=%async_computation.11 | async-start | bytes 524288 | tf_op jit(solution)/shard_map/all_to_all | solution.py:217
  983.3 29.2 %copy-start.203 = (f32[64,32]{1,0:T(8,128)S(1)}, f32[64,32]{1,0:T(8,128)}, u32[]{:S(2)}) copy-start(f32[64,32]{1,0:T(8,128)} %get-tuple-element.64) | copy-start | bytes 24580
  983.3 29.9 %copy-start.202 = (f32[64,32]{1,0:T(8,128)S(1)}, f32[64,32]{1,0:T(8,128)}, u32[]{:S(2)}) copy-start(f32[64,32]{1,0:T(8,128)} %get-tuple-element.241) | copy-start | bytes 24580
  983.3 30.5 %copy-start.201 = (f32[64,32]{1,0:T(8,128)S(1)}, f32[64,32]{1,0:T(8,128)}, u32[]{:S(2)}) copy-start(f32[64,32]{1,0:T(8,128)} %get-tuple-element.67) | copy-start | bytes 24580
  983.4 31.2 %copy-start.200 = (f32[64,32]{1,0:T(8,128)S(1)}, f32[64,32]{1,0:T(8,128)}, u32[]{:S(2)}) copy-start(f32[64,32]{1,0:T(8,128)} %get-tuple-element.243) | copy-start | bytes 24580
  983.4 52.3 %copy-start.134 = (f32[64,32,8]{0,1,2:T(8,128)S(1)}, f32[64,32,8]{0,1,2:T(8,128)}, u32[]{:S(2)}) copy-start(f32[64,32,8]{0,1,2:T(8,128)} %copy-done.133) | copy-start | bytes 196612
  1006.4 36.3 %copy-start.149 = (f32[64,32]{0,1:T(8,128)S(1)}, f32[64,32]{0,1:T(8,128)}, u32[]{:S(2)}) copy-start(f32[64,32]{0,1:T(8,128)} %copy-done.148) | copy-start | bytes 24580
  1015.2 30.2 %copy-start.2 = (f32[256,64,32]{0,2,1:T(8,128)S(1)}, f32[256,64,32]{0,2,1:T(8,128)}, u32[]{:S(2)}) copy-start(f32[256,64,32]{0,2,1:T(8,128)} %rev.44) | copy-start | bytes 6291460
  1015.2 30.2 %copy-start.113 = (f32[64,32,8]{1,2,0:T(8,128)S(1)}, f32[64,32,8]{1,2,0:T(8,128)}, u32[]{:S(2)}) copy-start(f32[64,32,8]{1,2,0:T(8,128)} %copy.477) | copy-start | bytes 196612
  1015.2 30.2 %copy-start.115 = (f32[64,32,8]{1,2,0:T(8,128)S(1)}, f32[64,32,8]{1,2,0:T(8,128)}, u32[]{:S(2)}) copy-start(f32[64,32,8]{1,2,0:T(8,128)} %copy.484) | copy-start | bytes 196612
  1076.8 23.5 %all-to-all-start.9 = ((bf16[8,256,64]{1,2,0:T(8,128)(2,1)}), bf16[8,256,64]{1,2,0:T(8,128)(2,1)S(1)}, u32[]{:S(2)}, u32[]{:S(2)}) async-start(bf16[8,256,64]{1,2,0:T(8,128)(2,1)} %copy.287), calls=%async_computation.9 | async-start | bytes 524288 | tf_op jit(solution)/shard_map/all_to_all | solution.py:217
  1100.4 11.2 all-to-all-start.7
  1109.5 46.1 %copy-start.247 = (f32[256]{0:T(256)S(1)}, f32[256]{0:T(256)}, u32[]{:S(2)}) copy-start(f32[256]{0:T(256)} %copy-done.246) | copy-start | bytes 3076
  1109.5 46.1 %copy-start.245 = (f32[256]{0:T(256)S(1)}, f32[256]{0:T(256)}, u32[]{:S(2)}) copy-start(f32[256]{0:T(256)} %copy-done.244) | copy-start | bytes 3076
  1109.5 46.1 %copy-start.243 = (f32[256]{0:T(256)S(1)}, f32[256]{0:T(256)}, u32[]{:S(2)}) copy-start(f32[256]{0:T(256)} %copy-done.242) | copy-start | bytes 3076
  1109.5 46.1 %copy-start.67 = (f32[1,256,512]{1,2,0:T(8,128)S(1)}, f32[1,256,512]{1,2,0:T(8,128)}, u32[]{:S(2)}) copy-start(f32[1,256,512]{1,2,0:T(8,128)} %copy-done.66) | copy-start | bytes 1572868
  1109.5 46.1 %copy-start.69 = (f32[1,256,512]{1,2,0:T(8,128)S(1)}, f32[1,256,512]{1,2,0:T(8,128)}, u32[]{:S(2)}) copy-start(f32[1,256,512]{1,2,0:T(8,128)} %copy-done.68) | copy-start | bytes 1572868
  1109.5 46.1 %copy-start.221 = (f32[8,64]{1,0:T(8,128)S(1)}, f32[8,64]{1,0:T(8,128)}, u32[]{:S(2)}) copy-start(f32[8,64]{1,0:T(8,128)} %copy-done.220) | copy-start | bytes 6148
  1113.3 44.2 %copy-start.59 = (bf16[3,256,512]{2,1,0:T(8,128)(2,1)S(1)}, bf16[3,256,512]{2,1,0:T(8,128)(2,1)}, u32[]{:S(2)}) copy-start(bf16[3,256,512]{2,1,0:T(8,128)(2,1)} %param.17) | copy-start | bytes 2359300
  1113.3 44.2 %copy-start.61 = (f32[256,512]{1,0:T(8,128)S(1)}, f32[256,512]{1,0:T(8,128)}, u32[]{:S(2)}) copy-start(f32[256,512]{1,0:T(8,128)} %copy-done.60) | copy-start | bytes 1572868
  1113.3 44.2 %copy-start.241 = (f32[256]{0:T(256)S(1)}, f32[256]{0:T(256)}, u32[]{:S(2)}) copy-start(f32[256]{0:T(256)} %copy-done.240) | copy-start | bytes 3076
  (235 other events, 1655.6 us)
Sparse Core Ops, SparseCore 0:
  10.9 56.3 all-gather.3
  70.2 55.4 all-gather.5
  360.9 56.7 all-gather.7
  440.3 135.8 reduce-scatter.3
  578.9 136.7 reduce-scatter.5
  718.5 136.6 reduce-scatter.7
where the time goes:
time: 1180 us; the launch traced here: 1170 us
  local copies, waits for them, and re-layouts  474 us (40%)
  matrix products  270 us (23%)
  other arithmetic  168 us (14%)
  blocking collectives  152 us (13%)
  starting transfers between devices  47.7 us (4%)
  waiting for transfers between devices  34.7 us (3%)
  between operations  19.8 us (2%)
    reshape x4, local copies, waits for them, and re-layouts, lower_toeplitz(): flat.reshape(block_size, 2 * block_size - 1, channels)[:, :block_size]  137 us
    unnamed x601, local copies, waits for them, and re-layouts  124 us
    dot_general x9, matrix products, state_mix(): within = jnp.einsum('tsc,bsc->btc', toeplitz, shaped, precision=highest)  97.5 us
    unnamed x2, blocking collectives  79.8 us
    reduce_sum x4, other arithmetic, mode_powers(): magnitude = jnp.exp(shaped * damping)  55.8 us
    dot_general x9, matrix products, state_mix(): jnp.einsum('tcn,icn->itc', read_imag, carry_imag, precision=highest)  44.5 us
    pad x3, local copies, waits for them, and re-layouts, lower_toeplitz(): flat.reshape(block_size, 2 * block_size - 1, channels)[:, :block_size]  37.7 us
    reduce_sum x3, other arithmetic, lower_toeplitz(): jnp.broadcast_to(row_base[None], (block_size, 2 * block_size, channels))  36.9 us
  transfers between devices with their start and end apart: 18, of which 9 were waited for; matrix products, arithmetic and copies ran while one was open for 76% of the time, Pallas kernels for 0%

commit v1 on v0

v1 whole, which is shorter than its diff:
```python
import functools
import jax
import jax.numpy as jnp
from jax import lax
from jax.experimental import pallas as pl
from jax.experimental.pallas import tpu as pltpu
from jax.sharding import PartitionSpec as P

SPAN = 128
PACK = 16
HI = lax.Precision.HIGHEST


def cmul(ar, ai, br, bi):
    return ar * br - ai * bi, ar * bi + ai * br


def mode_rows(ls, ld, fr, rr, ri):
    dt = jnp.exp(ls)
    a_r = -jnp.exp(ld)
    a_i = fr
    t_r, t_i = dt * a_r, dt * a_i
    mag = jnp.exp(t_r)
    l_r, l_i = mag * jnp.cos(t_i), mag * jnp.sin(t_i)
    mod = a_r * a_r + a_i * a_i
    u_r = l_r - 1.0
    q_r = (u_r * a_r + l_i * a_i) / mod
    q_i = (l_i * a_r - u_r * a_i) / mod
    w_r, w_i = cmul(rr, ri, q_r, q_i)
    return dict(dt=dt, a_r=a_r, a_i=a_i, t_r=t_r, t_i=t_i, l_r=l_r, l_i=l_i, mod=mod,
                q_r=q_r, q_i=q_i, w_r=w_r, w_i=w_i)


def mode_prelude(modes_ref, pw_ref):
    m = mode_rows(modes_ref[0], modes_ref[1], modes_ref[2], modes_ref[3], modes_ref[4])
    r, i = m["l_r"], m["l_i"]
    for k in range(8):
        pw_ref[2 * k] = r
        pw_ref[2 * k + 1] = i
        r, i = cmul(r, i, r, i)
    pw_ref[16] = 2.0 * m["w_r"]
    pw_ref[17] = 2.0 * m["w_i"]


def group_rows(pw_ref, g):
    rows = [pw_ref[k, pl.ds(g, 1), :] for k in range(18)]
    return [jnp.broadcast_to(x, (8, 128)) for x in rows]


def power_table(rows, reverse):
    sub = lax.broadcasted_iota(jnp.int32, (8, 128), 0)
    if reverse:
        sub = 7 - sub
        r, i = jnp.ones((8, 128), jnp.float32), jnp.zeros((8, 128), jnp.float32)
    else:
        r, i = rows[0], rows[1]
    for k in range(3):
        bit = ((sub >> k) & 1) == 1
        fr = jnp.where(bit, rows[2 * k], 1.0)
        fi = jnp.where(bit, rows[2 * k + 1], 0.0)
        r, i = cmul(r, i, fr, fi)
    parts = [(r, i)]
    for k in range(3, 7):
        more = [cmul(a, b, rows[2 * k], rows[2 * k + 1]) for a, b in parts]
        parts = more + parts if reverse else parts + more
    return (jnp.concatenate([p[0] for p in parts], 0), jnp.concatenate([p[1] for p in parts], 0))


def nt(a, b, **kw):
    return lax.dot_general(a, b, (((1,), (1,)), ((), ())), preferred_element_type=jnp.float32, **kw)


def tn(a, b, **kw):
    return lax.dot_general(a, b, (((0,), (0,)), ((), ())), preferred_element_type=jnp.float32, **kw)


def nn(a, b, **kw):
    return jnp.dot(a, b, preferred_element_type=jnp.float32, **kw)


def kernel_rows(rd_r, w_r):
    t = lax.broadcasted_iota(jnp.int32, (SPAN, 128), 0)
    src = jnp.where(t == SPAN - 1, jnp.concatenate([w_r] * 16, 0), rd_r)
    pick = (lax.broadcasted_iota(jnp.int32, (8, 128), 1) // 32
            == lax.broadcasted_iota(jnp.int32, (8, 128), 0)).astype(jnp.float32)
    return pltpu.roll(nt(pick, src, precision=HI), 1, 1)


def toeplitz(row):
    base = pltpu.roll(jnp.broadcast_to(row, (8, 128)), 0, 1, stride=1, stride_axis=0)
    parts = [base] + [pltpu.roll(base, 8 * v, 1) for v in range(1, 16)]
    whole = jnp.concatenate(parts, 0)
    s = lax.broadcasted_iota(jnp.int32, (SPAN, 128), 0)
    t = lax.broadcasted_iota(jnp.int32, (SPAN, 128), 1)
    return jnp.where(t >= s, whole, 0.0).astype(jnp.bfloat16)


def lag_sums(g):
    s = lax.broadcasted_iota(jnp.int32, (SPAN, 128), 0)
    t = lax.broadcasted_iota(jnp.int32, (SPAN, 128), 1)
    g = jnp.where(t >= s, g, 0.0)
    n = SPAN
    while n > 8:
        n //= 2
        g = g[:n] + pltpu.roll(g[n:], 128 - n, 1)
    for n in (4, 2, 1):
        g = g + pltpu.roll(pltpu.roll(g, 128 - n, 1), 8 - n, 0)
    return g[0:1]


def lane_owner(rows):
    return lax.broadcasted_iota(jnp.int32, (rows, 128), 1) // 32


def fold(stack, rows):
    width = stack.shape[1]
    own = (lax.broadcasted_iota(jnp.int32, (rows, width), 1) // 32) & 3
    out = stack[:rows]
    for k in range(1, 4):
        out = jnp.where(own == k, stack[k * rows:(k + 1) * rows], out)
    return out


def spread(packed, rows):
    width = packed.shape[1]
    own = (lax.broadcasted_iota(jnp.int32, (rows, width), 1) // 32) & 3
    return jnp.concatenate([jnp.where(own == k, packed, 0.0) for k in range(4)], 0)


def gelu_pair(v):
    half = 0.5 * (1.0 + lax.erf(v * 0.7071067811865476))
    return v * half, half + v * jnp.exp(-0.5 * v * v) * 0.3989422804014327


def block_rows(r):
    return pl.ds(pl.multiple_of(r * PACK, PACK), PACK)


def unpack(src_ref, q, xs, nj, mb, h, blocks, scale=None):
    def body(j, _):
        for m in range(mb):
            for k in range(h):
                x = src_ref[j, pl.ds(q * PACK, PACK), pl.ds((m * h + k) * 128, 128)]
                xs[block_rows(m * blocks + j * h + k), :] = x.astype(jnp.float32)
        return 0
    lax.fori_loop(0, nj, body, 0)


def forward_kernel(dims, modes_ref, skip_ref, keep_ref, u_ref, act_ref, slope_ref, carry_ref, pw_ref, xs, ys, sc):
    nj, chans, mb, h = dims
    blocks = nj * h
    rows = mb * blocks
    mode_prelude(modes_ref, pw_ref)

    def one_pack(q, _):
        unpack(u_ref, q, xs, nj, mb, h, blocks)

        def states(g, _):
            rws = group_rows(pw_ref, q * 4 + g)
            p_r, p_i = power_table(rws, True)
            back = (SPAN - 1 - lax.broadcasted_iota(jnp.int32, (SPAN, 128), 0)).astype(jnp.float32)
            table = jnp.concatenate([p_r, p_i, back * p_r, back * p_i], 1).astype(jnp.bfloat16)
            x = jnp.concatenate([xs[pl.ds(4 * g + k, rows, stride=PACK), :] for k in range(4)], 0).astype(jnp.bfloat16)
            s = fold(nn(x, table), rows)
            for a in range(4):
                for m in range(mb):
                    sc[a, pl.ds(g * mb + m, blocks, stride=PACK), :] = s[m * blocks:(m + 1) * blocks, a * 128:(a + 1) * 128]
            return 0
        lax.fori_loop(0, 4, states, 0)

        def rows_of(k):
            parts = [jnp.broadcast_to(pw_ref[k, pl.ds(q * 4 + g, 1), :], (mb, 128)) for g in range(4)]
            parts.append(jnp.zeros((PACK - 4 * mb, 128), jnp.float32))
            return jnp.concatenate(parts, 0)
        h_r, h_i = rows_of(14), rows_of(15)

        def step(i, c):
            at = pl.ds(pl.multiple_of(i * PACK, PACK), PACK)
            keep = keep_ref[i]
            c = [x * keep for x in c]
            s = [sc[a, at, :] for a in range(4)]
            for a in range(4):
                carry_ref[q, a, at, :] = c[a]
            z_r, z_i = cmul(c[0], c[1], h_r, h_i)
            d_r, d_i = cmul(c[2] + SPAN * c[0], c[3] + SPAN * c[1], h_r, h_i)
            return (z_r + s[0], z_i + s[1], d_r + s[2], d_i + s[3])
        zero = jnp.zeros((PACK, 128), jnp.float32)
        lax.fori_loop(0, blocks, step, (zero,) * 4)

        def outputs(g, _):
            rws = group_rows(pw_ref, q * 4 + g)
            e_r, e_i = power_table(rws, False)
            w_r, w_i = jnp.concatenate([rws[16]] * 16, 0), jnp.concatenate([rws[17]] * 16, 0)
            r_r, r_i = cmul(e_r, e_i, w_r, w_i)
            krow = kernel_rows(r_r, rws[16])
            table = jnp.concatenate([r_r, -r_i], 1).astype(jnp.bfloat16)
            c = jnp.concatenate([
                jnp.concatenate([carry_ref[q, a, pl.ds(g * mb + m, blocks, stride=PACK), :] for m in range(mb)], 0)
                for a in range(2)], 1)
            across = nt(spread(c, rows).astype(jnp.bfloat16), table)
            for k in range(4):
                x = xs[pl.ds(4 * g + k, rows, stride=PACK), :].astype(jnp.bfloat16)
                y = across[k * rows:(k + 1) * rows] + nn(x, toeplitz(krow[k:k + 1]))
                ys[pl.ds(4 * g + k, rows, stride=PACK), :] = y
            return 0
        lax.fori_loop(0, 4, outputs, 0)

        skip = skip_ref[pl.ds(pl.multiple_of(q * PACK, PACK), PACK), :]
        def finish(j, _):
            for m in range(mb):
                for k in range(h):
                    r = m * blocks + j * h + k
                    v = ys[block_rows(r), :] + skip * xs[block_rows(r), :]
                    a, d = gelu_pair(v)
                    act_ref[j, pl.ds(q * PACK, PACK), pl.ds((m * h + k) * 128, 128)] = a.astype(jnp.bfloat16)
                    slope_ref[q, r] = d
            return 0
        lax.fori_loop(0, nj, finish, 0)
        return 0
    lax.fori_loop(0, chans // PACK, one_pack, 0)


def backward_kernel(dims, modes_ref, skip_ref, keep_ref, u_ref, ga_ref, slope_ref, carry_ref, gn_ref, zw_ref, pw_ref, xs, gy, gx, sc):
    nj, chans, mb, h = dims
    blocks = nj * h
    rows = mb * blocks
    mode_prelude(modes_ref, pw_ref)

    def one_pack(q, _):
        unpack(u_ref, q, xs, nj, mb, h, blocks)
        def start(j, _):
            for m in range(mb):
                for k in range(h):
                    r = m * blocks + j * h + k
                    x = ga_ref[j, pl.ds(q * PACK, PACK), pl.ds((m * h + k) * 128, 128)]
                    gy[block_rows(r), :] = x.astype(jnp.float32) * slope_ref[q, r]
            return 0
        lax.fori_loop(0, nj, start, 0)

        def states(g, _):
            gg = q * 4 + g
            rws = group_rows(pw_ref, gg)
            e_r, e_i = power_table(rws, False)
            ahead = (1 + lax.broadcasted_iota(jnp.int32, (SPAN, 128), 0)).astype(jnp.float32)
            table = jnp.concatenate([e_r, e_i, ahead * e_r, ahead * e_i], 1).astype(jnp.bfloat16)
            ups = [gy[pl.ds(4 * g + k, rows, stride=PACK), :].astype(jnp.bfloat16) for k in range(4)]
            lag = []
            for k in range(4):
                x = xs[pl.ds(4 * g + k, rows, stride=PACK), :].astype(jnp.bfloat16)
                lag.append(lag_sums(tn(x, ups[k])))
            lag = jnp.concatenate(lag + [jnp.zeros((4, 128), jnp.float32)], 0)
            own8 = lax.broadcasted_iota(jnp.int32, (8, 128), 1) // 32 == lax.broadcasted_iota(jnp.int32, (8, 128), 0)
            lag0 = jnp.sum(jnp.where(own8, jnp.broadcast_to(lag[:, 0:1], (8, 128)), 0.0), axis=0, keepdims=True)
            lane = lax.broadcasted_iota(jnp.int32, (8, 128), 1)
            later = jnp.where(lane == 127, 0.0, pltpu.roll(lag, 127, 1))
            top = later.astype(jnp.bfloat16)
            low = (later - top.astype(jnp.float32)).astype(jnp.bfloat16)
            stack = jnp.concatenate(ups + [top, low], 0)
            s = nn(stack, table)
            near = s[4 * rows:4 * rows + 8] + s[4 * rows + 8:]
            own = jnp.concatenate([own8] * 4, 1)
            near = jnp.sum(jnp.where(own, near, 0.0), axis=0, keepdims=True)
            zw_ref[0, pl.ds(gg, 1), :] = near[:, 0:128] + lag0
            for a in range(1, 4):
                zw_ref[a, pl.ds(gg, 1), :] = near[:, a * 128:(a + 1) * 128]
            zw_ref[4, pl.ds(gg, 1), :] = lag0
            s = fold(s[:4 * rows], rows)
            for a in range(4):
                for m in range(mb):
                    sc[a, pl.ds(g * mb + m, blocks, stride=PACK), :] = s[m * blocks:(m + 1) * blocks, a * 128:(a + 1) * 128]
            return 0
        lax.fori_loop(0, 4, states, 0)

        def rows_of(k):
            parts = [jnp.broadcast_to(pw_ref[k, pl.ds(q * 4 + g, 1), :], (mb, 128)) for g in range(4)]
            parts.append(jnp.zeros((PACK - 4 * mb, 128), jnp.float32))
            return jnp.concatenate(parts, 0)
        h_r, h_i = rows_of(14), rows_of(15)

        def step(n, c):
            i = blocks - 1 - n
            at = pl.ds(pl.multiple_of(i * PACK, PACK), PACK)
            a_r, a_i, z_r, z_i, w_r, w_i = c
            q_ = [sc[a, at, :] for a in range(4)]
            f = [carry_ref[q, a, at, :] for a in range(4)]
            d = cmul(q_[0], q_[1], f[0], f[1])
            e1 = cmul(q_[2], q_[3], f[0], f[1])
            e2 = cmul(q_[0], q_[1], f[2], f[3])
            sc[0, at, :] = a_r
            sc[1, at, :] = a_i
            keep = keep_ref[i]
            n_r, n_i = cmul(a_r, a_i, h_r, h_i)
            return ((n_r + q_[0]) * keep, (n_i + q_[1]) * keep, z_r + d[0], z_i + d[1], w_r + e1[0] + e2[0], w_i + e1[1] + e2[1])
        zero = jnp.zeros((PACK, 128), jnp.float32)
        out = lax.fori_loop(0, blocks, step, (zero,) * 6)
        for a in range(4):
            for g in range(4):
                add = jnp.sum(out[2 + a][g * mb:(g + 1) * mb], axis=0, keepdims=True)
                zw_ref[a, pl.ds(q * 4 + g, 1), :] += add

        def outputs(g, _):
            rws = group_rows(pw_ref, q * 4 + g)
            e_r, e_i = power_table(rws, False)
            w_r, w_i = jnp.concatenate([rws[16]] * 16, 0), jnp.concatenate([rws[17]] * 16, 0)
            r_r = e_r * w_r - e_i * w_i
            krow = kernel_rows(r_r, rws[16])
            p_r, p_i = power_table(rws, True)
            r_r, r_i = cmul(p_r, p_i, w_r, w_i)
            table = jnp.concatenate([r_r, -r_i], 1).astype(jnp.bfloat16)
            c = jnp.concatenate([
                jnp.concatenate([sc[a, pl.ds(g * mb + m, blocks, stride=PACK), :] for m in range(mb)], 0)
                for a in range(2)], 1)
            across = nt(spread(c, rows).astype(jnp.bfloat16), table)
            for k in range(4):
                up = gy[pl.ds(4 * g + k, rows, stride=PACK), :].astype(jnp.bfloat16)
                y = across[k * rows:(k + 1) * rows] + nt(up, toeplitz(krow[k:k + 1]))
                gx[pl.ds(4 * g + k, rows, stride=PACK), :] = y
            return 0
        lax.fori_loop(0, 4, outputs, 0)

        skip = skip_ref[pl.ds(pl.multiple_of(q * PACK, PACK), PACK), :]
        def finish(j, _):
            for m in range(mb):
                for k in range(h):
                    r = m * blocks + j * h + k
                    v = gx[block_rows(r), :] + skip * gy[block_rows(r), :]
                    gn_ref[j, pl.ds(q * PACK, PACK), pl.ds((m * h + k) * 128, 128)] = v.astype(jnp.bfloat16)
            return 0
        lax.fori_loop(0, nj, finish, 0)
        return 0
    lax.fori_loop(0, chans // PACK, one_pack, 0)


def ssm_forward(modes, skip, keep, u, mb):
    nj, chans, width = u.shape
    h = width // mb // 128
    blocks = nj * h
    rows = mb * blocks
    packs = chans // PACK
    f32 = jnp.float32
    return pl.pallas_call(
        functools.partial(forward_kernel, (nj, chans, mb, h)),
        out_shape=(
            jax.ShapeDtypeStruct(u.shape, jnp.bfloat16),
            jax.ShapeDtypeStruct((packs, rows, PACK, 128), f32),
            jax.ShapeDtypeStruct((packs, 4, blocks * PACK, 128), f32),
        ),
        scratch_shapes=[
            pltpu.VMEM((18, modes.shape[1], 128), f32),
            pltpu.VMEM((rows * PACK, 128), f32),
            pltpu.VMEM((rows * PACK, 128), f32),
            pltpu.VMEM((4, blocks * PACK, 128), f32),
        ],
        compiler_params=pltpu.CompilerParams(vmem_limit_bytes=50 << 20),
        name="ssm_forward",
    )(modes, skip, keep, u)


def ssm_backward(modes, skip, keep, u, ga, slope, carry, mb):
    nj, chans, width = u.shape
    h = width // mb // 128
    blocks = nj * h
    rows = mb * blocks
    f32 = jnp.float32
    return pl.pallas_call(
        functools.partial(backward_kernel, (nj, chans, mb, h)),
        out_shape=(
            jax.ShapeDtypeStruct(u.shape, jnp.bfloat16),
            jax.ShapeDtypeStruct((5, modes.shape[1], 128), f32),
        ),
        scratch_shapes=[
            pltpu.VMEM((18, modes.shape[1], 128), f32),
            pltpu.VMEM((rows * PACK, 128), f32),
            pltpu.VMEM((rows * PACK, 128), f32),
            pltpu.VMEM((rows * PACK, 128), f32),
            pltpu.VMEM((4, blocks * PACK, 128), f32),
        ],
        compiler_params=pltpu.CompilerParams(vmem_limit_bytes=50 << 20),
        name="ssm_backward",
    )(modes, skip, keep, u, ga, slope, carry)


def mode_gradients(modes, zw):
    m = mode_rows(*modes)
    z_r, z_i, v_r, v_i = zw[0], zw[1], zw[2], zw[3]
    rr, ri = modes[3], modes[4]
    g_rr = 2.0 * (z_r * m["q_r"] - z_i * m["q_i"])
    g_ri = -2.0 * (z_r * m["q_i"] + z_i * m["q_r"])
    k_r, k_i = cmul(rr, ri, m["a_r"] / m["mod"], -m["a_i"] / m["mod"])
    s_r, s_i = cmul(k_r, k_i, m["l_r"], m["l_i"])
    h1 = cmul(z_r, z_i, s_r, s_i)
    h2 = cmul(m["w_r"], m["w_i"], v_r, v_i)
    h_r, h_i = h1[0] + h2[0], h1[1] + h2[1]
    zc = cmul(z_r, z_i, m["w_r"], m["w_i"])
    za = cmul(zc[0], zc[1], m["a_r"] / m["mod"], -m["a_i"] / m["mod"])
    j_r, j_i = h_r * m["dt"] - za[0], h_i * m["dt"] - za[1]
    g_ls = 2.0 * (h_r * m["t_r"] - h_i * m["t_i"])
    return g_ls, 2.0 * m["a_r"] * j_r, -2.0 * j_i, g_rr, g_ri


def keep_rows(lengths, blocks, mb):
    at = jnp.arange(blocks, dtype=jnp.int32)[:, None] * SPAN
    keep = (at % lengths[None, :] != 0).astype(jnp.float32)
    rows = jnp.concatenate([keep] * 4 + [jnp.zeros((blocks, PACK - 4 * mb), jnp.float32)], 1)
    return jnp.broadcast_to(rows[:, :, None], (blocks, PACK, 128))


def mode_stack(log_step, ld, fr, rr, ri):
    nh = ld.shape[1]
    ls = jnp.broadcast_to(log_step[:, None], ld.shape)
    return jnp.stack([x.reshape(-1, 128) for x in (ls, ld, fr, rr, ri)])


def layer_norm(values, gain_vector):
    average = jnp.mean(values, axis=-1, keepdims=True)
    centred = values - average
    spread = jnp.mean(centred * centred, axis=-1, keepdims=True)
    return centred * lax.rsqrt(spread + 1e-05) * gain_vector


def exact_gelu(values):
    return jax.nn.gelu(values, approximate=False)


def gate_mix(project):
    features = project.shape[1] // 2
    return project[:, :features] * jax.nn.sigmoid(project[:, features:])


def on_device(
    tokens, cotangent, lengths, norm_gain, log_step, log_decay, frequency, readout_real, readout_imaginary,
    skip_gain, out_weight, out_bias, ffn_gain, in_weight, in_bias, back_weight,
):
    both = ("dp", "chan")
    mb, rows, feats = tokens.shape
    chans = log_step.shape[0]
    nj = feats // chans
    groups = log_decay.shape[1]
    f32, bf16 = jnp.float32, jnp.bfloat16
    shards = lax.axis_size("dp") * nj

    small = jnp.concatenate([out_bias, norm_gain, ffn_gain, in_bias])
    small = lax.all_gather(small, both, axis=0, tiled=False).astype(f32)
    cuts = (out_bias.shape[0], norm_gain.shape[0], ffn_gain.shape[0], in_bias.shape[0])
    at = [sum(cuts[:k]) for k in range(5)]
    b_out, gain_one, gain_two, b_in = (small[:, at[k]:at[k + 1]].reshape(-1) for k in range(4))
    four = jnp.stack([log_decay, frequency, readout_real, readout_imaginary])
    four = lax.all_gather(four, "dp", axis=2, tiled=True)
    w_out = lax.all_gather(out_weight, both, axis=0, tiled=True)
    w_in = lax.all_gather(in_weight, both, axis=0, tiled=True)
    w_back = lax.all_gather(back_weight, both, axis=0, tiled=True)

    rows_all = tokens.reshape(mb * rows, feats).astype(f32)
    normed, norm_pull = jax.vjp(layer_norm, rows_all, gain_one)
    sent = normed.astype(bf16).T.reshape(nj, chans, mb * rows)
    u = lax.all_to_all(sent, "chan", split_axis=0, concat_axis=0, tiled=True)

    modes = mode_stack(log_step, *four)
    skip = jnp.broadcast_to(skip_gain[:, None], (chans, 128))
    keep = keep_rows(lengths[:, 0], nj * rows // SPAN, mb)
    act, slope, carry = ssm_forward(modes, skip, keep, u, mb)
    act_t = lax.all_to_all(act, "chan", split_axis=0, concat_axis=0, tiled=True).reshape(feats, mb * rows)

    project = tn(act_t, w_out) + b_out
    gated, gate_pull = jax.vjp(gate_mix, project)
    middle = rows_all + gated
    second_float, second_pull = jax.vjp(layer_norm, middle, gain_two)
    second = second_float.astype(bf16)
    before = nn(second, w_in) + b_in
    hidden_float, hidden_pull = jax.vjp(exact_gelu, before)
    hidden = hidden_float.astype(bf16)
    block_out = (middle + nn(hidden, w_back)).astype(bf16)
    upstream = cotangent.reshape(mb * rows, feats)
    grad_back = tn(hidden, upstream)
    grad_before = hidden_pull(nt(upstream, w_back))[0].astype(bf16)
    grad_in = tn(second, grad_before)
    grad_in_bias = jnp.sum(grad_before.astype(f32), axis=0)
    grad_middle, grad_gain_two = second_pull(nt(grad_before, w_in))
    grad_middle = grad_middle + upstream.astype(f32)
    grad_project = gate_pull(grad_middle)[0].astype(bf16)
    grad_out = nn(act_t, grad_project)
    grad_out_bias = jnp.sum(grad_project.astype(f32), axis=0)
    grad_act = nt(w_out, grad_project).astype(bf16).reshape(nj, chans, mb * rows)
    ga = lax.all_to_all(grad_act, "chan", split_axis=0, concat_axis=0, tiled=True)

    gn, zw = ssm_backward(modes, skip, keep, u, ga, slope, carry, mb)
    row_grad = lax.all_to_all(gn, "chan", split_axis=0, concat_axis=0, tiled=True).reshape(feats, mb * rows).T
    grad_rows, grad_gain_one = norm_pull(row_grad.astype(f32))
    grad_tokens = (grad_rows + grad_middle).astype(bf16)

    zw = lax.psum(zw, "dp")
    g_ls, g_ld, g_fr, g_rr, g_ri = (x.reshape(chans, -1) for x in mode_gradients(modes, zw))
    first = lax.axis_index("dp") * groups
    own = [lax.dynamic_slice_in_dim(x, first, groups, 1) for x in (g_ld, g_fr, g_rr, g_ri)]
    g_skip = zw[4].reshape(chans, -1)[:, 0]

    def scatter(x):
        return lax.psum_scatter(x, both, scatter_dimension=0, tiled=True)
    vec = jnp.concatenate([x.reshape(shards, -1) for x in (grad_out_bias, grad_gain_one, grad_gain_two, grad_in_bias)], 1)
    vec = scatter(vec)[0]
    g_bo, g_g1, g_g2, g_bi = (vec[at[k]:at[k + 1]] for k in range(4))
    return (
        block_out.reshape(tokens.shape), grad_tokens.reshape(tokens.shape), g_g1, jnp.sum(g_ls, 1), *own, g_skip,
        scatter(grad_out.astype(bf16)).astype(f32), g_bo, g_g2, scatter(grad_in.astype(bf16)).astype(f32), g_bi, scatter(grad_back.astype(bf16)).astype(f32),
    )


def solution(mesh):
    both = ("dp", "chan")
    rows, row, vec, chan, mode = P(None, both, None), P(both, None), P(both), P("chan"), P("chan", "dp")
    return jax.shard_map(
        on_device, mesh=mesh,
        in_specs=(rows, rows, P(None, "dp"), vec, chan, mode, mode, mode, mode, chan, row, vec, vec, row, vec, row),
        out_specs=(rows, rows, vec, chan, mode, mode, mode, mode, chan, row, vec, vec, row, vec, row),
        check_vma=False,
    )
```

time: 1180 us -> 616 us (0.52); the launches traced: 1170 us -> 615 us
  local copies, waits for them, and re-layouts: 474 us -> 16.2 us
  waiting for transfers between devices: 34.7 us -> 328 us
  matrix products: 270 us -> 54.4 us
  other arithmetic: 168 us -> 20.1 us
  Pallas kernels: 0 us -> 52.3 us
  blocking collectives: 152 us -> 113 us
  starting transfers between devices: 47.7 us -> 15.6 us
    reduce_scatter x3, waiting for transfers between devices: 0.01 us -> 267 us  [scatter(): return lax.psum_scatter(x, both, scatter_dimension=0, tiled=True)]
    dot_general x72 -> x9, matrix products: 270 us -> 54.4 us  [the longest x3 26.6 us: nn(): return jnp.dot(a, b, preferred_element_type=jnp.float32, **kw)]
    reshape x4, local copies, waits for them, and re-layouts: 137 us -> 0.3 us  [on_device(): x.reshape(shards, -1)]
    unnamed x601 -> x49, local copies, waits for them, and re-layouts: 124 us -> 8.27 us
    reduce_sum x14 -> x2, other arithmetic: 99.2 us -> 2.75 us  [the longest x1 2.11 us: on_device(): grad_out_bias = jnp.sum(grad_project.astype(f32), axis=0)]
    pad x6 -> x0, local copies, waits for them, and re-layouts: 73.5 us -> none  [the longest x3 37.7 us: lower_toeplitz(): flat.reshape(block_size, 2 * block_size - 1, channels)[:, :block_size]]
    pallas_call x0 -> x2, Pallas kernels: none -> 52.3 us  [the longest x1 32.8 us: ssm_backward(): pl.pallas_call(functools.partial(backward_kernel, (nj, chans, mb, h)), ou...]
    all_gather x3, waiting for transfers between devices: 3.15 us -> 47.3 us  [the longest x1 39.2 us: on_device(): w_back = lax.all_gather(back_weight, both, axis=0, tiled=True)]
  transfers between devices with their start and end apart: 18 -> 10, of which waited for: 9 -> 7; matrix products, arithmetic and copies ran while one was open for 76% -> 11% of each run, Pallas kernels for 0% -> 9%
where the time goes in v1:
time: 616 us; the launch traced here: 615 us
  waiting for transfers between devices  328 us (53%)
  blocking collectives  113 us (18%)
  matrix products  54.4 us (9%)
  Pallas kernels  52.3 us (8%)
  other arithmetic  20.1 us (3%)
  local copies, waits for them, and re-layouts  16.2 us (3%)
  starting transfers between devices  15.6 us (3%)
  between operations  14.6 us (2%)
    reduce_scatter x3, waiting for transfers between devices, scatter(): return lax.psum_scatter(x, both, scatter_dimension=0, tiled=True)  267 us
    all_gather x1, blocking collectives, on_device(): small = lax.all_gather(small, both, axis=0, tiled=False).astype(f32)  43 us
    all_gather x1, waiting for transfers between devices, on_device(): w_back = lax.all_gather(back_weight, both, axis=0, tiled=True)  39.2 us
    unnamed x1, blocking collectives  38.9 us
    pallas_call x1, Pallas kernels, ssm_backward(): pl.pallas_call(functools.partial(backward_kernel, (nj, chans, mb, h)), ou...  32.8 us
    dot_general x3, matrix products, nn(): return jnp.dot(a, b, preferred_element_type=jnp.float32, **kw)  26.6 us
    pallas_call x1, Pallas kernels, ssm_forward(): pl.pallas_call(functools.partial(forward_kernel, (nj, chans, mb, h)), out...  19.5 us
    psum x1, blocking collectives, on_device(): zw = lax.psum(zw, 'dp')  18.4 us
  transfers between devices with their start and end apart: 10, of which 7 were waited for; matrix products, arithmetic and copies ran while one was open for 11% of the time, Pallas kernels for 9%

profile of v1, /device:TPU:0, one launch (start us, length us, event | category | flops | bytes accessed | tf_op | source)
XLA Modules:
  0.0 614.7 jit_solution(7105509133138976508)
XLA Ops:
  7.2 0.7 all-gather.6.cloned.1.call-update
  8.0 0.7 all-gather.8.cloned.1.call-update
  8.7 0.8 maximum_bitcast_fusion
  9.5 43.0 %all-gather.1 = bf16[32,1,128]{2,1,0:T(2,128)(2,1)S(1)} all-gather(bf16[1,1,128]{2,1,0:T(2,128)(2,1)S(1)} %maximum_bitcast_fusion), channel_id=2, replica_groups=mesh['dp'=4,'chan'=8] {'dp','chan'}, dimensions={0}, use_global_device_ids=true | all-gather | bytes 8448 | tf_op jit(solution)/shard_map/all_gather | solution.py:443
  52.7 1.3 convert_reduce_fusion.2
  54.0 1.5 fusion.18
  55.6 0.3 fusion.15
  56.0 1.2 copy.94
  57.1 3.5 all-to-all-start
  60.7 13.2 %all_gather.18 = f32[4,64,32]{1,0,2:T(4,128)S(1)} all-gather(f32[4,64,8]{1,0,2:T(4,128)S(1)} %copy.85), channel_id=1, replica_groups=mesh['dp'=4,'chan'=8] {'dp'}, dimensions={2}, use_global_device_ids=true | all-gather | bytes 40960 | tf_op jit(solution)/shard_map/all_gather | solution.py:448
  74.9 0.2 fusion.20
  75.4 19.5 %ssm_forward.1 = (bf16[8,64,768]{2,1,0:T(8,128)(2,1)}, f32[4,48,16,128]{3,2,1,0:T(8,128)S(1)}, f32[4,4,256,128]{3,2,1,0:T(8,128)}) custom-call(f32[5,16,128]{2,1,0:T(8,128)S(1)} %constant_dynamic-update-slice_fusion.modes_ref, f32[64,128]{1,0:T(8,128)S(1)} %broadcast_in_dim.47.skip_ref, f32[16,16,128]{2,1,0:T(8,128)S(1)} %broadcast_in_dim.49.keep_ref, ...), custom_call_target="tpu_custom_call" | custom-call | tf_op jit(solution)/shard_map/ssm_forward/pallas_call | solution.py:341
  95.0 1.2 copy-done
  96.2 4.1 all-to-all-start.1
  100.3 0.7 all-gather.10.cloned.1.call-update
  101.3 11.5 %all-to-all-done.1 = bf16[8,64,768]{2,1,0:T(8,128)(2,1)S(1)} async-done(((bf16[8,64,768]{2,1,0:T(8,128)(2,1)}), bf16[8,64,768]{2,1,0:T(8,128)(2,1)S(1)}, u32[]{:S(2)}, u32[]{:S(2)}) %all-to-all-start.1) | async-done | bytes 786464 | tf_op jit(solution)/shard_map/all_to_all | solution.py:462
  112.9 0.9 copy-done.12
  113.7 2.3 convolution_add_fusion
  116.0 0.5 fusion.35
  116.5 1.1 copy-done.4
  117.7 0.3 multiply_reduce_fusion.2
  118.0 8.2 %all-gather.8.cloned.1.call-done = bf16[512,2048]{1,0:T(8,128)(2,1)} async-done(((bf16[16,2048]{1,0:T(8,128)(2,1)}), bf16[512,2048]{1,0:T(8,128)(2,1)}) %all-gather.8.cloned.1.call-update) | async-done | bytes 2097168 | tf_op jit(solution)/shard_map/all_gather | solution.py:450
  126.2 18.9 %multiply_convert_fusion = (bf16[768,2048]{1,0:T(8,128)(2,1)}, f32[768,2048]{1,0:T(8,128)}, f32[768,2048]{1,0:T(8,128)}) fusion(f32[2048]{0:T(1024)S(1)} %add.210, bf16[512,2048]{1,0:T(8,128)(2,1)} %all-gather.8.cloned.1.call-done, f32[768,512]{1,0:T(8,128)S(1)} %get-tuple-element.92, f32[512]{0:T(512)S(1)} %mul.597, f32[768]{0:T(1024)S(1)} %fusion.28, ...), kind=kOutput, calls=%fused_computation.4 | convolution fusion | flops 1715994624 | bytes 19415040 | tf_op jit(solution)/shard_map/dot_general | solution.py:78
  145.1 39.2 %all-gather.10.cloned.1.call-done = bf16[2048,512]{1,0:T(8,128)(2,1)} async-done(((bf16[64,512]{1,0:T(8,128)(2,1)}), bf16[2048,512]{1,0:T(8,128)(2,1)}) %all-gather.10.cloned.1.call-update) | async-done | bytes 2097168 | tf_op jit(solution)/shard_map/all_gather | solution.py:451
  184.3 9.3 %convert_reduce_fusion = (f32[2048]{0:T(1024)S(1)}, bf16[768,2048]{1,0:T(8,128)(2,1)S(1)}) fusion(f32[768,2048]{1,0:T(8,128)} %get-tuple-element.90, bf16[768,512]{1,0:T(8,128)(2,1)} %bitcast.132, bf16[2048,512]{1,0:T(8,128)(2,1)} %all-gather.10.cloned.1.call-done, f32[768,2048]{1,0:T(8,128)} %get-tuple-element.118, f32[2048]{0:T(1024)S(1)} %add.210), kind=kOutput, calls=%fused_computation.2 | convolution fusion | flops 1637349376 | bytes 18628608 | tf_op jit(solution)/shard_map/dot_general | solution.py:70
  193.6 2.1 multiply_reduce_fusion
  195.8 0.6 fusion.33
  196.5 1.8 copy-done.5
  198.3 0.2 copy-done.10
  198.4 0.7 fusion.6
  199.1 1.2 copy-done.6
  200.3 0.5 copy-done.8
  200.8 2.0 convolution_convert_fusion.2
  202.8 0.3 reduce-scatter.6.cloned.1.call-start
  203.1 5.2 convolution_convert_fusion.1
  208.3 1.3 copy-done.7
  209.7 3.6 convolution_convert_fusion.3
  213.3 3.5 all-to-all-start.2
  216.9 5.3 convolution_convert_fusion
  222.2 2.1 convert_reduce_fusion.1
  224.5 5.7 add_convert_fusion.3
  230.2 0.1 all-to-all-done.2.ga_ref
  230.3 32.8 %ssm_backward.1 = (bf16[8,64,768]{2,1,0:T(8,128)(2,1)}, f32[5,16,128]{2,1,0:T(8,128)S(1)}) custom-call(f32[5,16,128]{2,1,0:T(8,128)S(1)} %constant_dynamic-update-slice_fusion.modes_ref, f32[64,128]{1,0:T(8,128)S(1)} %broadcast_in_dim.47.skip_ref, f32[16,16,128]{2,1,0:T(8,128)S(1)} %broadcast_in_dim.49.keep_ref, bf16[8,64,768]{2,1,0:T(8,128)(2,1)S(1)} %all-to-all-done.u_ref, ...), custom_call_target="tpu_custom_call" | custom-call | tf_op jit(solution)/shard_map/ssm_backward/pallas_call | solution.py:365
  263.1 4.0 all-to-all-start.3
  267.0 18.4 %psum.7 = f32[5,16,128]{2,1,0:T(8,128)S(1)} all-reduce(f32[5,16,128]{2,1,0:T(8,128)S(1)} %get-tuple-element.24), channel_id=1, replica_groups=mesh['dp'=4,'chan'=8] {'dp'}, use_global_device_ids=true, to_apply=%region_13.14 | all-reduce | flops 10240 | bytes 81920 | tf_op jit(solution)/shard_map/psum | solution.py:491
  285.5 0.6 slice_reduce_fusion
  286.7 0.2 multiply_add_fusion.2
  286.9 0.6 multiply_reduce_fusion.3
  287.5 0.6 fusion.25
  288.1 1.4 bitcast_convert_fusion
  289.5 1.9 copy.95
  291.4 0.5 fusion.16
  291.9 0.8 fusion.10
  292.8 38.9 %all-reduce.2 = f32[32,128]{1,0:T(8,128)S(1)} all-reduce(f32[32,128]{1,0:T(8,128)S(1)} %pad_maximum_fusion.1), channel_id=3, replica_groups=mesh['dp'=4,'chan'=8] {'dp','chan'}, use_global_device_ids=true, to_apply=%region_12.13.clone | all-reduce | flops 4096 | bytes 32768
  331.8 0.6 slice_bitcast_fusion
  332.3 0.5 slice_bitcast_fusion.2
  332.9 0.6 slice_bitcast_fusion.1
  333.4 3.1 add_convert_fusion.2
  336.5 1.1 reduce-scatter.4.cloned.1.call-done
  337.6 1.4 convert_element_type.100
  338.9 133.1 %reduce-scatter.6.cloned.1.call-done = bf16[16,2048]{1,0:T(8,128)(2,1)} async-done(((bf16[512,2048]{1,0:T(8,128)(2,1)}), bf16[16,2048]{1,0:T(8,128)(2,1)}) %reduce-scatter.6.cloned.1.call-update) | async-done | bytes 65552 | tf_op jit(solution)/shard_map/reduce_scatter | solution.py:498
  472.1 1.5 convert_element_type.102
  473.6 132.8 %reduce-scatter.8.cloned.1.call-done = bf16[64,512]{1,0:T(8,128)(2,1)} async-done(((bf16[2048,512]{1,0:T(8,128)(2,1)}), bf16[64,512]{1,0:T(8,128)(2,1)}) %reduce-scatter.8.cloned.1.call-update) | async-done | bytes 65552 | tf_op jit(solution)/shard_map/reduce_scatter | solution.py:498
  606.4 1.5 convert_element_type.104
  (109 shorter events, 3.2 us)
Async XLA Ops:
  7.2 48.4 %copy-start.1 = (bf16[3,256,512]{2,1,0:T(8,128)(2,1)S(1)}, bf16[3,256,512]{2,1,0:T(8,128)(2,1)}, u32[]{:S(2)}) copy-start(bf16[3,256,512]{2,1,0:T(8,128)(2,1)} %param.16) | copy-start | bytes 2359300
  7.2 105.7 %all-gather.6.cloned.1.call-start = ((), (), s32[]{:S(2)}) async-start(), calls=%async_computation.7 | async-start | bytes 1081344 | tf_op jit(solution)/shard_map/all_gather | solution.py:449
  7.9 118.2 %all-gather.8.cloned.1.call-start = ((), (), s32[]{:S(2)}) async-start(), calls=%async_computation.8 | async-start | bytes 2162688 | tf_op jit(solution)/shard_map/all_gather | solution.py:450
  55.5 5.1 copy-start.14
  55.6 5.1 copy-start.15
  55.6 5.1 copy-start.16
  55.6 5.1 copy-start.17
  55.9 18.2 %copy-start.19 = (f32[64]{0:T(128)S(1)}, f32[64]{0:T(128)}, u32[]{:S(2)}) copy-start(f32[64]{0:T(128)} %param.20) | copy-start | bytes 772
  55.9 18.9 %copy-start.21 = (s32[3,1]{0,1:T(1,128)S(1)}, s32[3,1]{0,1:T(1,128)}, u32[]{:S(2)}) copy-start(s32[3,1]{0,1:T(1,128)} %param.18) | copy-start | bytes 40
  56.0 19.4 %copy-start.18 = (f32[64]{0:T(128)S(1)}, f32[64]{0:T(128)}, u32[]{:S(2)}) copy-start(f32[64]{0:T(128)} %param.25) | copy-start | bytes 772
  57.1 18.1 %all-to-all-start = ((bf16[8,64,768]{2,1,0:T(8,128)(2,1)}), bf16[8,64,768]{2,1,0:T(8,128)(2,1)S(1)}, u32[]{:S(2)}, u32[]{:S(2)}) async-start(bf16[8,64,768]{2,1,0:T(8,128)(2,1)} %bitcast.9), calls=%async_computation | async-start | bytes 1572864 | tf_op jit(solution)/shard_map/all_to_all | solution.py:456
  95.0 1.2 copy-start
  96.2 16.7 %all-to-all-start.1 = ((bf16[8,64,768]{2,1,0:T(8,128)(2,1)}), bf16[8,64,768]{2,1,0:T(8,128)(2,1)S(1)}, u32[]{:S(2)}, u32[]{:S(2)}) async-start(bf16[8,64,768]{2,1,0:T(8,128)(2,1)} %get-tuple-element.20), calls=%async_computation.1 | async-start | bytes 1572864 | tf_op jit(solution)/shard_map/all_to_all | solution.py:462
  100.2 84.1 %all-gather.10.cloned.1.call-start = ((), (), s32[]{:S(2)}) async-start(), calls=%async_computation.9 | async-start | bytes 2162688 | tf_op jit(solution)/shard_map/all_gather | solution.py:451
  101.0 236.6 %reduce-scatter.4.cloned.1.call-start = ((), (), s32[]{:S(2)}) async-start(), calls=%async_computation.10 | async-start | bytes 1081344 | tf_op jit(solution)/shard_map/reduce_scatter | solution.py:498
  112.8 0.9 copy-start.12
  116.0 1.7 copy-start.4
  117.7 85.4 %copy-start.2 = (f32[768,512]{1,0:T(8,128)}, f32[768,512]{1,0:T(8,128)S(1)}, u32[]{:S(2)}) copy-start(f32[768,512]{1,0:T(8,128)S(1)} %get-tuple-element.92) | copy-start | bytes 4718596
  184.3 9.3 %copy-start.20 = (bf16[512,2048]{1,0:T(8,128)(2,1)S(1)}, bf16[512,2048]{1,0:T(8,128)(2,1)}, u32[]{:S(2)}) copy-start(bf16[512,2048]{1,0:T(8,128)(2,1)} %all-gather.8.cloned.1.call-done) | copy-start | bytes 6291460
  193.6 2.2 copy-start.9
  195.8 2.5 copy-start.5
  195.8 2.6 copy-start.10
  196.5 2.6 copy-start.3
  198.4 2.3 copy-start.13
  199.1 1.2 copy-start.6
  199.1 1.7 copy-start.8
  202.8 269.3 %reduce-scatter.6.cloned.1.call-start = ((), (), s32[]{:S(2)}) async-start(), calls=%async_computation.11 | async-start | bytes 2162688 | tf_op jit(solution)/shard_map/reduce_scatter | solution.py:498
  208.3 1.4 copy-start.7
  213.3 17.0 %all-to-all-start.2 = ((bf16[8,64,768]{2,1,0:T(8,128)(2,1)}), bf16[8,64,768]{2,1,0:T(8,128)(2,1)S(1)}, u32[]{:S(2)}, u32[]{:S(2)}) async-start(bf16[8,64,768]{2,1,0:T(8,128)(2,1)} %bitcast.136), calls=%async_computation.2 | async-start | bytes 1572864 | tf_op jit(solution)/shard_map/all_to_all | solution.py:484
  216.8 389.5 %reduce-scatter.8.cloned.1.call-start = ((), (), s32[]{:S(2)}) async-start(), calls=%async_computation.12 | async-start | bytes 2162688 | tf_op jit(solution)/shard_map/reduce_scatter | solution.py:498
  263.1 25.0 %all-to-all-start.3 = ((bf16[8,64,768]{2,1,0:T(8,128)(2,1)}), bf16[8,64,768]{2,1,0:T(8,128)(2,1)S(1)}, u32[]{:S(2)}, u32[]{:S(2)}) async-start(bf16[8,64,768]{2,1,0:T(8,128)(2,1)} %get-tuple-element.23), calls=%async_computation.3 | async-start | bytes 1572864 | tf_op jit(solution)/shard_map/all_to_all | solution.py:487
  291.4 42.1 %copy-start.11 = (bf16[3,256,512]{2,1,0:T(8,128)(2,1)S(1)}, bf16[3,256,512]{2,1,0:T(8,128)(2,1)}, u32[]{:S(2)}) copy-start(bf16[3,256,512]{2,1,0:T(8,128)(2,1)} %param.17) | copy-start | bytes 2359300
Sparse Core Ops, SparseCore 0:
  10.9 57.4 all-gather.5
  71.2 54.9 all-gather.7
  129.0 55.2 all-gather.9
  202.9 134.5 reduce-scatter.3
  339.8 132.2 reduce-scatter.5
  474.2 132.1 reduce-scatter.7

commit v2 on v1

v2 whole, which is shorter than its diff:
```python
import functools
import jax
import jax.numpy as jnp
from jax import lax
from jax.experimental import pallas as pl
from jax.experimental.pallas import tpu as pltpu
from jax.sharding import PartitionSpec as P

SPAN = 128
PACK = 16
HI = lax.Precision.HIGHEST


def cmul(ar, ai, br, bi):
    return ar * br - ai * bi, ar * bi + ai * br


def mode_rows(ls, ld, fr, rr, ri):
    dt = jnp.exp(ls)
    a_r = -jnp.exp(ld)
    a_i = fr
    t_r, t_i = dt * a_r, dt * a_i
    mag = jnp.exp(t_r)
    l_r, l_i = mag * jnp.cos(t_i), mag * jnp.sin(t_i)
    mod = a_r * a_r + a_i * a_i
    u_r = l_r - 1.0
    q_r = (u_r * a_r + l_i * a_i) / mod
    q_i = (l_i * a_r - u_r * a_i) / mod
    w_r, w_i = cmul(rr, ri, q_r, q_i)
    return dict(dt=dt, a_r=a_r, a_i=a_i, t_r=t_r, t_i=t_i, l_r=l_r, l_i=l_i, mod=mod,
                q_r=q_r, q_i=q_i, w_r=w_r, w_i=w_i)


def mode_prelude(modes_ref, pw_ref):
    m = mode_rows(modes_ref[0], modes_ref[1], modes_ref[2], modes_ref[3], modes_ref[4])
    r, i = m["l_r"], m["l_i"]
    for k in range(8):
        pw_ref[2 * k] = r
        pw_ref[2 * k + 1] = i
        r, i = cmul(r, i, r, i)
    pw_ref[16] = 2.0 * m["w_r"]
    pw_ref[17] = 2.0 * m["w_i"]


def group_rows(pw_ref, g):
    rows = [pw_ref[k, pl.ds(g, 1), :] for k in range(18)]
    return [jnp.broadcast_to(x, (8, 128)) for x in rows]


def power_table(rows, reverse):
    sub = lax.broadcasted_iota(jnp.int32, (8, 128), 0)
    if reverse:
        sub = 7 - sub
        r, i = jnp.ones((8, 128), jnp.float32), jnp.zeros((8, 128), jnp.float32)
    else:
        r, i = rows[0], rows[1]
    for k in range(3):
        bit = ((sub >> k) & 1) == 1
        fr = jnp.where(bit, rows[2 * k], 1.0)
        fi = jnp.where(bit, rows[2 * k + 1], 0.0)
        r, i = cmul(r, i, fr, fi)
    parts = [(r, i)]
    for k in range(3, 7):
        more = [cmul(a, b, rows[2 * k], rows[2 * k + 1]) for a, b in parts]
        parts = more + parts if reverse else parts + more
    return (jnp.concatenate([p[0] for p in parts], 0), jnp.concatenate([p[1] for p in parts], 0))


def nt(a, b, **kw):
    return lax.dot_general(a, b, (((1,), (1,)), ((), ())), preferred_element_type=jnp.float32, **kw)


def tn(a, b, **kw):
    return lax.dot_general(a, b, (((0,), (0,)), ((), ())), preferred_element_type=jnp.float32, **kw)


def nn(a, b, **kw):
    return jnp.dot(a, b, preferred_element_type=jnp.float32, **kw)


def kernel_rows(rd_r, w_r):
    t = lax.broadcasted_iota(jnp.int32, (SPAN, 128), 0)
    src = jnp.where(t == SPAN - 1, jnp.concatenate([w_r] * 16, 0), rd_r)
    pick = (lax.broadcasted_iota(jnp.int32, (8, 128), 1) // 32
            == lax.broadcasted_iota(jnp.int32, (8, 128), 0)).astype(jnp.float32)
    return pltpu.roll(nt(pick, src, precision=HI), 1, 1)


def toeplitz(row):
    base = pltpu.roll(jnp.broadcast_to(row, (8, 128)), 0, 1, stride=1, stride_axis=0)
    parts = [base] + [pltpu.roll(base, 8 * v, 1) for v in range(1, 16)]
    whole = jnp.concatenate(parts, 0)
    s = lax.broadcasted_iota(jnp.int32, (SPAN, 128), 0)
    t = lax.broadcasted_iota(jnp.int32, (SPAN, 128), 1)
    return jnp.where(t >= s, whole, 0.0).astype(jnp.bfloat16)


def lag_sums(g):
    s = lax.broadcasted_iota(jnp.int32, (SPAN, 128), 0)
    t = lax.broadcasted_iota(jnp.int32, (SPAN, 128), 1)
    g = jnp.where(t >= s, g, 0.0)
    n = SPAN
    while n > 8:
        n //= 2
        g = g[:n] + pltpu.roll(g[n:], 128 - n, 1)
    for n in (4, 2, 1):
        g = g + pltpu.roll(pltpu.roll(g, 128 - n, 1), 8 - n, 0)
    return g[0:1]


def lane_owner(rows):
    return lax.broadcasted_iota(jnp.int32, (rows, 128), 1) // 32


def fold(stack, rows):
    width = stack.shape[1]
    own = (lax.broadcasted_iota(jnp.int32, (rows, width), 1) // 32) & 3
    out = stack[:rows]
    for k in range(1, 4):
        out = jnp.where(own == k, stack[k * rows:(k + 1) * rows], out)
    return out


def spread(packed, rows):
    width = packed.shape[1]
    own = (lax.broadcasted_iota(jnp.int32, (rows, width), 1) // 32) & 3
    return jnp.concatenate([jnp.where(own == k, packed, 0.0) for k in range(4)], 0)


def gelu_pair(v):
    half = 0.5 * (1.0 + lax.erf(v * 0.7071067811865476))
    return v * half, half + v * jnp.exp(-0.5 * v * v) * 0.3989422804014327


def block_rows(r):
    return pl.ds(pl.multiple_of(r * PACK, PACK), PACK)


def unpack(src_ref, q, xs, nj, mb, h, blocks, scale=None):
    def body(j, _):
        for m in range(mb):
            for k in range(h):
                x = src_ref[j, block_rows(q), pl.ds((m * h + k) * 128, 128)]
                xs[block_rows(m * blocks + j * h + k), :] = x.astype(jnp.float32)
        return 0
    lax.fori_loop(0, nj, body, 0)


def rows_of(pw_ref, k, q, mb):
    parts = [jnp.broadcast_to(pw_ref[k, pl.ds(q * 4 + g, 1), :], (mb, 128)) for g in range(4)]
    parts.append(jnp.zeros((PACK - 4 * mb, 128), jnp.float32))
    return jnp.concatenate(parts, 0)


def forward_pack(dims, q, skip_ref, keep_ref, u_ref, act_ref, slope_ref, carry_ref, pw_ref, xs, ys, sc):
    nj, chans, mb, h = dims
    blocks = nj * h
    rows = mb * blocks
    unpack(u_ref, q, xs, nj, mb, h, blocks)

    def states(g, _):
        rws = group_rows(pw_ref, q * 4 + g)
        p_r, p_i = power_table(rws, True)
        back = (SPAN - 1 - lax.broadcasted_iota(jnp.int32, (SPAN, 128), 0)).astype(jnp.float32)
        table = jnp.concatenate([p_r, p_i, back * p_r, back * p_i], 1).astype(jnp.bfloat16)
        x = jnp.concatenate([xs[pl.ds(4 * g + k, rows, stride=PACK), :] for k in range(4)], 0).astype(jnp.bfloat16)
        s = fold(nn(x, table), rows)
        for a in range(4):
            for m in range(mb):
                sc[a, pl.ds(g * mb + m, blocks, stride=PACK), :] = s[m * blocks:(m + 1) * blocks, a * 128:(a + 1) * 128]
        return 0
    lax.fori_loop(0, 4, states, 0, unroll=2)
    h_r, h_i = rows_of(pw_ref, 14, q, mb), rows_of(pw_ref, 15, q, mb)

    def step(i, c):
        at = block_rows(i)
        keep = keep_ref[i]
        c = [x * keep for x in c]
        s = [sc[a, at, :] for a in range(4)]
        for a in range(4):
            carry_ref[q, a, at, :] = c[a]
        z_r, z_i = cmul(c[0], c[1], h_r, h_i)
        d_r, d_i = cmul(c[2] + SPAN * c[0], c[3] + SPAN * c[1], h_r, h_i)
        return (z_r + s[0], z_i + s[1], d_r + s[2], d_i + s[3])
    zero = jnp.zeros((PACK, 128), jnp.float32)
    lax.fori_loop(0, blocks, step, (zero,) * 4)

    def outputs(g, _):
        rws = group_rows(pw_ref, q * 4 + g)
        e_r, e_i = power_table(rws, False)
        w_r, w_i = jnp.concatenate([rws[16]] * 16, 0), jnp.concatenate([rws[17]] * 16, 0)
        r_r, r_i = cmul(e_r, e_i, w_r, w_i)
        krow = kernel_rows(r_r, rws[16])
        table = jnp.concatenate([r_r, -r_i], 1).astype(jnp.bfloat16)
        c = jnp.concatenate([
            jnp.concatenate([carry_ref[q, a, pl.ds(g * mb + m, blocks, stride=PACK), :] for m in range(mb)], 0)
            for a in range(2)], 1)
        across = nt(spread(c, rows).astype(jnp.bfloat16), table)
        for k in range(4):
            x = xs[pl.ds(4 * g + k, rows, stride=PACK), :].astype(jnp.bfloat16)
            y = across[k * rows:(k + 1) * rows] + nn(x, toeplitz(krow[k:k + 1]))
            ys[pl.ds(4 * g + k, rows, stride=PACK), :] = y
        return 0
    lax.fori_loop(0, 4, outputs, 0, unroll=2)
    skip = skip_ref[block_rows(q), :]

    def finish(j, _):
        for m in range(mb):
            for k in range(h):
                r = m * blocks + j * h + k
                v = ys[block_rows(r), :] + skip * xs[block_rows(r), :]
                a, d = gelu_pair(v)
                act_ref[j, block_rows(q), pl.ds((m * h + k) * 128, 128)] = a.astype(jnp.bfloat16)
                slope_ref[q, block_rows(r), :] = d
        return 0
    lax.fori_loop(0, nj, finish, 0)


def backward_pack(dims, q, skip_ref, keep_ref, u_ref, ga_ref, slope_ref, carry_ref, gn_ref, zw_ref, pw_ref, xs, gy, gx, sc):
    nj, chans, mb, h = dims
    blocks = nj * h
    rows = mb * blocks
    unpack(u_ref, q, xs, nj, mb, h, blocks)
    def start(j, _):
        for m in range(mb):
            for k in range(h):
                r = m * blocks + j * h + k
                x = ga_ref[j, block_rows(q), pl.ds((m * h + k) * 128, 128)]
                gy[block_rows(r), :] = x.astype(jnp.float32) * slope_ref[q, block_rows(r), :]
        return 0
    lax.fori_loop(0, nj, start, 0)

    def states(g, _):
        gg = q * 4 + g
        rws = group_rows(pw_ref, gg)
        e_r, e_i = power_table(rws, False)
        ahead = (1 + lax.broadcasted_iota(jnp.int32, (SPAN, 128), 0)).astype(jnp.float32)
        table = jnp.concatenate([e_r, e_i, ahead * e_r, ahead * e_i], 1).astype(jnp.bfloat16)
        ups = [gy[pl.ds(4 * g + k, rows, stride=PACK), :].astype(jnp.bfloat16) for k in range(4)]
        lag = []
        for k in range(4):
            x = xs[pl.ds(4 * g + k, rows, stride=PACK), :].astype(jnp.bfloat16)
            lag.append(lag_sums(tn(x, ups[k])))
        lag = jnp.concatenate(lag + [jnp.zeros((4, 128), jnp.float32)], 0)
        own8 = lax.broadcasted_iota(jnp.int32, (8, 128), 1) // 32 == lax.broadcasted_iota(jnp.int32, (8, 128), 0)
        lag0 = jnp.sum(jnp.where(own8, jnp.broadcast_to(lag[:, 0:1], (8, 128)), 0.0), axis=0, keepdims=True)
        lane = lax.broadcasted_iota(jnp.int32, (8, 128), 1)
        later = jnp.where(lane == 127, 0.0, pltpu.roll(lag, 127, 1))
        top = later.astype(jnp.bfloat16)
        low = (later - top.astype(jnp.float32)).astype(jnp.bfloat16)
        stack = jnp.concatenate(ups + [top, low], 0)
        s = nn(stack, table)
        near = s[4 * rows:4 * rows + 8] + s[4 * rows + 8:]
        own = jnp.concatenate([own8] * 4, 1)
        near = jnp.sum(jnp.where(own, near, 0.0), axis=0, keepdims=True)
        zw_ref[0, pl.ds(gg, 1), :] = near[:, 0:128] + lag0
        for a in range(1, 4):
            zw_ref[a, pl.ds(gg, 1), :] = near[:, a * 128:(a + 1) * 128]
        zw_ref[4, pl.ds(gg, 1), :] = lag0
        s = fold(s[:4 * rows], rows)
        for a in range(4):
            for m in range(mb):
                sc[a, pl.ds(g * mb + m, blocks, stride=PACK), :] = s[m * blocks:(m + 1) * blocks, a * 128:(a + 1) * 128]
        return 0
    lax.fori_loop(0, 4, states, 0, unroll=2)

    h_r, h_i = rows_of(pw_ref, 14, q, mb), rows_of(pw_ref, 15, q, mb)

    def step(n, c):
        i = blocks - 1 - n
        at = block_rows(i)
        a_r, a_i, z_r, z_i, w_r, w_i = c
        q_ = [sc[a, at, :] for a in range(4)]
        f = [carry_ref[q, a, at, :] for a in range(4)]
        d = cmul(q_[0], q_[1], f[0], f[1])
        e1 = cmul(q_[2], q_[3], f[0], f[1])
        e2 = cmul(q_[0], q_[1], f[2], f[3])
        sc[0, at, :] = a_r
        sc[1, at, :] = a_i
        keep = keep_ref[i]
        n_r, n_i = cmul(a_r, a_i, h_r, h_i)
        return ((n_r + q_[0]) * keep, (n_i + q_[1]) * keep, z_r + d[0], z_i + d[1], w_r + e1[0] + e2[0], w_i + e1[1] + e2[1])
    zero = jnp.zeros((PACK, 128), jnp.float32)
    out = lax.fori_loop(0, blocks, step, (zero,) * 6)
    for a in range(4):
        for g in range(4):
            add = jnp.sum(out[2 + a][g * mb:(g + 1) * mb], axis=0, keepdims=True)
            zw_ref[a, pl.ds(q * 4 + g, 1), :] += add

    def outputs(g, _):
        rws = group_rows(pw_ref, q * 4 + g)
        e_r, e_i = power_table(rws, False)
        w_r, w_i = jnp.concatenate([rws[16]] * 16, 0), jnp.concatenate([rws[17]] * 16, 0)
        r_r = e_r * w_r - e_i * w_i
        krow = kernel_rows(r_r, rws[16])
        p_r, p_i = power_table(rws, True)
        r_r, r_i = cmul(p_r, p_i, w_r, w_i)
        table = jnp.concatenate([r_r, -r_i], 1).astype(jnp.bfloat16)
        c = jnp.concatenate([
            jnp.concatenate([sc[a, pl.ds(g * mb + m, blocks, stride=PACK), :] for m in range(mb)], 0)
            for a in range(2)], 1)
        across = nt(spread(c, rows).astype(jnp.bfloat16), table)
        for k in range(4):
            up = gy[pl.ds(4 * g + k, rows, stride=PACK), :].astype(jnp.bfloat16)
            y = across[k * rows:(k + 1) * rows] + nt(up, toeplitz(krow[k:k + 1]))
            gx[pl.ds(4 * g + k, rows, stride=PACK), :] = y
        return 0
    lax.fori_loop(0, 4, outputs, 0, unroll=2)

    skip = skip_ref[block_rows(q), :]
    def finish(j, _):
        for m in range(mb):
            for k in range(h):
                r = m * blocks + j * h + k
                v = gx[block_rows(r), :] + skip * gy[block_rows(r), :]
                gn_ref[j, block_rows(q), pl.ds((m * h + k) * 128, 128)] = v.astype(jnp.bfloat16)
        return 0
    lax.fori_loop(0, nj, finish, 0)


def backward_kernel(dims, modes_ref, skip_ref, keep_ref, u_ref, ga_ref, slope_ref, carry_ref, gn_ref, zw_ref, pw_ref, xs, gy, gx, sc):
    mode_prelude(modes_ref, pw_ref)
    sc[...] = jnp.zeros(sc.shape, jnp.float32)

    def one(q, _):
        backward_pack(dims, q, skip_ref, keep_ref, u_ref, ga_ref, slope_ref, carry_ref, gn_ref, zw_ref, pw_ref, xs, gy, gx, sc)
        return 0
    lax.fori_loop(0, dims[1] // PACK, one, 0)


def ssm_backward(modes, skip, keep, u, ga, slope, carry, mb):
    nj, chans, width = u.shape
    h = width // mb // 128
    blocks = nj * h
    rows = mb * blocks
    f32 = jnp.float32
    return pl.pallas_call(
        functools.partial(backward_kernel, (nj, chans, mb, h)),
        out_shape=(
            jax.ShapeDtypeStruct(u.shape, jnp.bfloat16),
            jax.ShapeDtypeStruct((5, modes.shape[1], 128), f32),
        ),
        scratch_shapes=[
            pltpu.VMEM((18, modes.shape[1], 128), f32),
            pltpu.VMEM((rows * PACK, 128), f32),
            pltpu.VMEM((rows * PACK, 128), f32),
            pltpu.VMEM((rows * PACK, 128), f32),
            pltpu.VMEM((4, blocks * PACK, 128), f32),
        ],
        compiler_params=pltpu.CompilerParams(vmem_limit_bytes=50 << 20),
        name="ssm_backward",
    )(modes, skip, keep, u, ga, slope, carry)


def mode_gradients(modes, zw):
    m = mode_rows(*modes)
    z_r, z_i, v_r, v_i = zw[0], zw[1], zw[2], zw[3]
    rr, ri = modes[3], modes[4]
    g_rr = 2.0 * (z_r * m["q_r"] - z_i * m["q_i"])
    g_ri = -2.0 * (z_r * m["q_i"] + z_i * m["q_r"])
    k_r, k_i = cmul(rr, ri, m["a_r"] / m["mod"], -m["a_i"] / m["mod"])
    s_r, s_i = cmul(k_r, k_i, m["l_r"], m["l_i"])
    h1 = cmul(z_r, z_i, s_r, s_i)
    h2 = cmul(m["w_r"], m["w_i"], v_r, v_i)
    h_r, h_i = h1[0] + h2[0], h1[1] + h2[1]
    zc = cmul(z_r, z_i, m["w_r"], m["w_i"])
    za = cmul(zc[0], zc[1], m["a_r"] / m["mod"], -m["a_i"] / m["mod"])
    j_r, j_i = h_r * m["dt"] - za[0], h_i * m["dt"] - za[1]
    g_ls = 2.0 * (h_r * m["t_r"] - h_i * m["t_i"])
    return g_ls, 2.0 * m["a_r"] * j_r, -2.0 * j_i, g_rr, g_ri


def keep_rows(lengths, blocks, mb):
    at = jnp.arange(blocks, dtype=jnp.int32)[:, None] * SPAN
    keep = (at % lengths[None, :] != 0).astype(jnp.float32)
    rows = jnp.concatenate([keep] * 4 + [jnp.zeros((blocks, PACK - 4 * mb), jnp.float32)], 1)
    return jnp.broadcast_to(rows[:, :, None], (blocks, PACK, 128))


def mode_stack(log_step, ld, fr, rr, ri):
    nh = ld.shape[1]
    ls = jnp.broadcast_to(log_step[:, None], ld.shape)
    return jnp.stack([x.reshape(-1, 128) for x in (ls, ld, fr, rr, ri)])


MESH = pl.DeviceIdType.MESH


def layer_stats(v):
    average = jnp.mean(v, axis=-1, keepdims=True)
    centred = v - average
    spread = jnp.mean(centred * centred, axis=-1, keepdims=True)
    return centred, lax.rsqrt(spread + 1e-05)


def peers(count, me):
    return [lax.rem(me + k, count) for k in range(1, count)]


def greet(n_dp, n_chan, d, c):
    barrier = pltpu.get_barrier_semaphore()
    for p in peers(n_dp, d):
        pl.semaphore_signal(barrier, inc=1, device_id=(p, c), device_id_type=MESH)
    for p in peers(n_chan, c):
        pl.semaphore_signal(barrier, inc=1, device_id=(d, p), device_id_type=MESH)
    pl.semaphore_wait(barrier, n_dp + n_chan - 2)


def send(src, dst, send_sem, recv_sem, to):
    copy = pltpu.make_async_remote_copy(src_ref=src, dst_ref=dst, send_sem=send_sem, recv_sem=recv_sem, device_id=to, device_id_type=MESH)
    copy.start()
    return copy


def exchange_start(box, sems, axis_count, me, to):
    for p in peers(axis_count, me):
        send(box.at[me], box.at[me], sems.at[0], sems.at[1], to(p))


def exchange_wait(box, sems, axis_count, to):
    if axis_count > 1:
        whole = box.at[pl.ds(0, axis_count - 1)]
        pltpu.make_async_remote_copy(src_ref=whole, dst_ref=whole, send_sem=sems.at[0], recv_sem=sems.at[1], device_id=to, device_id_type=MESH).wait()


class Spread:
    def __init__(self, wholes, sems, d, c):
        self.wholes, self.sems = wholes, sems
        self.d, self.c = d, c
        self.a, self.b, self.core = c // 4, lax.rem(c // 2, 2), lax.rem(c, 2)
        self.used = 0
        self.open = []

    def chan(self, a, b, core):
        return (self.d, a * 4 + b * 2 + core)

    def put(self, ref, to):
        n = self.used
        self.used += 1
        return send(ref, ref, self.sems.at[0, n], self.sems.at[1, n], to)

    def halves(self, w):
        cols = w.shape[-1] // 2
        return pl.ds(0, cols), pl.ds(cols, cols)

    def along_dp(self, owns, n_dp):
        a, b, core, d = self.a, self.b, self.core, self.d
        self.step = []
        for own, w in zip(owns, self.wholes):
            w[d, a, b, core] = own[...]
        for w in self.wholes:
            for p in peers(n_dp, d):
                self.step.append(self.put(w.at[d, a, b, core], (p, self.c)))

    def arrived(self):
        for copy in self.step:
            copy.wait_recv()
        self.open += self.step
        self.step = []

    def first_hop(self):
        a, b, core = self.a, self.b, self.core
        self.arrived()
        for w in self.wholes:
            low, high = self.halves(w)
            self.step.append(self.put(w.at[:, a, b, core, :, low], self.chan(a, 1 - b, core)))
            self.step.append(self.put(w.at[:, a, b, core, :, high], self.chan(1 - a, b, core)))
        self.side = [self.put(w.at[:, a, b, core], self.chan(a, b, 1 - core)) for w in self.wholes]

    def second_hop(self):
        a, b, core = self.a, self.b, self.core
        self.arrived()
        for w in self.wholes:
            low, high = self.halves(w)
            self.step.append(self.put(w.at[:, a, :, core, :, low], self.chan(1 - a, b, core)))
            self.step.append(self.put(w.at[:, :, b, core, :, high], self.chan(a, 1 - b, core)))
        other = self.chan(a, b, 1 - core)
        for w in self.wholes:
            low, high = self.halves(w)
            self.side.append(self.put(w.at[:, a, 1 - b, core, :, low], other))
            self.side.append(self.put(w.at[:, 1 - a, b, core, :, high], other))

    def last_hop(self):
        a, b, core = self.a, self.b, self.core
        self.arrived()
        other = self.chan(a, b, 1 - core)
        for w in self.wholes:
            low, high = self.halves(w)
            self.side.append(self.put(w.at[:, 1 - a, :, core, :, low], other))
            self.side.append(self.put(w.at[:, :, 1 - b, core, :, high], other))

    def finish(self):
        for copy in self.side:
            copy.wait_recv()
        for copy in self.open + self.side:
            copy.wait_send()


def entry_kernel(dims, n_dp, direct, *refs):
    (nj, chans, mb, h) = dims
    refs = list(refs)
    tokens_ref, vec_ref, modes_ref, skip_ref, keep_ref = refs[:5]
    del refs[:5]
    owns = [refs.pop(0) for _ in range(3)] if direct else []
    u_ref, act_ref, slope_ref, carry_ref, vec_out, modes_out = refs[:6]
    del refs[:6]
    wholes = [refs.pop(0) for _ in range(3)] if direct else []
    snd, out, vec_dp, vec_chan, modes_dp, pw, xs, ys, sc = refs[:9]
    del refs[:9]
    vec_sems, modes_sems, in_sems, out_sems = refs[:4]
    del refs[:4]
    d, c = lax.axis_index("dp"), lax.axis_index("chan")
    packs = chans // PACK
    width = tokens_ref.shape[0]
    t = width // mb
    feats = nj * chans

    greet(n_dp, nj, d, c)
    vec_dp[d] = vec_ref[...]
    modes_dp[d] = modes_ref[pl.ds(1, 4)]
    exchange_start(vec_dp, vec_sems.at[0], n_dp, d, lambda p: (p, c))
    exchange_start(modes_dp, modes_sems, n_dp, d, lambda p: (p, c))
    if direct:
        spread = Spread(wholes, refs[0], d, c)
        spread.along_dp(owns, n_dp)
    exchange_wait(vec_dp, vec_sems.at[0], n_dp, (d, c))
    vec_chan[c] = sum(vec_dp[k] for k in range(n_dp))
    exchange_start(vec_chan, vec_sems.at[1], nj, c, lambda p: (d, p))
    exchange_wait(modes_dp, modes_sems, n_dp, (d, c))
    modes_out[0] = modes_ref[0]
    modes_out[pl.ds(1, 4)] = sum(modes_dp[k] for k in range(n_dp))
    mode_prelude(modes_out, pw)
    sc[...] = jnp.zeros(sc.shape, jnp.float32)
    exchange_wait(vec_chan, vec_sems.at[1], nj, (d, c))
    vec_out[...] = sum(vec_chan[k] for k in range(nj))
    gain = jnp.concatenate([vec_out[8 + k:9 + k, :] for k in range(feats // 128)], 1)

    def normalize(m, _):
        at = pl.ds(pl.multiple_of(m * t, t), t)
        centred, scale = layer_stats(tokens_ref[at, :].astype(jnp.float32))
        normed = (centred * scale * gain).T.astype(jnp.bfloat16)
        snd[:, :, at] = normed.reshape(nj, chans, t)
        return 0
    lax.fori_loop(0, mb, normalize, 0)

    def share(box, where, sems, q):
        for p in peers(nj, c):
            send(box.at[p, block_rows(q)], where.at[c, block_rows(q)], sems.at[0, q], sems.at[1, q], (d, p))
        where[c, block_rows(q), :] = box[c, block_rows(q), :]

    def settle(where, sems, q):
        whole = where.at[pl.ds(0, nj - 1), block_rows(q)]
        pltpu.make_async_remote_copy(src_ref=whole, dst_ref=whole, send_sem=sems.at[0, q], recv_sem=sems.at[1, q], device_id=(d, c), device_id_type=MESH).wait()

    for q in range(packs):
        share(snd, u_ref, in_sems, q)
    for q in range(packs):
        settle(u_ref, in_sems, q)
        forward_pack(dims, q, skip_ref, keep_ref, u_ref, out, slope_ref, carry_ref, pw, xs, ys, sc)
        share(out, act_ref, out_sems, q)
        if direct:
            if q == 0:
                spread.first_hop()
            if q == 1:
                spread.second_hop()
            if q == 3:
                spread.last_hop()
    for q in range(packs):
        settle(act_ref, out_sems, q)
    if direct:
        spread.finish()


def entry(tokens, vec, modes, skip, keep, weights, mb, n_dp, nj):
    width, feats = tokens.shape
    chans = feats // nj
    t = width // mb
    h = t // SPAN
    blocks = nj * h
    rows = mb * blocks
    packs = chans // PACK
    groups = modes.shape[1]
    f32, bf16 = jnp.float32, jnp.bfloat16
    direct = nj == 8 and packs == 4 and all(w.shape[0] % 16 == 0 for w in weights)
    owns = list(weights) if direct else []
    shapes = [
        jax.ShapeDtypeStruct((nj, chans, width), bf16),
        jax.ShapeDtypeStruct((nj, chans, width), bf16),
        jax.ShapeDtypeStruct((packs, rows * PACK, 128), f32),
        jax.ShapeDtypeStruct((packs, 4, blocks * PACK, 128), f32),
        jax.ShapeDtypeStruct(vec.shape, f32),
        jax.ShapeDtypeStruct(modes.shape, f32),
    ] + [jax.ShapeDtypeStruct((n_dp, 2, 2, 2) + w.shape, bf16) for w in owns]
    dma = pltpu.SemaphoreType.DMA
    scratch = [
        pltpu.VMEM((nj, chans, width), bf16),
        pltpu.VMEM((nj, chans, width), bf16),
        pltpu.VMEM((n_dp,) + vec.shape, f32),
        pltpu.VMEM((nj,) + vec.shape, f32),
        pltpu.VMEM((n_dp, 4) + modes.shape[1:], f32),
        pltpu.VMEM((18, groups, 128), f32),
        pltpu.VMEM((rows * PACK, 128), f32),
        pltpu.VMEM((rows * PACK, 128), f32),
        pltpu.VMEM((4, blocks * PACK, 128), f32),
        dma((2, 2)), dma((2,)), dma((2, packs)), dma((2, packs)),
    ]
    if direct:
        scratch.append(dma((2, 48)))
    vmem = pl.BlockSpec(memory_space=pltpu.VMEM)
    outs = pl.pallas_call(
        functools.partial(entry_kernel, (nj, chans, mb, h), n_dp, direct),
        out_shape=shapes,
        in_specs=[vmem] * (5 + len(owns)),
        out_specs=[vmem] * len(shapes),
        scratch_shapes=scratch,
        compiler_params=pltpu.CompilerParams(collective_id=0, has_side_effects=True, vmem_limit_bytes=56 << 20),
        name="entry",
    )(tokens, vec, modes, skip, keep, *owns)
    u, act, slope, carry, vec, modes = outs[:6]
    wholes = [w.reshape(-1, w.shape[-1]) for w in outs[6:]]
    if not direct:
        wholes = [lax.all_gather(w, ("dp", "chan"), axis=0, tiled=True) for w in weights]
    return u, act.reshape(feats, width), slope, carry, vec, modes, wholes


def layer_norm(values, gain_vector):
    average = jnp.mean(values, axis=-1, keepdims=True)
    centred = values - average
    spread = jnp.mean(centred * centred, axis=-1, keepdims=True)
    return centred * lax.rsqrt(spread + 1e-05) * gain_vector


def exact_gelu(values):
    return jax.nn.gelu(values, approximate=False)


def gate_mix(project):
    features = project.shape[1] // 2
    return project[:, :features] * jax.nn.sigmoid(project[:, features:])


def on_device(
    tokens, cotangent, lengths, norm_gain, log_step, log_decay, frequency, readout_real, readout_imaginary,
    skip_gain, out_weight, out_bias, ffn_gain, in_weight, in_bias, back_weight,
):
    both = ("dp", "chan")
    mb, rows, feats = tokens.shape
    chans = log_step.shape[0]
    nj = feats // chans
    groups = log_decay.shape[1]
    f32, bf16 = jnp.float32, jnp.bfloat16
    shards = lax.axis_size("dp") * nj

    place = lax.axis_index("dp") * nj + lax.axis_index("chan")
    def placed(x):
        return lax.dynamic_update_slice(jnp.zeros((shards * x.shape[0],), f32), x.astype(f32), (place * x.shape[0],))
    vec = jnp.concatenate([placed(x) for x in (out_bias, norm_gain, ffn_gain, in_bias)]).reshape(-1, 128)
    cuts = (out_bias.shape[0], norm_gain.shape[0], ffn_gain.shape[0], in_bias.shape[0])
    at = [sum(cuts[:k]) for k in range(5)]
    n_dp = lax.axis_size("dp")
    mine = jnp.arange(groups * n_dp) // groups == lax.axis_index("dp")
    modes = [jnp.broadcast_to(log_step[:, None], (chans, groups * n_dp))]
    modes += [jnp.where(mine, jnp.tile(x, (1, n_dp)), 0.0) for x in (log_decay, frequency, readout_real, readout_imaginary)]
    modes = jnp.stack([x.reshape(-1, 128) for x in modes])
    skip = jnp.broadcast_to(skip_gain[:, None], (chans, 128))
    keep = keep_rows(lengths[:, 0], nj * rows // SPAN, mb)
    u, act_t, slope, carry, vec, modes, (w_out, w_in, w_back) = entry(
        tokens.reshape(mb * rows, feats), vec, modes, skip, keep, (out_weight, in_weight, back_weight), mb, n_dp, nj)
    vec = vec.reshape(-1)
    b_out, gain_one, gain_two, b_in = (vec[shards * at[k]:shards * at[k + 1]] for k in range(4))

    rows_all = tokens.reshape(mb * rows, feats).astype(f32)
    normed, norm_pull = jax.vjp(layer_norm, rows_all, gain_one)
    project = tn(act_t, w_out) + b_out
    gated, gate_pull = jax.vjp(gate_mix, project)
    middle = rows_all + gated
    second_float, second_pull = jax.vjp(layer_norm, middle, gain_two)
    second = second_float.astype(bf16)
    before = nn(second, w_in) + b_in
    hidden_float, hidden_pull = jax.vjp(exact_gelu, before)
    hidden = hidden_float.astype(bf16)
    block_out = (middle + nn(hidden, w_back)).astype(bf16)
    upstream = cotangent.reshape(mb * rows, feats)
    grad_back = tn(hidden, upstream)
    grad_before = hidden_pull(nt(upstream, w_back))[0].astype(bf16)
    grad_in = tn(second, grad_before)
    grad_in_bias = jnp.sum(grad_before.astype(f32), axis=0)
    grad_middle, grad_gain_two = second_pull(nt(grad_before, w_in))
    grad_middle = grad_middle + upstream.astype(f32)
    grad_project = gate_pull(grad_middle)[0].astype(bf16)
    grad_out = nn(act_t, grad_project)
    grad_out_bias = jnp.sum(grad_project.astype(f32), axis=0)
    grad_act = nt(w_out, grad_project).astype(bf16).reshape(nj, chans, mb * rows)
    ga = lax.all_to_all(grad_act, "chan", split_axis=0, concat_axis=0, tiled=True)

    gn, zw = ssm_backward(modes, skip, keep, u, ga, slope, carry, mb)
    row_grad = lax.all_to_all(gn, "chan", split_axis=0, concat_axis=0, tiled=True).reshape(feats, mb * rows).T
    grad_rows, grad_gain_one = norm_pull(row_grad.astype(f32))
    grad_tokens = (grad_rows + grad_middle).astype(bf16)

    zw = lax.psum(zw, "dp")
    g_ls, g_ld, g_fr, g_rr, g_ri = (x.reshape(chans, -1) for x in mode_gradients(modes, zw))
    first = lax.axis_index("dp") * groups
    own = [lax.dynamic_slice_in_dim(x, first, groups, 1) for x in (g_ld, g_fr, g_rr, g_ri)]
    g_skip = zw[4].reshape(chans, -1)[:, 0]

    def scatter(x):
        return lax.psum_scatter(x, both, scatter_dimension=0, tiled=True)
    vec = jnp.concatenate([x.reshape(shards, -1) for x in (grad_out_bias, grad_gain_one, grad_gain_two, grad_in_bias)], 1)
    vec = scatter(vec)[0]
    g_bo, g_g1, g_g2, g_bi = (vec[at[k]:at[k + 1]] for k in range(4))
    return (
        block_out.reshape(tokens.shape), grad_tokens.reshape(tokens.shape), g_g1, jnp.sum(g_ls, 1), *own, g_skip,
        scatter(grad_out.astype(bf16)).astype(f32), g_bo, g_g2, scatter(grad_in.astype(bf16)).astype(f32), g_bi, scatter(grad_back.astype(bf16)).astype(f32),
    )


def solution(mesh):
    both = ("dp", "chan")
    rows, row, vec, chan, mode = P(None, both, None), P(both, None), P(both), P("chan"), P("chan", "dp")
    return jax.shard_map(
        on_device, mesh=mesh,
        in_specs=(rows, rows, P(None, "dp"), vec, chan, mode, mode, mode, mode, chan, row, vec, vec, row, vec, row),
        out_specs=(rows, rows, vec, chan, mode, mode, mode, mode, chan, row, vec, vec, row, vec, row),
        check_vma=False,
    )
```

time: 616 us -> 529 us (0.86)
  waiting for transfers between devices: 328 us -> 270 us
  blocking collectives: 113 us -> 56.6 us
  Pallas kernels: 52.3 us -> 91.2 us
  starting transfers between devices: 15.6 us -> 7.73 us
  matrix products: 54.4 us -> 47.2 us
    all_gather x2 -> x0, blocking collectives: 56.2 us -> none  [the longest x1 43 us: on_device(): small = lax.all_gather(small, both, axis=0, tiled=False).astype(f32)]
    all_gather x3 -> x0, waiting for transfers between devices: 47.3 us -> none  [the longest x1 39.2 us: on_device(): w_back = lax.all_gather(back_weight, both, axis=0, tiled=True)]
    pallas_call x1, Pallas kernels: 19.5 us -> 60.6 us  [entry(): pl.pallas_call(functools.partial(entry_kernel, (nj, chans, mb, h), n_dp,...]
    all_to_all x2 -> x0, waiting for transfers between devices: 11.5 us -> none  [the longest x1 11.5 us: on_device(): lax.all_to_all(act, 'chan', split_axis=0, concat_axis=0, tiled=True)]
    all_to_all x1, waiting for transfers between devices: 0.01 us -> 11 us  [on_device(): lax.all_to_all(gn, 'chan', split_axis=0, concat_axis=0, tiled=True)]
    reduce_scatter x3, waiting for transfers between devices: 267 us -> 259 us  [scatter(): return lax.psum_scatter(x, both, scatter_dimension=0, tiled=True)]
    all_to_all x2 -> x0, starting transfers between devices: 7.62 us -> none  [the longest x1 4.07 us: on_device(): lax.all_to_all(act, 'chan', split_axis=0, concat_axis=0, tiled=True)]
  transfers between devices with their start and end apart: 10 -> 5, of which waited for: 7 -> 3; matrix products, arithmetic and copies ran while one was open for 11% -> 7% of each run, Pallas kernels for 9% -> 6%
where the time goes in v2:
time: 529 us; the launch traced here: 528 us
  waiting for transfers between devices  270 us (51%)
  Pallas kernels  91.2 us (17%)
  blocking collectives  56.6 us (11%)
  matrix products  47.2 us (9%)
  other arithmetic  21 us (4%)
  local copies, waits for them, and re-layouts  19.9 us (4%)
  between operations  14.1 us (3%)
  starting transfers between devices  7.73 us (1%)
    reduce_scatter x3, waiting for transfers between devices, scatter(): return lax.psum_scatter(x, both, scatter_dimension=0, tiled=True)  259 us
    pallas_call x1, Pallas kernels, entry(): pl.pallas_call(functools.partial(entry_kernel, (nj, chans, mb, h), n_dp,...  60.6 us
    unnamed x1, blocking collectives  37.7 us
    pallas_call x1, Pallas kernels, ssm_backward(): pl.pallas_call(functools.partial(backward_kernel, (nj, chans, mb, h)), ou...  30.7 us
    dot_general x3, matrix products, nn(): return jnp.dot(a, b, preferred_element_type=jnp.float32, **kw)  24.2 us
    psum x1, blocking collectives, on_device(): zw = lax.psum(zw, 'dp')  18.9 us
    dot_general x3, matrix products, tn(): lax.dot_general(a, b, (((0,), (0,)), ((), ())), preferred_element_type=jn...  13 us
    all_to_all x1, waiting for transfers between devices, on_device(): lax.all_to_all(gn, 'chan', split_axis=0, concat_axis=0, tiled=True)  11 us
  transfers between devices with their start and end apart: 5, of which 3 were waited for; matrix products, arithmetic and copies ran while one was open for 7% of the time, Pallas kernels for 6%

profile of v2, /device:TPU:0, one launch (start us, length us, event | category | flops | bytes accessed | tf_op | source)
XLA Modules:
  0.0 527.9 jit_solution(6512249044707340172)
XLA Ops:
  7.2 0.7 broadcast_compare_fusion
  7.9 0.7 compare_select_fusion
  8.7 0.8 copy.104
  9.5 0.2 tile.17
  9.6 0.7 broadcast_in_dim.72
  10.5 0.8 copy.105
  11.5 0.8 copy.106
  12.4 0.8 copy.107
  13.4 0.8 convert_dynamic-update-slice_fusion.1
  14.2 0.7 convert_dynamic-update-slice_fusion.2
  14.9 0.2 fusion.27
  15.2 0.8 convert_dynamic-update-slice_fusion.3
  16.0 0.7 convert_dynamic-update-slice_fusion
  16.8 0.6 maximum_bitcast_fusion.refs_1_
  17.4 0.8 broadcast_in_dim.81.refs_4_.keep_ref
  18.1 1.3 broadcast_in_dim.79.refs_3_.skip_ref
  19.5 60.6 %entry.1 = (bf16[8,64,768]{2,1,0:T(8,128)(2,1)}, bf16[8,64,768]{2,1,0:T(8,128)(2,1)}, f32[4,768,128]{2,1,0:T(8,128)}, f32[4,4,256,128]{3,2,1,0:T(8,128)}, f32[32...) custom-call(bf16[768,512]{1,0:T(8,128)(2,1)} %bitcast.94, ...), custom_call_target="tpu_custom_call" | custom-call | tf_op jit(solution)/shard_map/entry/pallas_call | solution.py:610
  80.0 0.7 slice_bitcast_fusion.1
  80.7 0.8 slice_bitcast_fusion.2
  81.5 0.7 slice_bitcast_fusion
  82.2 2.5 convolution_add_fusion
  84.7 0.6 fusion.44
  85.3 0.3 multiply_reduce_fusion.2
  85.7 0.8 copy-done.15
  86.4 16.4 %multiply_convert_fusion = (bf16[768,2048]{1,0:T(8,128)(2,1)}, f32[768,2048]{1,0:T(8,128)S(1)}, f32[768,2048]{1,0:T(8,128)S(1)}) fusion(f32[2048]{0:T(1024)S(1)} %slice_bitcast_fusion, bf16[512,2048]{1,0:T(8,128)(2,1)S(1)} %bitcast.101, f32[768,512]{1,0:T(8,128)S(1)} %get-tuple-element.106, f32[512]{0:T(512)S(1)} %get-tuple-element.126, ...), kind=kOutput, calls=%fused_computation.12 | convolution fusion | flops 1715994624 | bytes 19415040 | tf_op jit(solution)/shard_map/dot_general | solution.py:78
  102.8 4.3 convert_reduce_fusion
  107.1 2.2 multiply_reduce_fusion
  109.3 0.6 fusion.42
  110.0 0.7 fusion.21
  110.7 0.4 copy-done.6
  111.1 1.2 copy-done.7
  112.3 0.5 copy-done.9
  112.8 2.0 convolution_convert_fusion.2
  114.9 5.2 convolution_convert_fusion.1
  120.1 1.4 copy-done.8
  121.5 3.6 convolution_convert_fusion.3
  125.1 3.5 all-to-all-start
  128.7 5.3 %convolution_convert_fusion = bf16[2048,512]{1,0:T(8,128)(2,1)} fusion(bf16[768,2048]{1,0:T(8,128)(2,1)} %get-tuple-element.103, bf16[768,512]{1,0:T(8,128)(2,1)} %bitcast.95), kind=kOutput, calls=%fused_computation.28 | convolution fusion | flops 1611661312 | bytes 6029312 | tf_op jit(solution)/shard_map/dot_general | solution.py:74
  134.0 0.2 convert_reduce_fusion.2
  134.2 0.6 copy-done.3
  134.8 0.4 fusion.20
  136.1 1.7 convert_reduce_fusion.1
  138.0 5.7 %add_convert_fusion.2 = bf16[768,512]{1,0:T(8,128)(2,1)} fusion(f32[768,512]{1,0:T(8,128)} %copy-done.5, bf16[768,2048]{1,0:T(8,128)(2,1)} %get-tuple-element.103, bf16[2048,512]{1,0:T(8,128)(2,1)} %bitcast.99), kind=kOutput, calls=%fused_computation.56 | convolution fusion | flops 1611399168 | bytes 7602176 | tf_op jit(solution)/shard_map/dot_general | solution.py:78
  143.8 30.7 %ssm_backward.1 = (bf16[8,64,768]{2,1,0:T(8,128)(2,1)}, f32[5,16,128]{2,1,0:T(8,128)S(1)}) custom-call(f32[5,16,128]{2,1,0:T(8,128)S(1)} %copy-done.3, f32[64,128]{1,0:T(8,128)S(1)} %copy-done.2, f32[16,16,128]{2,1,0:T(8,128)S(1)} %copy-done, bf16[8,64,768]{2,1,0:T(8,128)(2,1)S(1)} %copy-done.1, bf16[8,64,768]{2,1,0:T(8,128)(2,1)S(1)} %all-to-all-done.ga_ref, ...), custom_call_target="tpu_custom_call" | custom-call | tf_op jit(solution)/shard_map/ssm_backward/pallas_call | solution.py:337
  174.5 18.9 %psum.7 = f32[5,16,128]{2,1,0:T(8,128)S(1)} all-reduce(f32[5,16,128]{2,1,0:T(8,128)S(1)} %get-tuple-element.36), channel_id=1, replica_groups=mesh['dp'=4,'chan'=8] {'dp'}, use_global_device_ids=true, to_apply=%region_13.14 | all-reduce | flops 10240 | bytes 81920 | tf_op jit(solution)/shard_map/psum | solution.py:701
  193.6 4.1 all-to-all-start.1
  198.3 0.6 multiply_reduce_fusion.3
  198.9 0.6 fusion.33
  199.5 0.6 slice_reduce_fusion
  200.1 11.0 %all-to-all-done.1 = bf16[8,64,768]{2,1,0:T(8,128)(2,1)S(1)} async-done(((bf16[8,64,768]{2,1,0:T(8,128)(2,1)}), bf16[8,64,768]{2,1,0:T(8,128)(2,1)S(1)}, u32[]{:S(2)}, u32[]{:S(2)}) %all-to-all-start.1) | async-done | bytes 786464 | tf_op jit(solution)/shard_map/all_to_all | solution.py:697
  211.1 1.4 bitcast_convert_fusion
  212.4 1.9 copy.108
  214.3 0.4 fusion.16
  214.8 0.8 fusion.18
  215.7 37.7 %all-reduce.2 = f32[32,128]{1,0:T(8,128)S(1)} all-reduce(f32[32,128]{1,0:T(8,128)S(1)} %pad_maximum_fusion), channel_id=2, replica_groups=mesh['dp'=4,'chan'=8] {'dp','chan'}, use_global_device_ids=true, to_apply=%region_12.13.clone | all-reduce | flops 4096 | bytes 32768
  253.5 0.6 slice_bitcast_fusion.4
  254.0 0.5 slice_bitcast_fusion.6
  254.6 0.6 slice_bitcast_fusion.5
  255.1 2.7 add_convert_fusion.1
  257.9 1.4 convert_element_type.100
  259.3 126.1 %reduce-scatter.6.cloned.1.call-done = bf16[16,2048]{1,0:T(8,128)(2,1)} async-done(((bf16[512,2048]{1,0:T(8,128)(2,1)}), bf16[16,2048]{1,0:T(8,128)(2,1)}) %reduce-scatter.6.cloned.1.call-update) | async-done | bytes 65552 | tf_op jit(solution)/shard_map/reduce_scatter | solution.py:708
  385.3 1.5 convert_element_type.102
  386.8 133.0 %reduce-scatter.8.cloned.1.call-done = bf16[64,512]{1,0:T(8,128)(2,1)} async-done(((bf16[2048,512]{1,0:T(8,128)(2,1)}), bf16[64,512]{1,0:T(8,128)(2,1)}) %reduce-scatter.8.cloned.1.call-update) | async-done | bytes 65552 | tf_op jit(solution)/shard_map/reduce_scatter | solution.py:708
  519.9 1.5 convert_element_type.104
  (101 shorter events, 3.3 us)
Async XLA Ops:
  7.2 250.7 %reduce-scatter.4.cloned.1.call-start = ((), (), s32[]{:S(2)}) async-start(), calls=%async_computation.5 | async-start | bytes 1081344 | tf_op jit(solution)/shard_map/reduce_scatter | solution.py:708
  14.9 4.5 copy-start.13
  82.2 2.6 copy-start.4
  84.7 1.7 copy-start.15
  85.3 29.6 %copy-start.5 = (f32[768,512]{1,0:T(8,128)}, f32[768,512]{1,0:T(8,128)S(1)}, u32[]{:S(2)}) copy-start(f32[768,512]{1,0:T(8,128)S(1)} %get-tuple-element.106) | copy-start | bytes 4718596
  86.4 16.4 %copy-start.11 = (bf16[3,256,512]{2,1,0:T(8,128)(2,1)S(1)}, bf16[3,256,512]{2,1,0:T(8,128)(2,1)}, u32[]{:S(2)}) copy-start(bf16[3,256,512]{2,1,0:T(8,128)(2,1)} %param.17) | copy-start | bytes 2359300
  86.4 16.4 %copy-start.14 = (bf16[4,2,2,2,64,512]{5,4,3,2,1,0:T(8,128)(2,1)S(1)}, bf16[4,2,2,2,64,512]{5,4,3,2,1,0:T(8,128)(2,1)}, u32[]{:S(2)}) copy-start(bf16[4,2,2,2,64,512]{5,4,3,2,1,0:T(8,128)(2,1)} %get-tuple-element.30) | copy-start | bytes 6291460
  107.1 2.2 copy-start.10
  110.0 1.1 copy-start.6
  110.0 2.8 copy-start.16
  111.1 1.2 copy-start.7
  111.1 1.7 copy-start.9
  114.8 270.5 %reduce-scatter.6.cloned.1.call-start = ((), (), s32[]{:S(2)}) async-start(), calls=%async_computation.6 | async-start | bytes 2162688 | tf_op jit(solution)/shard_map/reduce_scatter | solution.py:708
  120.0 1.4 copy-start.8
  125.1 18.7 %all-to-all-start = ((bf16[8,64,768]{2,1,0:T(8,128)(2,1)}), bf16[8,64,768]{2,1,0:T(8,128)(2,1)S(1)}, u32[]{:S(2)}, u32[]{:S(2)}) async-start(bf16[8,64,768]{2,1,0:T(8,128)(2,1)} %bitcast.97), calls=%async_computation | async-start | bytes 1572864 | tf_op jit(solution)/shard_map/all_to_all | solution.py:694
  128.6 391.2 %reduce-scatter.8.cloned.1.call-start = ((), (), s32[]{:S(2)}) async-start(), calls=%async_computation.7 | async-start | bytes 2162688 | tf_op jit(solution)/shard_map/reduce_scatter | solution.py:708
  134.0 0.8 copy-start.3
  138.0 5.7 %copy-start = (f32[16,16,128]{2,1,0:T(8,128)S(1)}, f32[16,16,128]{2,1,0:T(8,128)}, u32[]{:S(2)}) copy-start(f32[16,16,128]{2,1,0:T(8,128)} %broadcast_in_dim.81.refs_4_.keep_ref) | copy-start | bytes 393220
  138.0 5.7 %copy-start.1 = (bf16[8,64,768]{2,1,0:T(8,128)(2,1)S(1)}, bf16[8,64,768]{2,1,0:T(8,128)(2,1)}, u32[]{:S(2)}) copy-start(bf16[8,64,768]{2,1,0:T(8,128)(2,1)} %get-tuple-element.32.u_ref) | copy-start | bytes 2359300
  138.0 5.7 %copy-start.2 = (f32[64,128]{1,0:T(8,128)S(1)}, f32[64,128]{1,0:T(8,128)}, u32[]{:S(2)}) copy-start(f32[64,128]{1,0:T(8,128)} %broadcast_in_dim.79.refs_3_.skip_ref) | copy-start | bytes 98308
  193.6 17.5 %all-to-all-start.1 = ((bf16[8,64,768]{2,1,0:T(8,128)(2,1)}), bf16[8,64,768]{2,1,0:T(8,128)(2,1)S(1)}, u32[]{:S(2)}, u32[]{:S(2)}) async-start(bf16[8,64,768]{2,1,0:T(8,128)(2,1)} %get-tuple-element.35), calls=%async_computation.1 | async-start | bytes 1572864 | tf_op jit(solution)/shard_map/all_to_all | solution.py:697
  214.3 40.8 %copy-start.12 = (bf16[3,256,512]{2,1,0:T(8,128)(2,1)S(1)}, bf16[3,256,512]{2,1,0:T(8,128)(2,1)}, u32[]{:S(2)}) copy-start(bf16[3,256,512]{2,1,0:T(8,128)(2,1)} %param.17) | copy-start | bytes 2359300
Sparse Core Ops, SparseCore 0:
  114.9 135.4 reduce-scatter.3
  252.8 132.4 reduce-scatter.5
  387.6 132.2 reduce-scatter.7

commit v3 on v2

--- a/solution.py
+++ b/solution.py
@@ -318,40 +318,6 @@
     lax.fori_loop(0, nj, finish, 0)
 
 
-def backward_kernel(dims, modes_ref, skip_ref, keep_ref, u_ref, ga_ref, slope_ref, carry_ref, gn_ref, zw_ref, pw_ref, xs, gy, gx, sc):
-    mode_prelude(modes_ref, pw_ref)
-    sc[...] = jnp.zeros(sc.shape, jnp.float32)
-
-    def one(q, _):
-        backward_pack(dims, q, skip_ref, keep_ref, u_ref, ga_ref, slope_ref, carry_ref, gn_ref, zw_ref, pw_ref, xs, gy, gx, sc)
-        return 0
-    lax.fori_loop(0, dims[1] // PACK, one, 0)
-
-
-def ssm_backward(modes, skip, keep, u, ga, slope, carry, mb):
-    nj, chans, width = u.shape
-    h = width // mb // 128
-    blocks = nj * h
-    rows = mb * blocks
-    f32 = jnp.float32
-    return pl.pallas_call(
-        functools.partial(backward_kernel, (nj, chans, mb, h)),
-        out_shape=(
-            jax.ShapeDtypeStruct(u.shape, jnp.bfloat16),
-            jax.ShapeDtypeStruct((5, modes.shape[1], 128), f32),
-        ),
-        scratch_shapes=[
-            pltpu.VMEM((18, modes.shape[1], 128), f32),
-            pltpu.VMEM((rows * PACK, 128), f32),
-            pltpu.VMEM((rows * PACK, 128), f32),
-            pltpu.VMEM((rows * PACK, 128), f32),
-            pltpu.VMEM((4, blocks * PACK, 128), f32),
-        ],
-        compiler_params=pltpu.CompilerParams(vmem_limit_bytes=50 << 20),
-        name="ssm_backward",
-    )(modes, skip, keep, u, ga, slope, carry)
-
-
 def mode_gradients(modes, zw):
     m = mode_rows(*modes)
     z_r, z_i, v_r, v_i = zw[0], zw[1], zw[2], zw[3]
@@ -377,20 +343,24 @@
     return jnp.broadcast_to(rows[:, :, None], (blocks, PACK, 128))
 
 
-def mode_stack(log_step, ld, fr, rr, ri):
-    nh = ld.shape[1]
-    ls = jnp.broadcast_to(log_step[:, None], ld.shape)
-    return jnp.stack([x.reshape(-1, 128) for x in (ls, ld, fr, rr, ri)])
-
-
 MESH = pl.DeviceIdType.MESH
+F32, BF16 = jnp.float32, jnp.bfloat16
 
 
 def layer_stats(v):
     average = jnp.mean(v, axis=-1, keepdims=True)
     centred = v - average
     spread = jnp.mean(centred * centred, axis=-1, keepdims=True)
-    return centred, lax.rsqrt(spread + 1e-05)
+    scale = lax.rsqrt(spread + 1e-05)
+    return centred * scale, scale
+
+
+def layer_back(q, n, scale):
+    return scale * (q - jnp.mean(q, axis=-1, keepdims=True) - n * jnp.mean(q * n, axis=-1, keepdims=True))
+
+
+def column_sum(x):
+    return jnp.sum(x, axis=0, keepdims=True)
 
 
 def peers(count, me):
@@ -412,134 +382,324 @@
     return copy
 
 
-def exchange_start(box, sems, axis_count, me, to):
-    for p in peers(axis_count, me):
+def exchange_start(box, sems, count, me, to):
+    for p in peers(count, me):
         send(box.at[me], box.at[me], sems.at[0], sems.at[1], to(p))
 
 
-def exchange_wait(box, sems, axis_count, to):
-    if axis_count > 1:
-        whole = box.at[pl.ds(0, axis_count - 1)]
-        pltpu.make_async_remote_copy(src_ref=whole, dst_ref=whole, send_sem=sems.at[0], recv_sem=sems.at[1], device_id=to, device_id_type=MESH).wait()
-
-
-class Spread:
-    def __init__(self, wholes, sems, d, c):
-        self.wholes, self.sems = wholes, sems
+def exchange_wait(box, sems, count, here):
+    whole = box.at[pl.ds(0, count - 1)]
+    pltpu.make_async_remote_copy(src_ref=whole, dst_ref=whole, send_sem=sems.at[0], recv_sem=sems.at[1], device_id=here, device_id_type=MESH).wait()
+
+
+class Copies:
+    def __init__(self, sems):
+        self.sems = sems
+        self.used = 0
+        self.unsent = []
+
+    def put(self, src, dst, to):
+        n = self.used
+        self.used += 1
+        copy = send(src, dst, self.sems.at[0, n], self.sems.at[1, n], to)
+        self.unsent.append(copy)
+        return copy
+
+    def finish(self):
+        for copy in self.unsent:
+            copy.wait_send()
+
+
+def arrive(copies):
+    for copy in copies:
+        copy.wait_recv()
+
+
+class Place:
+    def __init__(self, d, c):
         self.d, self.c = d, c
         self.a, self.b, self.core = c // 4, lax.rem(c // 2, 2), lax.rem(c, 2)
-        self.used = 0
-        self.open = []
-
-    def chan(self, a, b, core):
+
+    def at(self, a, b, core):
         return (self.d, a * 4 + b * 2 + core)
 
-    def put(self, ref, to):
-        n = self.used
-        self.used += 1
-        return send(ref, ref, self.sems.at[0, n], self.sems.at[1, n], to)
-
-    def halves(self, w):
-        cols = w.shape[-1] // 2
-        return pl.ds(0, cols), pl.ds(cols, cols)
+    @property
+    def over_a(self):
+        return self.at(1 - self.a, self.b, self.core)
+
+    @property
+    def over_b(self):
+        return self.at(self.a, 1 - self.b, self.core)
+
+    @property
+    def twin(self):
+        return self.at(self.a, self.b, 1 - self.core)
+
+
+def halves(w):
+    cols = w.shape[-1] // 2
+    return pl.ds(0, cols), pl.ds(cols, cols)
+
+
+class Gather:
+    def __init__(self, wholes, copies, here):
+        self.wholes, self.copies, self.here = wholes, copies, here
+        self.side = []
 
     def along_dp(self, owns, n_dp):
-        a, b, core, d = self.a, self.b, self.core, self.d
+        i = self.here
+        for own, w in zip(owns, self.wholes):
+            w[i.d, i.a, i.b, i.core] = own[...]
         self.step = []
-        for own, w in zip(owns, self.wholes):
-            w[d, a, b, core] = own[...]
         for w in self.wholes:
-            for p in peers(n_dp, d):
-                self.step.append(self.put(w.at[d, a, b, core], (p, self.c)))
-
-    def arrived(self):
-        for copy in self.step:
-            copy.wait_recv()
-        self.open += self.step
+            ref = w.at[i.d, i.a, i.b, i.core]
+            self.step += [self.copies.put(ref, ref, (p, i.c)) for p in peers(n_dp, i.d)]
+
+    def same(self, ref, to):
+        return self.copies.put(ref, ref, to)
+
+    def first_hop(self):
+        i = self.here
+        arrive(self.step)
         self.step = []
-
-    def first_hop(self):
-        a, b, core = self.a, self.b, self.core
-        self.arrived()
         for w in self.wholes:
-            low, high = self.halves(w)
-            self.step.append(self.put(w.at[:, a, b, core, :, low], self.chan(a, 1 - b, core)))
-            self.step.append(self.put(w.at[:, a, b, core, :, high], self.chan(1 - a, b, core)))
-        self.side = [self.put(w.at[:, a, b, core], self.chan(a, b, 1 - core)) for w in self.wholes]
+            low, high = halves(w)
+            self.step.append(self.same(w.at[:, i.a, i.b, i.core, :, low], i.over_b))
+            self.step.append(self.same(w.at[:, i.a, i.b, i.core, :, high], i.over_a))
+        self.side += [self.same(w.at[:, i.a, i.b, i.core], i.twin) for w in self.wholes]
 
     def second_hop(self):
-        a, b, core = self.a, self.b, self.core
-        self.arrived()
+        i = self.here
+        arrive(self.step)
+        self.step = []
         for w in self.wholes:
-            low, high = self.halves(w)
-            self.step.append(self.put(w.at[:, a, :, core, :, low], self.chan(1 - a, b, core)))
-            self.step.append(self.put(w.at[:, :, b, core, :, high], self.chan(a, 1 - b, core)))
-        other = self.chan(a, b, 1 - core)
+            low, high = halves(w)
+            self.step.append(self.same(w.at[:, i.a, :, i.core, :, low], i.over_a))
+            self.step.append(self.same(w.at[:, :, i.b, i.core, :, high], i.over_b))
         for w in self.wholes:
-            low, high = self.halves(w)
-            self.side.append(self.put(w.at[:, a, 1 - b, core, :, low], other))
-            self.side.append(self.put(w.at[:, 1 - a, b, core, :, high], other))
+            low, high = halves(w)
+            self.side.append(self.same(w.at[:, i.a, 1 - i.b, i.core, :, low], i.twin))
+            self.side.append(self.same(w.at[:, 1 - i.a, i.b, i.core, :, high], i.twin))
 
     def last_hop(self):
-        a, b, core = self.a, self.b, self.core
-        self.arrived()
-        other = self.chan(a, b, 1 - core)
+        i = self.here
+        arrive(self.step)
         for w in self.wholes:
-            low, high = self.halves(w)
-            self.side.append(self.put(w.at[:, 1 - a, :, core, :, low], other))
-            self.side.append(self.put(w.at[:, :, 1 - b, core, :, high], other))
+            low, high = halves(w)
+            self.side.append(self.same(w.at[:, 1 - i.a, :, i.core, :, low], i.twin))
+            self.side.append(self.same(w.at[:, :, 1 - i.b, i.core, :, high], i.twin))
 
     def finish(self):
-        for copy in self.side:
-            copy.wait_recv()
-        for copy in self.open + self.side:
-            copy.wait_send()
-
-
-def entry_kernel(dims, n_dp, direct, *refs):
-    (nj, chans, mb, h) = dims
+        arrive(self.side)
+
+
+class Scatter:
+    def __init__(self, grads, boxes, copies, here):
+        self.grads, self.copies, self.here = grads, copies, here
+        self.twins, self.lows, self.highs, self.low2s, self.high2s, self.lasts = boxes
+        self.first = []
+        self.step = []
+
+    def to_twin(self, k):
+        i = self.here
+        self.first.append(self.copies.put(self.grads[k].at[:, :, :, 1 - i.core], self.twins[k], i.twin))
+
+    def add_twin(self):
+        i = self.here
+        arrive(self.first)
+        for g, t in zip(self.grads, self.twins):
+            def add(n, _):
+                for a in range(2):
+                    for b in range(2):
+                        t[n, a, b] = (t[n, a, b].astype(F32) + g[n, a, b, i.core].astype(F32)).astype(BF16)
+                return 0
+            lax.fori_loop(0, t.shape[0], add, 0)
+        for t, low_box, high_box in zip(self.twins, self.lows, self.highs):
+            low, high = halves(t)
+            self.step.append(self.copies.put(t.at[:, 1 - i.a, :, :, low], low_box, i.over_a))
+            self.step.append(self.copies.put(t.at[:, :, 1 - i.b, :, high], high_box, i.over_b))
+
+    def add_first(self):
+        i = self.here
+        arrive(self.step)
+        self.step = []
+        for t, low_box, high_box in zip(self.twins, self.lows, self.highs):
+            low, high = halves(t)
+            def add(n, _):
+                for k in range(2):
+                    low_box[n, k] = (low_box[n, k].astype(F32) + t[n, i.a, k, :, low].astype(F32)).astype(BF16)
+                    high_box[n, k] = (high_box[n, k].astype(F32) + t[n, k, i.b, :, high].astype(F32)).astype(BF16)
+                return 0
+            lax.fori_loop(0, t.shape[0], add, 0)
+        for low_box, high_box, low2, high2 in zip(self.lows, self.highs, self.low2s, self.high2s):
+            self.step.append(self.copies.put(low_box.at[:, 1 - i.b], low2, i.over_b))
+            self.step.append(self.copies.put(high_box.at[:, 1 - i.a], high2, i.over_a))
+
+    def add_second(self, n_dp):
+        i = self.here
+        arrive(self.step)
+        self.step = []
+        for low_box, high_box, low2, high2, last in zip(self.lows, self.highs, self.low2s, self.high2s, self.lasts):
+            low, high = halves(last)
+            for n in range(n_dp):
+                low2[n] = (low2[n].astype(F32) + low_box[n, i.b].astype(F32)).astype(BF16)
+                high2[n] = (high2[n].astype(F32) + high_box[n, i.a].astype(F32)).astype(BF16)
+            for p in peers(n_dp, i.d):
+                self.step.append(self.copies.put(low2.at[p], last.at[i.d, :, low], (p, i.c)))
+                self.step.append(self.copies.put(high2.at[p], last.at[i.d, :, high], (p, i.c)))
+
+    def finish(self, outs, n_dp):
+        i = self.here
+        arrive(self.step)
+        for low2, high2, last, out in zip(self.low2s, self.high2s, self.lasts, outs):
+            low, high = halves(last)
+            for cut, box in ((low, low2), (high, high2)):
+                total = box[i.d].astype(F32)
+                for p in peers(n_dp, i.d):
+                    total = total + last[p, :, cut].astype(F32)
+                out[:, cut] = total
+
+
+def wide(vec_ref, first, count):
+    return jnp.concatenate([vec_ref[first + k:first + k + 1, :] for k in range(count)], 1)
+
+
+def add_wide(vec_ref, first, row):
+    for k in range(row.shape[1] // 128):
+        vec_ref[first + k:first + k + 1, :] += row[:, k * 128:(k + 1) * 128]
+
+
+def flat(x):
+    return x.reshape(-1, x.shape[-1])
+
+
+def dense_rows(m, t, tokens, cot, act, wholes, vec, block_out, second, hidden, gb, gp, gm, snd, sums, nj, chans):
+    w_out, w_in, w_back = wholes
+    at = pl.ds(pl.multiple_of(m * t, t), t)
+    feats = nj * chans
+    ff = w_in.shape[-1]
+    tile = ff // 4
+    x = tokens[at, :].astype(F32)
+    project = tn(act[:, :, at].reshape(feats, t), flat(w_out[...])) + wide(vec, 0, 2 * feats // 128)
+    gate = jax.nn.sigmoid(project[:, feats:])
+    gated = project[:, :feats] * gate
+    middle = x + gated
+    n, scale = layer_stats(middle)
+    gain = wide(vec, 12, feats // 128)
+    after = (n * gain).astype(BF16)
+    second[at, :] = after
+    up = cot[at, :]
+    total = middle
+    back = jnp.zeros((t, feats), F32)
+    for f in range(4):
+        cols = slice(f * tile, (f + 1) * tile)
+        w = flat(w_in[:, :, :, :, :, cols])
+        before = nn(after, w) + wide(vec, 16 + f * tile // 128, tile // 128)
+        high, slope = gelu_pair(before)
+        high = high.astype(BF16)
+        hidden[at, cols] = high
+        wb = flat(w_back[f])
+        low = (slope * nt(up, wb)).astype(BF16)
+        gb[at, cols] = low
+        add_wide(sums, 16 + f * tile // 128, column_sum(low.astype(F32)))
+        total = total + nn(high, wb)
+        back = back + nt(low, w)
+    block_out[at, :] = total.astype(BF16)
+    add_wide(sums, 12, column_sum(back * n))
+    grad = up.astype(F32) + layer_back(back * gain, n, scale)
+    gm[at, :] = grad
+    first = (grad * gate).astype(BF16)
+    last = (grad * gated * (1.0 - gate)).astype(BF16)
+    gp[at, :feats] = first
+    gp[at, feats:] = last
+    add_wide(sums, 0, column_sum(first.astype(F32)))
+    add_wide(sums, feats // 128, column_sum(last.astype(F32)))
+    both = jnp.concatenate([first, last], 1)
+    snd[:, :, at] = nt(flat(w_out[...]), both).astype(BF16).reshape(nj, chans, t)
+
+
+def weight_grads(act, gp, second, gb, hidden, cot, grads, nj, scatter):
+    g_out, g_in, g_back = grads
+    def shaped(x, g):
+        return x.astype(BF16).reshape(g.shape[1:])
+    def back(n, _):
+        size = hidden.shape[1] // 4
+        g_back[n] = shaped(tn(hidden[:, pl.ds(pl.multiple_of(n * size, size), size)], cot[...]), g_back)
+        return 0
+    lax.fori_loop(0, 4, back, 0)
+    if scatter:
+        scatter.to_twin(2)
+    def inner(n, _):
+        size = second.shape[1] // 4
+        g_in[n] = shaped(tn(second[:, pl.ds(pl.multiple_of(n * size, size), size)], gb[...]), g_in)
+        return 0
+    lax.fori_loop(0, 4, inner, 0)
+    if scatter:
+        scatter.to_twin(1)
+    def outer(n, _):
+        g_out[n] = shaped(nn(flat(act[pl.ds(n * (nj // 4), nj // 4)]), gp[...]), g_out)
+        return 0
+    lax.fori_loop(0, 4, outer, 0)
+    if scatter:
+        scatter.to_twin(0)
+
+
+def whole_kernel(dims, n_dp, direct, *refs):
+    nj, chans, mb, h = dims
     refs = list(refs)
-    tokens_ref, vec_ref, modes_ref, skip_ref, keep_ref = refs[:5]
-    del refs[:5]
-    owns = [refs.pop(0) for _ in range(3)] if direct else []
-    u_ref, act_ref, slope_ref, carry_ref, vec_out, modes_out = refs[:6]
-    del refs[:6]
-    wholes = [refs.pop(0) for _ in range(3)] if direct else []
-    snd, out, vec_dp, vec_chan, modes_dp, pw, xs, ys, sc = refs[:9]
-    del refs[:9]
-    vec_sems, modes_sems, in_sems, out_sems = refs[:4]
-    del refs[:4]
+    def take(n):
+        out = refs[:n]
+        del refs[:n]
+        return out
+    tokens, cot, vec_own, modes_own, skip, keep = take(6)
+    given = take(3)
+    block_out, grad_tokens, mode_out, vec_out = take(4)
+    results = take(3)
+    u, snd, act, out, ga, gn, slope, carry = take(8)
+    second, hidden, gb, gp, gm = take(5)
+    vec_dp, vec_chan, modes_dp, zw_dp, modes, vec, sums = take(7)
+    pw, xs, ys, gy, sc = take(5)
+    box_sems, in_sems, out_sems, back_sems, gn_sems = take(5)
     d, c = lax.axis_index("dp"), lax.axis_index("chan")
+    here = (d, c)
     packs = chans // PACK
-    width = tokens_ref.shape[0]
-    t = width // mb
+    t = tokens.shape[0] // mb
     feats = nj * chans
+    over_dp, over_chan = (lambda p: (p, c)), (lambda p: (d, p))
+    if direct:
+        wholes, grads = take(3), take(3)
+        boxes = [take(3) for _ in range(6)]
+        place = Place(d, c)
+        gather_copies, scatter_copies = Copies(refs[0]), Copies(refs[1])
+        gather = Gather(wholes, gather_copies, place)
+        scatter = Scatter(grads, boxes, scatter_copies, place)
+    else:
+        wholes, grads, scatter = given, results, None
 
     greet(n_dp, nj, d, c)
-    vec_dp[d] = vec_ref[...]
-    modes_dp[d] = modes_ref[pl.ds(1, 4)]
-    exchange_start(vec_dp, vec_sems.at[0], n_dp, d, lambda p: (p, c))
-    exchange_start(modes_dp, modes_sems, n_dp, d, lambda p: (p, c))
+    vec_dp[d] = vec_own[...]
+    modes_dp[d] = modes_own[pl.ds(1, 4)]
+    exchange_start(vec_dp, box_sems.at[0], n_dp, d, over_dp)
+    exchange_start(modes_dp, box_sems.at[1], n_dp, d, over_dp)
     if direct:
-        spread = Spread(wholes, refs[0], d, c)
-        spread.along_dp(owns, n_dp)
-    exchange_wait(vec_dp, vec_sems.at[0], n_dp, (d, c))
+        gather.along_dp(given, n_dp)
+    sums[...] = jnp.zeros(sums.shape, F32)
+    sc[...] = jnp.zeros(sc.shape, F32)
+    exchange_wait(vec_dp, box_sems.at[0], n_dp, here)
     vec_chan[c] = sum(vec_dp[k] for k in range(n_dp))
-    exchange_start(vec_chan, vec_sems.at[1], nj, c, lambda p: (d, p))
-    exchange_wait(modes_dp, modes_sems, n_dp, (d, c))
-    modes_out[0] = modes_ref[0]
-    modes_out[pl.ds(1, 4)] = sum(modes_dp[k] for k in range(n_dp))
-    mode_prelude(modes_out, pw)
-    sc[...] = jnp.zeros(sc.shape, jnp.float32)
-    exchange_wait(vec_chan, vec_sems.at[1], nj, (d, c))
-    vec_out[...] = sum(vec_chan[k] for k in range(nj))
-    gain = jnp.concatenate([vec_out[8 + k:9 + k, :] for k in range(feats // 128)], 1)
+    exchange_start(vec_chan, box_sems.at[2], nj, c, over_chan)
+    exchange_wait(modes_dp, box_sems.at[1], n_dp, here)
+    modes[0] = modes_own[0]
+    modes[pl.ds(1, 4)] = sum(modes_dp[k] for k in range(n_dp))
+    mode_prelude(modes, pw)
+    exchange_wait(vec_chan, box_sems.at[2], nj, here)
+    vec[...] = sum(vec_chan[k] for k in range(nj))
+    gain = wide(vec, 8, feats // 128)
 
     def normalize(m, _):
         at = pl.ds(pl.multiple_of(m * t, t), t)
-        centred, scale = layer_stats(tokens_ref[at, :].astype(jnp.float32))
-        normed = (centred * scale * gain).T.astype(jnp.bfloat16)
-        snd[:, :, at] = normed.reshape(nj, chans, t)
+        n, _scale = layer_stats(tokens[at, :].astype(F32))
+        snd[:, :, at] = (n * gain).T.astype(BF16).reshape(nj, chans, t)
         return 0
     lax.fori_loop(0, mb, normalize, 0)
 
@@ -550,28 +710,80 @@
 
     def settle(where, sems, q):
         whole = where.at[pl.ds(0, nj - 1), block_rows(q)]
-        pltpu.make_async_remote_copy(src_ref=whole, dst_ref=whole, send_sem=sems.at[0, q], recv_sem=sems.at[1, q], device_id=(d, c), device_id_type=MESH).wait()
+        pltpu.make_async_remote_copy(src_ref=whole, dst_ref=whole, send_sem=sems.at[0, q], recv_sem=sems.at[1, q], device_id=here, device_id_type=MESH).wait()
 
     for q in range(packs):
-        share(snd, u_ref, in_sems, q)
+        share(snd, u, in_sems, q)
     for q in range(packs):
-        settle(u_ref, in_sems, q)
-        forward_pack(dims, q, skip_ref, keep_ref, u_ref, out, slope_ref, carry_ref, pw, xs, ys, sc)
-        share(out, act_ref, out_sems, q)
+        settle(u, in_sems, q)
+        forward_pack(dims, q, skip, keep, u, out, slope, carry, pw, xs, ys, sc)
+        share(out, act, out_sems, q)
         if direct:
             if q == 0:
-                spread.first_hop()
+                gather.first_hop()
             if q == 1:
-                spread.second_hop()
+                gather.second_hop()
             if q == 3:
-                spread.last_hop()
+                gather.last_hop()
     for q in range(packs):
-        settle(act_ref, out_sems, q)
+        settle(act, out_sems, q)
     if direct:
-        spread.finish()
-
-
-def entry(tokens, vec, modes, skip, keep, weights, mb, n_dp, nj):
+        gather.finish()
+
+    for m in range(mb):
+        dense_rows(m, t, tokens, cot, act, wholes, vec, block_out, second, hidden, gb, gp, gm, snd, sums, nj, chans)
+        at = pl.ds(m * t, t)
+        for p in peers(nj, c):
+            send(snd.at[p, :, at], ga.at[c, :, at], back_sems.at[0, m], back_sems.at[1, m], (d, p))
+        ga[c, :, at] = snd[c, :, at]
+    weight_grads(act, gp, second, gb, hidden, cot, grads, nj, scatter)
+    for m in range(mb):
+        whole = ga.at[pl.ds(0, nj - 1), :, pl.ds(m * t, t)]
+        pltpu.make_async_remote_copy(src_ref=whole, dst_ref=whole, send_sem=back_sems.at[0, m], recv_sem=back_sems.at[1, m], device_id=here, device_id_type=MESH).wait()
+
+    for q in range(packs):
+        backward_pack(dims, q, skip, keep, u, ga, slope, carry, out, zw_dp.at[d], pw, xs, gy, ys, sc)
+        share(out, gn, gn_sems, q)
+        if direct:
+            if q == 0:
+                scatter.add_twin()
+            if q == 2:
+                scatter.add_first()
+            if q == 3:
+                scatter.add_second(n_dp)
+    exchange_start(zw_dp, box_sems.at[3], n_dp, d, over_dp)
+    for q in range(packs):
+        settle(gn, gn_sems, q)
+
+    def finish_rows(m, _):
+        at = pl.ds(pl.multiple_of(m * t, t), t)
+        n, scale = layer_stats(tokens[at, :].astype(F32))
+        grad = gn[:, :, at].reshape(feats, t).astype(F32).T
+        add_wide(sums, 8, column_sum(grad * n))
+        grad_tokens[at, :] = (gm[at, :] + layer_back(grad * gain, n, scale)).astype(BF16)
+        return 0
+    lax.fori_loop(0, mb, finish_rows, 0)
+
+    vec_chan[c] = sums[...]
+    exchange_start(vec_chan, box_sems.at[4], nj, c, over_chan)
+    exchange_wait(zw_dp, box_sems.at[3], n_dp, here)
+    zw = [sum(zw_dp[k, a] for k in range(n_dp)) for a in range(5)]
+    for k, x in enumerate(mode_gradients([modes[a] for a in range(5)], zw)):
+        mode_out[k] = x
+    mode_out[5] = zw[4]
+    exchange_wait(vec_chan, box_sems.at[4], nj, here)
+    vec_dp[d] = sum(vec_chan[k] for k in range(nj))
+    exchange_start(vec_dp, box_sems.at[5], n_dp, d, over_dp)
+    if direct:
+        scatter.finish(results, n_dp)
+    exchange_wait(vec_dp, box_sems.at[5], n_dp, here)
+    vec_out[...] = sum(vec_dp[k] for k in range(n_dp))
+    if direct:
+        gather_copies.finish()
+        scatter_copies.finish()
+
+
+def whole(tokens, cot, vec, modes, skip, keep, weights, mb, n_dp, nj):
     width, feats = tokens.shape
     chans = feats // nj
     t = width // mb
@@ -580,138 +792,88 @@
     rows = mb * blocks
     packs = chans // PACK
     groups = modes.shape[1]
-    f32, bf16 = jnp.float32, jnp.bfloat16
-    direct = nj == 8 and packs == 4 and all(w.shape[0] % 16 == 0 for w in weights)
-    owns = list(weights) if direct else []
+    direct = nj == 8 and n_dp == 4 and packs == 4 and all(w.shape[0] % 16 == 0 for w in weights)
+    if not direct:
+        weights = [lax.all_gather(w, ("dp", "chan"), axis=0, tiled=True) for w in weights]
+        weights = [w.reshape(4, 2, 2, 2, -1, w.shape[1]) for w in weights]
+    per = [w.shape[-2:] for w in weights]
+    full = [(4, 2, 2, 2) + p for p in per]
+    ff = per[1][1]
+    shape = jax.ShapeDtypeStruct
     shapes = [
-        jax.ShapeDtypeStruct((nj, chans, width), bf16),
-        jax.ShapeDtypeStruct((nj, chans, width), bf16),
-        jax.ShapeDtypeStruct((packs, rows * PACK, 128), f32),
-        jax.ShapeDtypeStruct((packs, 4, blocks * PACK, 128), f32),
-        jax.ShapeDtypeStruct(vec.shape, f32),
-        jax.ShapeDtypeStruct(modes.shape, f32),
-    ] + [jax.ShapeDtypeStruct((n_dp, 2, 2, 2) + w.shape, bf16) for w in owns]
-    dma = pltpu.SemaphoreType.DMA
-    scratch = [
-        pltpu.VMEM((nj, chans, width), bf16),
-        pltpu.VMEM((nj, chans, width), bf16),
-        pltpu.VMEM((n_dp,) + vec.shape, f32),
-        pltpu.VMEM((nj,) + vec.shape, f32),
-        pltpu.VMEM((n_dp, 4) + modes.shape[1:], f32),
-        pltpu.VMEM((18, groups, 128), f32),
-        pltpu.VMEM((rows * PACK, 128), f32),
-        pltpu.VMEM((rows * PACK, 128), f32),
-        pltpu.VMEM((4, blocks * PACK, 128), f32),
-        dma((2, 2)), dma((2,)), dma((2, packs)), dma((2, packs)),
+        shape((width, feats), BF16), shape((width, feats), BF16), shape((6,) + modes.shape[1:], F32), shape(vec.shape, F32),
+    ] + ([shape(p, F32) for p in per] if direct else [shape(f, BF16) for f in full])
+    dma, vm = pltpu.SemaphoreType.DMA, pltpu.VMEM
+    scratch = [vm((nj, chans, width), BF16)] * 6 + [
+        vm((packs, rows * PACK, 128), F32),
+        vm((packs, 4, blocks * PACK, 128), F32),
+        vm((width, feats), BF16), vm((width, ff), BF16), vm((width, ff), BF16), vm((width, 2 * feats), BF16), vm((width, feats), F32),
+        vm((n_dp,) + vec.shape, F32), vm((nj,) + vec.shape, F32), vm((n_dp, 4) + modes.shape[1:], F32),
+        vm((n_dp, 5) + modes.shape[1:], F32), vm(modes.shape, F32), vm(vec.shape, F32), vm(vec.shape, F32),
+        vm((18, groups, 128), F32),
+        vm((rows * PACK, 128), F32), vm((rows * PACK, 128), F32), vm((rows * PACK, 128), F32),
+        vm((4, blocks * PACK, 128), F32),
+        dma((6, 2)), dma((2, packs)), dma((2, packs)), dma((2, mb)), dma((2, packs)),
     ]
     if direct:
-        scratch.append(dma((2, 48)))
+        scratch += [vm(f, BF16) for f in full] * 2
+        half = [(r, k // 2) for r, k in per]
+        scratch += [vm((4, 2, 2) + p, BF16) for p in per]
+        scratch += [vm((4, 2) + p, BF16) for p in half] * 2
+        scratch += [vm((4,) + p, BF16) for p in half] * 2
+        scratch += [vm((4,) + p, BF16) for p in per]
+        scratch += [dma((2, 36)), dma((2, 33))]
     vmem = pl.BlockSpec(memory_space=pltpu.VMEM)
     outs = pl.pallas_call(
-        functools.partial(entry_kernel, (nj, chans, mb, h), n_dp, direct),
+        functools.partial(whole_kernel, (nj, chans, mb, h), n_dp, direct),
         out_shape=shapes,
-        in_specs=[vmem] * (5 + len(owns)),
-        out_specs=[vmem] * len(shapes),
+        in_specs=[vmem] * 9,
+        out_specs=[vmem] * 7,
         scratch_shapes=scratch,
-        compiler_params=pltpu.CompilerParams(collective_id=0, has_side_effects=True, vmem_limit_bytes=56 << 20),
-        name="entry",
-    )(tokens, vec, modes, skip, keep, *owns)
-    u, act, slope, carry, vec, modes = outs[:6]
-    wholes = [w.reshape(-1, w.shape[-1]) for w in outs[6:]]
+        compiler_params=pltpu.CompilerParams(collective_id=0, has_side_effects=True, vmem_limit_bytes=60 << 20),
+        name="whole",
+    )(tokens, cot, vec, modes, skip, keep, *weights)
+    grads = outs[4:]
     if not direct:
-        wholes = [lax.all_gather(w, ("dp", "chan"), axis=0, tiled=True) for w in weights]
-    return u, act.reshape(feats, width), slope, carry, vec, modes, wholes
-
-
-def layer_norm(values, gain_vector):
-    average = jnp.mean(values, axis=-1, keepdims=True)
-    centred = values - average
-    spread = jnp.mean(centred * centred, axis=-1, keepdims=True)
-    return centred * lax.rsqrt(spread + 1e-05) * gain_vector
-
-
-def exact_gelu(values):
-    return jax.nn.gelu(values, approximate=False)
-
-
-def gate_mix(project):
-    features = project.shape[1] // 2
-    return project[:, :features] * jax.nn.sigmoid(project[:, features:])
+        grads = [lax.psum_scatter(g.reshape(-1, g.shape[-1]).astype(F32), ("dp", "chan"), scatter_dimension=0, tiled=True) for g in grads]
+    return outs[:4], grads
 
 
 def on_device(
     tokens, cotangent, lengths, norm_gain, log_step, log_decay, frequency, readout_real, readout_imaginary,
     skip_gain, out_weight, out_bias, ffn_gain, in_weight, in_bias, back_weight,
 ):
-    both = ("dp", "chan")
     mb, rows, feats = tokens.shape
-    chans = log_step.shape[0]
-    nj = feats // chans
-    groups = log_decay.shape[1]
-    f32, bf16 = jnp.float32, jnp.bfloat16
-    shards = lax.axis_size("dp") * nj
-
+    chans, groups = log_decay.shape
+    nj, n_dp = lax.axis_size("chan"), lax.axis_size("dp")
+    shards = n_dp * nj
     place = lax.axis_index("dp") * nj + lax.axis_index("chan")
+    vectors = (out_bias, norm_gain, ffn_gain, in_bias)
+
     def placed(x):
-        return lax.dynamic_update_slice(jnp.zeros((shards * x.shape[0],), f32), x.astype(f32), (place * x.shape[0],))
-    vec = jnp.concatenate([placed(x) for x in (out_bias, norm_gain, ffn_gain, in_bias)]).reshape(-1, 128)
-    cuts = (out_bias.shape[0], norm_gain.shape[0], ffn_gain.shape[0], in_bias.shape[0])
-    at = [sum(cuts[:k]) for k in range(5)]
-    n_dp = lax.axis_size("dp")
+        return lax.dynamic_update_slice(jnp.zeros((shards * x.shape[0],), F32), x.astype(F32), (place * x.shape[0],))
+    vec = jnp.concatenate([placed(x) for x in vectors]).reshape(-1, 128)
     mine = jnp.arange(groups * n_dp) // groups == lax.axis_index("dp")
     modes = [jnp.broadcast_to(log_step[:, None], (chans, groups * n_dp))]
     modes += [jnp.where(mine, jnp.tile(x, (1, n_dp)), 0.0) for x in (log_decay, frequency, readout_real, readout_imaginary)]
     modes = jnp.stack([x.reshape(-1, 128) for x in modes])
     skip = jnp.broadcast_to(skip_gain[:, None], (chans, 128))
     keep = keep_rows(lengths[:, 0], nj * rows // SPAN, mb)
-    u, act_t, slope, carry, vec, modes, (w_out, w_in, w_back) = entry(
-        tokens.reshape(mb * rows, feats), vec, modes, skip, keep, (out_weight, in_weight, back_weight), mb, n_dp, nj)
-    vec = vec.reshape(-1)
-    b_out, gain_one, gain_two, b_in = (vec[shards * at[k]:shards * at[k + 1]] for k in range(4))
-
-    rows_all = tokens.reshape(mb * rows, feats).astype(f32)
-    normed, norm_pull = jax.vjp(layer_norm, rows_all, gain_one)
-    project = tn(act_t, w_out) + b_out
-    gated, gate_pull = jax.vjp(gate_mix, project)
-    middle = rows_all + gated
-    second_float, second_pull = jax.vjp(layer_norm, middle, gain_two)
-    second = second_float.astype(bf16)
-    before = nn(second, w_in) + b_in
-    hidden_float, hidden_pull = jax.vjp(exact_gelu, before)
-    hidden = hidden_float.astype(bf16)
-    block_out = (middle + nn(hidden, w_back)).astype(bf16)
-    upstream = cotangent.reshape(mb * rows, feats)
-    grad_back = tn(hidden, upstream)
-    grad_before = hidden_pull(nt(upstream, w_back))[0].astype(bf16)
-    grad_in = tn(second, grad_before)
-    grad_in_bias = jnp.sum(grad_before.astype(f32), axis=0)
-    grad_middle, grad_gain_two = second_pull(nt(grad_before, w_in))
-    grad_middle = grad_middle + upstream.astype(f32)
-    grad_project = gate_pull(grad_middle)[0].astype(bf16)
-    grad_out = nn(act_t, grad_project)
-    grad_out_bias = jnp.sum(grad_project.astype(f32), axis=0)
-    grad_act = nt(w_out, grad_project).astype(bf16).reshape(nj, chans, mb * rows)
-    ga = lax.all_to_all(grad_act, "chan", split_axis=0, concat_axis=0, tiled=True)
-
-    gn, zw = ssm_backward(modes, skip, keep, u, ga, slope, carry, mb)
-    row_grad = lax.all_to_all(gn, "chan", split_axis=0, concat_axis=0, tiled=True).reshape(feats, mb * rows).T
-    grad_rows, grad_gain_one = norm_pull(row_grad.astype(f32))
-    grad_tokens = (grad_rows + grad_middle).astype(bf16)
-
-    zw = lax.psum(zw, "dp")
-    g_ls, g_ld, g_fr, g_rr, g_ri = (x.reshape(chans, -1) for x in mode_gradients(modes, zw))
+    (block_out, grad_tokens, mode_grads, vec), (g_out, g_in, g_back) = whole(
+        tokens.reshape(mb * rows, feats), cotangent.reshape(mb * rows, feats), vec, modes, skip, keep,
+        (out_weight, in_weight, back_weight), mb, n_dp, nj)
+    g_ls, g_ld, g_fr, g_rr, g_ri, g_skip = (x.reshape(chans, -1) for x in mode_grads)
     first = lax.axis_index("dp") * groups
     own = [lax.dynamic_slice_in_dim(x, first, groups, 1) for x in (g_ld, g_fr, g_rr, g_ri)]
-    g_skip = zw[4].reshape(chans, -1)[:, 0]
-
-    def scatter(x):
-        return lax.psum_scatter(x, both, scatter_dimension=0, tiled=True)
-    vec = jnp.concatenate([x.reshape(shards, -1) for x in (grad_out_bias, grad_gain_one, grad_gain_two, grad_in_bias)], 1)
-    vec = scatter(vec)[0]
-    g_bo, g_g1, g_g2, g_bi = (vec[at[k]:at[k + 1]] for k in range(4))
+    vec = vec.reshape(-1)
+    cuts, start = [], 0
+    for x in vectors:
+        cuts.append(lax.dynamic_slice_in_dim(vec, start + place * x.shape[0], x.shape[0], 0))
+        start += shards * x.shape[0]
+    g_bo, g_g1, g_g2, g_bi = cuts
     return (
-        block_out.reshape(tokens.shape), grad_tokens.reshape(tokens.shape), g_g1, jnp.sum(g_ls, 1), *own, g_skip,
-        scatter(grad_out.astype(bf16)).astype(f32), g_bo, g_g2, scatter(grad_in.astype(bf16)).astype(f32), g_bi, scatter(grad_back.astype(bf16)).astype(f32),
+        block_out.reshape(tokens.shape), grad_tokens.reshape(tokens.shape), g_g1, jnp.sum(g_ls, 1), *own, g_skip[:, 0],
+        g_out, g_bo, g_g2, g_in, g_bi, g_back,
     )
 
 

time: 529 us -> 166 us (0.31)
  waiting for transfers between devices: 270 us -> 0 us
  blocking collectives: 56.6 us -> 0 us
  Pallas kernels: 91.2 us -> 140 us
  matrix products: 47.2 us -> 0 us
  other arithmetic: 21 us -> 1.82 us
  between operations: 14.1 us -> 0.82 us
  starting transfers between devices: 7.73 us -> 0 us
    reduce_scatter x3 -> x0, waiting for transfers between devices: 259 us -> none  [scatter(): return lax.psum_scatter(x, both, scatter_dimension=0, tiled=True)]
    pallas_call x2 -> x1, Pallas kernels: 91.2 us -> 140 us  [whole(): pl.pallas_call(functools.partial(whole_kernel, (nj, chans, mb, h), n_dp,...]
    dot_general x9 -> x0, matrix products: 47.2 us -> none  [the longest x3 24.2 us: nn(): return jnp.dot(a, b, preferred_element_type=jnp.float32, **kw)]
    unnamed x1 -> x0, blocking collectives: 37.7 us -> none
    psum x1 -> x0, blocking collectives: 18.9 us -> none  [on_device(): zw = lax.psum(zw, 'dp')]
    all_to_all x2 -> x0, waiting for transfers between devices: 11 us -> none  [the longest x1 11 us: on_device(): lax.all_to_all(gn, 'chan', split_axis=0, concat_axis=0, tiled=True)]
    convert_element_type x5 -> x0, other arithmetic: 8.48 us -> none  [the longest x1 2.73 us: on_device(): grad_tokens = (grad_rows + grad_middle).astype(bf16)]
    all_to_all x2 -> x0, starting transfers between devices: 7.61 us -> none  [the longest x1 4.07 us: on_device(): lax.all_to_all(gn, 'chan', split_axis=0, concat_axis=0, tiled=True)]
  transfers between devices with their start and end apart: 5 -> 0, of which waited for: 3 -> 0; matrix products, arithmetic and copies ran while one was open for 7% -> 0% of each run, Pallas kernels for 6% -> 0%
where the time goes in v3:
time: 166 us; the launch traced here: 165 us
  Pallas kernels  140 us (84%)
  local copies, waits for them, and re-layouts  22.7 us (14%)
  other arithmetic  1.82 us (1%)
    pallas_call x1, Pallas kernels, whole(): pl.pallas_call(functools.partial(whole_kernel, (nj, chans, mb, h), n_dp,...  140 us
    unnamed x48, local copies, waits for them, and re-layouts  14.2 us
    dynamic_slice x3, local copies, waits for them, and re-layouts, on_device(): lax.dynamic_slice_in_dim(vec, start + place * x.shape[0], x.shape[0], 0)  3.86 us

profile of v3, /device:TPU:0, one launch (start us, length us, event | category | flops | bytes accessed | tf_op | source)
XLA Modules:
  0.0 165.3 jit_solution(9363519647403358071)
XLA Ops:
  0.7 0.0 copy-start.12
  0.7 0.6 copy-done.12
  1.3 0.1 convert_dynamic-update-slice_fusion.1
  1.4 0.7 copy-done.13
  2.1 0.1 convert_dynamic-update-slice_fusion.2
  2.1 0.7 copy-done.14
  2.8 0.1 convert_dynamic-update-slice_fusion.3
  2.9 0.7 copy-done.15
  3.5 0.1 convert_dynamic-update-slice_fusion
  3.6 0.6 maximum_bitcast_fusion.refs_2_
  4.3 0.1 broadcast_in_dim.56
  4.3 0.6 copy-done.6
  4.9 0.1 copy.48
  5.0 0.0 copy-start.11
  5.0 0.2 tile.17
  5.2 0.5 copy-done.11
  5.7 0.1 broadcast_in_dim.52
  5.8 0.1 broadcast_in_dim.53
  5.9 0.1 broadcast_in_dim.54
  6.0 0.7 copy-done.7
  6.6 0.1 copy.49
  6.8 0.2 tile.19
  6.9 0.7 copy-done.8
  7.6 0.1 copy.50
  7.7 0.2 tile.41
  7.9 0.7 copy-done.9
  8.6 0.1 copy.51
  8.7 0.2 tile.43
  8.8 0.6 copy-done.16
  9.5 0.2 fusion.1
  9.7 0.1 concatenate.7
  9.8 0.8 broadcast_in_dim.61.refs_5_
  10.6 0.0 copy-done.5
  10.6 0.0 copy-done.10
  10.6 0.7 broadcast_in_dim.59.refs_4_
  11.3 139.9 %whole.1 = (bf16[768,512]{1,0:T(8,128)(2,1)}, bf16[768,512]{1,0:T(8,128)(2,1)}, f32[6,16,128]{2,1,0:T(8,128)}, f32[32,128]{1,0:T(8,128)}, f32[16,1024]{1,0:T(8,1...) custom-call(bf16[768,512]{1,0:T(8,128)(2,1)} %bitcast.13, bf16[768,512]{1,0:T(8,128)(2,1)} %bitcast.14, ...), custom_call_target="tpu_custom_call" | custom-call | tf_op jit(solution)/shard_map/whole/pallas_call | solution.py:827
  151.2 0.0 copy-start.1
  151.2 0.9 fusion.5
  152.0 0.1 reshape_unstack.21
  152.1 0.1 reshape_unstack.22
  152.2 0.1 constant_dynamic-slice_fusion
  152.3 0.7 copy.54
  152.9 0.7 copy.55
  153.6 0.1 reshape_unstack.19
  153.7 0.1 reshape_unstack.20
  153.7 0.1 constant_dynamic-slice_fusion.2
  153.8 0.7 copy.52
  154.5 0.7 copy.53
  155.2 0.1 reshape_unstack.18
  155.2 0.6 reduce_sum.9
  155.9 0.1 reshape_unstack.23
  155.9 0.6 slice_reduce_fusion
  156.6 1.3 fusion.6
  157.9 1.3 dynamic_slice.31
  159.2 1.3 dynamic_slice.29
  160.4 0.0 copy-done.1
  160.4 0.9 copy.70
  161.3 0.5 copy-done
  161.9 0.9 copy.71
  162.7 0.6 copy.72
  163.4 0.3 copy-done.3
  163.7 0.7 copy.73
  164.3 0.3 copy-done.2
  164.6 0.7 copy.74
  (34 shorter events, 0.2 us)
Async XLA Ops:
  0.7 0.7 copy-start.12
  1.4 0.7 copy-start.13
  2.1 0.7 copy-start.14
  2.9 0.7 copy-start.15
  4.2 0.7 copy-start.6
  5.0 0.7 copy-start.11
  6.0 0.7 copy-start.7
  6.9 0.7 copy-start.8
  7.9 0.7 copy-start.9
  8.8 0.7 copy-start.16
  9.5 1.1 copy-start.5
  9.8 0.8 copy-start.10
  151.2 9.3 %copy-start.1 = (bf16[768,512]{1,0:T(8,128)(2,1)S(1)}, bf16[768,512]{1,0:T(8,128)(2,1)}, u32[]{:S(2)}) copy-start(bf16[768,512]{1,0:T(8,128)(2,1)} %get-tuple-element.22) | copy-start | bytes 2359300
  160.4 1.4 copy-start
  161.9 0.9 copy-start.4
  162.7 0.9 copy-start.3
  163.7 1.0 copy-start.2

commit v4 on v3

--- a/solution.py
+++ b/solution.py
@@ -9,6 +9,10 @@
 SPAN = 128
 PACK = 16
 HI = lax.Precision.HIGHEST
+
+
+def keep_row(span, i):
+    return jnp.where((span & (i * SPAN)) == 0, 0.0, 1.0)
 
 
 def cmul(ar, ai, br, bi):
@@ -136,12 +140,12 @@
     return pl.ds(pl.multiple_of(r * PACK, PACK), PACK)
 
 
-def unpack(src_ref, q, xs, nj, mb, h, blocks, scale=None):
+def unpack(src_ref, q, xs, nj, mb, h, blocks, gain):
     def body(j, _):
         for m in range(mb):
             for k in range(h):
                 x = src_ref[j, block_rows(q), pl.ds((m * h + k) * 128, 128)]
-                xs[block_rows(m * blocks + j * h + k), :] = x.astype(jnp.float32)
+                xs[block_rows(m * blocks + j * h + k), :] = x.astype(jnp.float32) * gain
         return 0
     lax.fori_loop(0, nj, body, 0)
 
@@ -152,11 +156,11 @@
     return jnp.concatenate(parts, 0)
 
 
-def forward_pack(dims, q, skip_ref, keep_ref, u_ref, act_ref, slope_ref, carry_ref, pw_ref, xs, ys, sc):
+def forward_pack(dims, q, skip_ref, gain_ref, span, u_ref, act_ref, slope_ref, carry_ref, pw_ref, xs, ys, sc):
     nj, chans, mb, h = dims
     blocks = nj * h
     rows = mb * blocks
-    unpack(u_ref, q, xs, nj, mb, h, blocks)
+    unpack(u_ref, q, xs, nj, mb, h, blocks, gain_ref[block_rows(q), :])
 
     def states(g, _):
         rws = group_rows(pw_ref, q * 4 + g)
@@ -174,7 +178,7 @@
 
     def step(i, c):
         at = block_rows(i)
-        keep = keep_ref[i]
+        keep = keep_row(span, i)
         c = [x * keep for x in c]
         s = [sc[a, at, :] for a in range(4)]
         for a in range(4):
@@ -216,11 +220,11 @@
     lax.fori_loop(0, nj, finish, 0)
 
 
-def backward_pack(dims, q, skip_ref, keep_ref, u_ref, ga_ref, slope_ref, carry_ref, gn_ref, zw_ref, pw_ref, xs, gy, gx, sc):
+def backward_pack(dims, q, skip_ref, gain_ref, span, u_ref, ga_ref, slope_ref, carry_ref, gn_ref, zw_ref, ng_ref, pw_ref, xs, gy, gx, sc):
     nj, chans, mb, h = dims
     blocks = nj * h
     rows = mb * blocks
-    unpack(u_ref, q, xs, nj, mb, h, blocks)
+    unpack(u_ref, q, xs, nj, mb, h, blocks, gain_ref[block_rows(q), :])
     def start(j, _):
         for m in range(mb):
             for k in range(h):
@@ -277,7 +281,7 @@
         e2 = cmul(q_[0], q_[1], f[2], f[3])
         sc[0, at, :] = a_r
         sc[1, at, :] = a_i
-        keep = keep_ref[i]
+        keep = keep_row(span, i)
         n_r, n_i = cmul(a_r, a_i, h_r, h_i)
         return ((n_r + q_[0]) * keep, (n_i + q_[1]) * keep, z_r + d[0], z_i + d[1], w_r + e1[0] + e2[0], w_i + e1[1] + e2[1])
     zero = jnp.zeros((PACK, 128), jnp.float32)
@@ -308,14 +312,16 @@
     lax.fori_loop(0, 4, outputs, 0, unroll=2)
 
     skip = skip_ref[block_rows(q), :]
-    def finish(j, _):
+    def finish(j, total):
         for m in range(mb):
             for k in range(h):
                 r = m * blocks + j * h + k
-                v = gx[block_rows(r), :] + skip * gy[block_rows(r), :]
-                gn_ref[j, block_rows(q), pl.ds((m * h + k) * 128, 128)] = v.astype(jnp.bfloat16)
-        return 0
-    lax.fori_loop(0, nj, finish, 0)
+                v = (gx[block_rows(r), :] + skip * gy[block_rows(r), :]).astype(jnp.bfloat16)
+                cols = pl.ds((m * h + k) * 128, 128)
+                gn_ref[j, block_rows(q), cols] = v
+                total = total + v.astype(jnp.float32) * u_ref[j, block_rows(q), cols].astype(jnp.float32)
+        return total
+    ng_ref[block_rows(q), :] = lax.fori_loop(0, nj, finish, jnp.zeros((PACK, 128), jnp.float32))
 
 
 def mode_gradients(modes, zw):
@@ -382,14 +388,23 @@
     return copy
 
 
-def exchange_start(box, sems, count, me, to):
-    for p in peers(count, me):
-        send(box.at[me], box.at[me], sems.at[0], sems.at[1], to(p))
-
-
-def exchange_wait(box, sems, count, here):
-    whole = box.at[pl.ds(0, count - 1)]
-    pltpu.make_async_remote_copy(src_ref=whole, dst_ref=whole, send_sem=sems.at[0], recv_sem=sems.at[1], device_id=here, device_id_type=MESH).wait()
+def settle(whole, send_sem, recv_sem, here):
+    pltpu.make_async_remote_copy(src_ref=whole, dst_ref=whole, send_sem=send_sem, recv_sem=recv_sem, device_id=here, device_id_type=MESH).wait()
+
+
+class Exchange:
+    def __init__(self, box, sems, count, me, to, here):
+        self.box, self.sems, self.count, self.me, self.to, self.here = box, sems, count, me, to, here
+
+    def start(self):
+        for p in peers(self.count, self.me):
+            send(self.box.at[self.me], self.box.at[self.me], self.sems.at[0], self.sems.at[1], self.to(p))
+
+    def wait(self):
+        settle(self.box.at[pl.ds(0, self.count - 1)], self.sems.at[0], self.sems.at[1], self.here)
+
+    def total(self):
+        return sum(self.box[k] for k in range(self.count))
 
 
 class Copies:
@@ -442,21 +457,20 @@
 
 
 class Gather:
-    def __init__(self, wholes, copies, here):
-        self.wholes, self.copies, self.here = wholes, copies, here
+    def __init__(self, owns, wholes, copies, here):
+        self.owns, self.wholes, self.copies, self.here = owns, wholes, copies, here
         self.side = []
-
-    def along_dp(self, owns, n_dp):
-        i = self.here
-        for own, w in zip(owns, self.wholes):
-            w[i.d, i.a, i.b, i.core] = own[...]
-        self.step = []
-        for w in self.wholes:
-            ref = w.at[i.d, i.a, i.b, i.core]
-            self.step += [self.copies.put(ref, ref, (p, i.c)) for p in peers(n_dp, i.d)]
 
     def same(self, ref, to):
         return self.copies.put(ref, ref, to)
+
+    def along_dp(self, n_dp):
+        i = self.here
+        self.step = []
+        for own, w in zip(self.owns, self.wholes):
+            w[i.d, i.a, i.b, i.core] = own[...]
+            ref = w.at[i.d, i.a, i.b, i.core]
+            self.step += [self.same(ref, (p, i.c)) for p in peers(n_dp, i.d)]
 
     def first_hop(self):
         i = self.here
@@ -569,79 +583,131 @@
         vec_ref[first + k:first + k + 1, :] += row[:, k * 128:(k + 1) * 128]
 
 
+def put_own(vec_ref, first, own, shard, shards):
+    size = own.shape[1]
+    rows = size * shards // 128
+    while own.shape[1] < 128:
+        own = jnp.concatenate([own, own], 1)
+    index = 128 * lax.broadcasted_iota(jnp.int32, (rows, 128), 0) + lax.broadcasted_iota(jnp.int32, (rows, 128), 1)
+    inside = (index >= shard * size) & (index < (shard + 1) * size)
+    vec_ref[first:first + rows, :] = jnp.where(inside, jnp.broadcast_to(own, (rows, 128)), 0.0)
+
+
+def pick_own(vec_ref, first, size, shard):
+    start = shard * size
+    row = vec_ref[pl.ds(first + start // 128, 1), :]
+    row = pltpu.roll(jnp.broadcast_to(row, (8, 128)), lax.rem(128 - lax.rem(start, 128), 128), 1)
+    return row[0:1, :size]
+
+
+def to_column(row):
+    return jnp.broadcast_to(row, (128, row.shape[1])).T
+
+
+def padded(x, lanes=128):
+    if x.shape[1] == lanes:
+        return x
+    return jnp.concatenate([x, jnp.zeros((x.shape[0], lanes - x.shape[1]), x.dtype)], 1)
+
+
+def lane_pick(groups, k):
+    lane = lax.broadcasted_iota(jnp.int32, (groups, 128), 1)
+    return (lane == 4 * lax.broadcasted_iota(jnp.int32, (groups, 128), 0) + k).astype(F32)
+
+
+def spread_modes(rows, modes):
+    groups = modes.shape[1]
+    for k in range(4):
+        part = nt(lane_pick(groups, k), rows, precision=HI)
+        for a in range(modes.shape[0]):
+            modes[a, :, k * 32:(k + 1) * 32] = part[:, a * 32:(a + 1) * 32]
+
+
+def collect_modes(arrays):
+    groups = arrays[0].shape[0]
+    total = None
+    for k in range(4):
+        part = jnp.concatenate([x[:, k * 32:(k + 1) * 32] for x in arrays], 1)
+        part = tn(part, lane_pick(groups, k), precision=HI)
+        total = part if total is None else total + part
+    return total
+
+
 def flat(x):
     return x.reshape(-1, x.shape[-1])
 
 
-def dense_rows(m, t, tokens, cot, act, wholes, vec, block_out, second, hidden, gb, gp, gm, snd, sums, nj, chans):
-    w_out, w_in, w_back = wholes
-    at = pl.ds(pl.multiple_of(m * t, t), t)
-    feats = nj * chans
-    ff = w_in.shape[-1]
-    tile = ff // 4
-    x = tokens[at, :].astype(F32)
+def row_block(m, t):
+    return pl.ds(pl.multiple_of(m * t, t), t)
+
+
+def dense_up(m, t, tokens, act, w_out, w_in, vec, keeps):
+    middle, gate_ref, gated_ref, second, hidden, slopes = keeps
+    at = row_block(m, t)
+    feats = tokens.shape[1]
+    tile = w_in.shape[-1] // 4
     project = tn(act[:, :, at].reshape(feats, t), flat(w_out[...])) + wide(vec, 0, 2 * feats // 128)
     gate = jax.nn.sigmoid(project[:, feats:])
     gated = project[:, :feats] * gate
-    middle = x + gated
-    n, scale = layer_stats(middle)
+    total = tokens[at, :].astype(F32) + gated
+    gate_ref[at, :] = gate
+    gated_ref[at, :] = gated
+    middle[at, :] = total
+    n, _scale = layer_stats(total)
+    after = (n * wide(vec, 12, feats // 128)).astype(BF16)
+    second[at, :] = after
+    for f in range(4):
+        cols = slice(f * tile, (f + 1) * tile)
+        before = nn(after, flat(w_in[:, :, :, :, :, cols])) + wide(vec, 16 + f * tile // 128, tile // 128)
+        high, slope = gelu_pair(before)
+        hidden[at, cols] = high.astype(BF16)
+        slopes[at, cols] = slope
+
+
+def dense_down(m, t, cot, wholes, vec, block_out, keeps, gb, gp, snd, sums):
+    w_out, w_in, w_back = wholes
+    middle, gate_ref, gated_ref, second, hidden, slopes = keeps
+    at = row_block(m, t)
+    feats = cot.shape[1]
+    tile = w_in.shape[-1] // 4
+    up = cot[at, :]
+    total = middle[at, :]
+    n, scale = layer_stats(total)
     gain = wide(vec, 12, feats // 128)
-    after = (n * gain).astype(BF16)
-    second[at, :] = after
-    up = cot[at, :]
-    total = middle
     back = jnp.zeros((t, feats), F32)
     for f in range(4):
         cols = slice(f * tile, (f + 1) * tile)
-        w = flat(w_in[:, :, :, :, :, cols])
-        before = nn(after, w) + wide(vec, 16 + f * tile // 128, tile // 128)
-        high, slope = gelu_pair(before)
-        high = high.astype(BF16)
-        hidden[at, cols] = high
         wb = flat(w_back[f])
-        low = (slope * nt(up, wb)).astype(BF16)
+        low = (slopes[at, cols] * nt(up, wb)).astype(BF16)
         gb[at, cols] = low
         add_wide(sums, 16 + f * tile // 128, column_sum(low.astype(F32)))
-        total = total + nn(high, wb)
-        back = back + nt(low, w)
+        total = total + nn(hidden[at, cols], wb)
+        back = back + nt(low, flat(w_in[:, :, :, :, :, cols]))
     block_out[at, :] = total.astype(BF16)
     add_wide(sums, 12, column_sum(back * n))
     grad = up.astype(F32) + layer_back(back * gain, n, scale)
-    gm[at, :] = grad
+    middle[at, :] = grad
+    gate = gate_ref[at, :]
     first = (grad * gate).astype(BF16)
-    last = (grad * gated * (1.0 - gate)).astype(BF16)
+    last = (grad * gated_ref[at, :] * (1.0 - gate)).astype(BF16)
     gp[at, :feats] = first
     gp[at, feats:] = last
     add_wide(sums, 0, column_sum(first.astype(F32)))
     add_wide(sums, feats // 128, column_sum(last.astype(F32)))
     both = jnp.concatenate([first, last], 1)
-    snd[:, :, at] = nt(flat(w_out[...]), both).astype(BF16).reshape(nj, chans, t)
-
-
-def weight_grads(act, gp, second, gb, hidden, cot, grads, nj, scatter):
-    g_out, g_in, g_back = grads
-    def shaped(x, g):
-        return x.astype(BF16).reshape(g.shape[1:])
-    def back(n, _):
-        size = hidden.shape[1] // 4
-        g_back[n] = shaped(tn(hidden[:, pl.ds(pl.multiple_of(n * size, size), size)], cot[...]), g_back)
-        return 0
-    lax.fori_loop(0, 4, back, 0)
-    if scatter:
-        scatter.to_twin(2)
-    def inner(n, _):
-        size = second.shape[1] // 4
-        g_in[n] = shaped(tn(second[:, pl.ds(pl.multiple_of(n * size, size), size)], gb[...]), g_in)
-        return 0
-    lax.fori_loop(0, 4, inner, 0)
-    if scatter:
-        scatter.to_twin(1)
-    def outer(n, _):
-        g_out[n] = shaped(nn(flat(act[pl.ds(n * (nj // 4), nj // 4)]), gp[...]), g_out)
-        return 0
-    lax.fori_loop(0, 4, outer, 0)
-    if scatter:
-        scatter.to_twin(0)
+    snd[:, :, at] = nt(flat(w_out[...]), both).astype(BF16).reshape(snd.shape[:2] + (t,))
+
+
+def shaped(x, g):
+    return x.astype(BF16).reshape(g.shape[1:])
+
+
+def outer_products(left, right, g):
+    size = left.shape[1] // 4
+    def one(n, _):
+        g[n] = shaped(tn(left[:, row_block(n, size)], right[...]), g)
+        return 0
+    lax.fori_loop(0, 4, one, 0)
 
 
 def whole_kernel(dims, n_dp, direct, *refs):
@@ -651,55 +717,69 @@
         out = refs[:n]
         del refs[:n]
         return out
-    tokens, cot, vec_own, modes_own, skip, keep = take(6)
+    tokens, cot, lengths, log_step, skip_row, *mode_parts = take(9)
+    vectors = take(4)
     given = take(3)
-    block_out, grad_tokens, mode_out, vec_out = take(4)
+    block_out, grad_tokens = take(2)
+    g_step, g_skip, *g_modes = take(6)
+    g_vectors = take(4)
     results = take(3)
     u, snd, act, out, ga, gn, slope, carry = take(8)
-    second, hidden, gb, gp, gm = take(5)
-    vec_dp, vec_chan, modes_dp, zw_dp, modes, vec, sums = take(7)
+    second, hidden, gb, gp = take(4)
+    keeps = take(4)
+    middle = keeps[0]
+    keeps = keeps[:3] + [second, hidden] + keeps[3:]
+    vec_dp, vec_chan, vec2_dp, vec2_chan, modes_dp, zw_dp, ng_dp, ng_chan = take(8)
+    modes, vec, sums, skip, gain, mode_rows_box = take(6)
     pw, xs, ys, gy, sc = take(5)
     box_sems, in_sems, out_sems, back_sems, gn_sems = take(5)
     d, c = lax.axis_index("dp"), lax.axis_index("chan")
     here = (d, c)
+    shards, shard = n_dp * nj, d * nj + c
     packs = chans // PACK
-    t = tokens.shape[0] // mb
+    groups = modes.shape[1]
+    width = tokens.shape[0]
+    t = width // mb
     feats = nj * chans
     over_dp, over_chan = (lambda p: (p, c)), (lambda p: (d, p))
+
+    def along_dp(box, n):
+        return Exchange(box, box_sems.at[n], n_dp, d, over_dp, here)
+
+    def along_chan(box, n):
+        return Exchange(box, box_sems.at[n], nj, c, over_chan, here)
+    vec_first, vec_second = along_dp(vec_dp, 0), along_chan(vec_chan, 1)
+    modes_all = along_dp(modes_dp, 2)
+    sums_first, sums_second = along_chan(vec2_chan, 3), along_dp(vec2_dp, 4)
+    zw_all, ng_first, ng_second = along_dp(zw_dp, 5), along_dp(ng_dp, 6), along_chan(ng_chan, 7)
     if direct:
         wholes, grads = take(3), take(3)
         boxes = [take(3) for _ in range(6)]
         place = Place(d, c)
         gather_copies, scatter_copies = Copies(refs[0]), Copies(refs[1])
-        gather = Gather(wholes, gather_copies, place)
-        scatter = Scatter(grads, boxes, scatter_copies, place)
+        early = Gather(given[:2], wholes[:2], gather_copies, place)
+        late = Gather(given[2:], wholes[2:], gather_copies, place)
+        rest = Scatter(grads[:2], [b[:2] for b in boxes], scatter_copies, place)
+        ahead = Scatter(grads[2:], [b[2:] for b in boxes], scatter_copies, place)
     else:
-        wholes, grads, scatter = given, results, None
-
+        wholes, grads = given, results
+    g_out, g_in, g_back = grads
+
+    for k, (own, first) in enumerate(zip(vectors, (0, 8, 12, 16))):
+        put_own(vec_dp.at[d], first, own[...].astype(F32), shard, shards)
+    for a in range(4):
+        modes_dp[d, a] = padded(mode_parts[a][...])
     greet(n_dp, nj, d, c)
-    vec_dp[d] = vec_own[...]
-    modes_dp[d] = modes_own[pl.ds(1, 4)]
-    exchange_start(vec_dp, box_sems.at[0], n_dp, d, over_dp)
-    exchange_start(modes_dp, box_sems.at[1], n_dp, d, over_dp)
-    if direct:
-        gather.along_dp(given, n_dp)
-    sums[...] = jnp.zeros(sums.shape, F32)
-    sc[...] = jnp.zeros(sc.shape, F32)
-    exchange_wait(vec_dp, box_sems.at[0], n_dp, here)
-    vec_chan[c] = sum(vec_dp[k] for k in range(n_dp))
-    exchange_start(vec_chan, box_sems.at[2], nj, c, over_chan)
-    exchange_wait(modes_dp, box_sems.at[1], n_dp, here)
-    modes[0] = modes_own[0]
-    modes[pl.ds(1, 4)] = sum(modes_dp[k] for k in range(n_dp))
-    mode_prelude(modes, pw)
-    exchange_wait(vec_chan, box_sems.at[2], nj, here)
-    vec[...] = sum(vec_chan[k] for k in range(nj))
-    gain = wide(vec, 8, feats // 128)
+    vec_first.start()
+    modes_all.start()
+    if direct:
+        early.along_dp(n_dp)
+        late.along_dp(n_dp)
 
     def normalize(m, _):
-        at = pl.ds(pl.multiple_of(m * t, t), t)
+        at = row_block(m, t)
         n, _scale = layer_stats(tokens[at, :].astype(F32))
-        snd[:, :, at] = (n * gain).T.astype(BF16).reshape(nj, chans, t)
+        snd[:, :, at] = n.T.astype(BF16).reshape(nj, chans, t)
         return 0
     lax.fori_loop(0, mb, normalize, 0)
 
@@ -708,82 +788,149 @@
             send(box.at[p, block_rows(q)], where.at[c, block_rows(q)], sems.at[0, q], sems.at[1, q], (d, p))
         where[c, block_rows(q), :] = box[c, block_rows(q), :]
 
-    def settle(where, sems, q):
-        whole = where.at[pl.ds(0, nj - 1), block_rows(q)]
-        pltpu.make_async_remote_copy(src_ref=whole, dst_ref=whole, send_sem=sems.at[0, q], recv_sem=sems.at[1, q], device_id=here, device_id_type=MESH).wait()
+    def shared(where, sems, q):
+        settle(where.at[pl.ds(0, nj - 1), block_rows(q)], sems.at[0, q], sems.at[1, q], here)
 
     for q in range(packs):
         share(snd, u, in_sems, q)
+    sums[...] = jnp.zeros(sums.shape, F32)
+    sc[...] = jnp.zeros(sc.shape, F32)
+    skip[...] = to_column(skip_row[...])
+    long = lengths[...] - 1
+    row = lax.broadcasted_iota(jnp.int32, (PACK, 128), 0)
+    span = jnp.zeros((PACK, 128), jnp.int32)
+    for m in range(mb):
+        span = jnp.where(lax.rem(row, mb) == m, jnp.broadcast_to(long[:, m:m + 1], (PACK, 128)), span)
+    vec_first.wait()
+    vec_chan[c] = vec_first.total()
+    vec_second.start()
+    modes_all.wait()
+    kinds = [jnp.broadcast_to(padded(log_step[...]), (32, 128))]
+    kinds += [jnp.concatenate([modes_dp[p, a] for p in range(n_dp)], 0) for a in range(4)]
+    spread_modes(jnp.concatenate(kinds, 0), modes)
+    mode_prelude(modes, pw)
+    vec_second.wait()
+    vec[...] = vec_second.total()
+    for k in range(nj):
+        @pl.when(c == k)
+        def _():
+            first = k * chans
+            row = vec[8 + first // 128:9 + first // 128, :]
+            gain[...] = to_column(row[:, first % 128:first % 128 + chans])
+    if direct:
+        early.first_hop()
+
     for q in range(packs):
-        settle(u, in_sems, q)
-        forward_pack(dims, q, skip, keep, u, out, slope, carry, pw, xs, ys, sc)
+        shared(u, in_sems, q)
+        forward_pack(dims, q, skip, gain, span, u, out, slope, carry, pw, xs, ys, sc)
         share(out, act, out_sems, q)
         if direct:
             if q == 0:
-                gather.first_hop()
-            if q == 1:
-                gather.second_hop()
+                early.second_hop()
+                late.first_hop()
+            if q == 2:
+                early.last_hop()
             if q == 3:
-                gather.last_hop()
+                late.second_hop()
     for q in range(packs):
-        settle(act, out_sems, q)
-    if direct:
-        gather.finish()
-
+        shared(act, out_sems, q)
+    if direct:
+        early.finish()
+
+    def rows_up(m, _):
+        dense_up(m, t, tokens, act, wholes[0], wholes[1], vec, keeps)
+        return 0
+    lax.fori_loop(0, mb, rows_up, 0)
+    if direct:
+        late.last_hop()
+    outer_products(hidden, cot, g_back)
+    if direct:
+        ahead.to_twin(0)
+        late.finish()
     for m in range(mb):
-        dense_rows(m, t, tokens, cot, act, wholes, vec, block_out, second, hidden, gb, gp, gm, snd, sums, nj, chans)
+        dense_down(m, t, cot, wholes, vec, block_out, keeps, gb, gp, snd, sums)
         at = pl.ds(m * t, t)
         for p in peers(nj, c):
             send(snd.at[p, :, at], ga.at[c, :, at], back_sems.at[0, m], back_sems.at[1, m], (d, p))
         ga[c, :, at] = snd[c, :, at]
-    weight_grads(act, gp, second, gb, hidden, cot, grads, nj, scatter)
+        if direct and m == 0:
+            ahead.add_twin()
+    vec2_chan[c] = sums[...]
+    sums_first.start()
+    outer_products(second, gb, g_in)
+    if direct:
+        rest.to_twin(1)
+    def outer(n, _):
+        g_out[n] = shaped(nn(flat(act[pl.ds(n * (nj // 4), nj // 4)]), gp[...]), g_out)
+        return 0
+    lax.fori_loop(0, 4, outer, 0)
+    if direct:
+        rest.to_twin(0)
+        ahead.add_first()
     for m in range(mb):
-        whole = ga.at[pl.ds(0, nj - 1), :, pl.ds(m * t, t)]
-        pltpu.make_async_remote_copy(src_ref=whole, dst_ref=whole, send_sem=back_sems.at[0, m], recv_sem=back_sems.at[1, m], device_id=here, device_id_type=MESH).wait()
+        settle(ga.at[pl.ds(0, nj - 1), :, pl.ds(m * t, t)], back_sems.at[0, m], back_sems.at[1, m], here)
+    if direct:
+        rest.add_twin()
 
     for q in range(packs):
-        backward_pack(dims, q, skip, keep, u, ga, slope, carry, out, zw_dp.at[d], pw, xs, gy, ys, sc)
+        backward_pack(dims, q, skip, gain, span, u, ga, slope, carry, out, zw_dp.at[d], ng_dp.at[d], pw, xs, gy, ys, sc)
         share(out, gn, gn_sems, q)
+        if q == 0:
+            sums_first.wait()
+            vec2_dp[d] = sums_first.total()
+            sums_second.start()
         if direct:
             if q == 0:
-                scatter.add_twin()
+                ahead.add_second(n_dp)
+            if q == 1:
+                rest.add_first()
             if q == 2:
-                scatter.add_first()
-            if q == 3:
-                scatter.add_second(n_dp)
-    exchange_start(zw_dp, box_sems.at[3], n_dp, d, over_dp)
+                rest.add_second(n_dp)
+    zw_all.start()
+    ng_first.start()
+    sums_second.wait()
+    sums[...] = sums_second.total()
+    for k, (first, own) in enumerate(zip((0, 8, 12, 16), g_vectors)):
+        if k != 1:
+            own[...] = pick_own(sums, first, own.shape[1], shard)
+    ng_first.wait()
+    ng_chan[c, 0:1, :] = padded(column_sum(ng_first.total().T))
+    ng_chan[c, 1:8, :] = jnp.zeros((7, 128), F32)
+    ng_second.start()
+    if direct:
+        ahead.finish(results[2:], n_dp)
+        rest.finish(results[:2], n_dp)
+    zw_all.wait()
+    zw = [sum(zw_dp[k, a] for k in range(n_dp)) for a in range(5)]
+    found = list(mode_gradients([modes[a] for a in range(5)], zw)) + [zw[4]]
+    mode_rows_box[...] = collect_modes(found)
+    g_step[...] = column_sum(mode_rows_box[0:32, :])[:, :chans]
+    g_skip[...] = mode_rows_box[160:161, :chans]
+    for a in range(4):
+        each = g_modes[a].shape[0]
+        g_modes[a][...] = mode_rows_box[pl.ds(32 * (a + 1) + d * each, each), :chans]
     for q in range(packs):
-        settle(gn, gn_sems, q)
+        shared(gn, gn_sems, q)
+    wide_gain = wide(vec, 8, feats // 128)
 
     def finish_rows(m, _):
-        at = pl.ds(pl.multiple_of(m * t, t), t)
+        at = row_block(m, t)
         n, scale = layer_stats(tokens[at, :].astype(F32))
         grad = gn[:, :, at].reshape(feats, t).astype(F32).T
-        add_wide(sums, 8, column_sum(grad * n))
-        grad_tokens[at, :] = (gm[at, :] + layer_back(grad * gain, n, scale)).astype(BF16)
+        grad_tokens[at, :] = (middle[at, :] + layer_back(grad * wide_gain, n, scale)).astype(BF16)
         return 0
     lax.fori_loop(0, mb, finish_rows, 0)
-
-    vec_chan[c] = sums[...]
-    exchange_start(vec_chan, box_sems.at[4], nj, c, over_chan)
-    exchange_wait(zw_dp, box_sems.at[3], n_dp, here)
-    zw = [sum(zw_dp[k, a] for k in range(n_dp)) for a in range(5)]
-    for k, x in enumerate(mode_gradients([modes[a] for a in range(5)], zw)):
-        mode_out[k] = x
-    mode_out[5] = zw[4]
-    exchange_wait(vec_chan, box_sems.at[4], nj, here)
-    vec_dp[d] = sum(vec_chan[k] for k in range(nj))
-    exchange_start(vec_dp, box_sems.at[5], n_dp, d, over_dp)
-    if direct:
-        scatter.finish(results, n_dp)
-    exchange_wait(vec_dp, box_sems.at[5], n_dp, here)
-    vec_out[...] = sum(vec_dp[k] for k in range(n_dp))
+    ng_second.wait()
+    size = g_vectors[1].shape[1]
+    start = shard * size
+    row = ng_chan[start // chans]
+    g_vectors[1][...] = pltpu.roll(row, lax.rem(128 - lax.rem(start, chans), 128), 1)[0:1, :size]
     if direct:
         gather_copies.finish()
         scatter_copies.finish()
 
 
-def whole(tokens, cot, vec, modes, skip, keep, weights, mb, n_dp, nj):
+def whole(tokens, cot, lengths, log_step, skip, mode_parts, vectors, weights, mb, n_dp, nj):
     width, feats = tokens.shape
     chans = feats // nj
     t = width // mb
@@ -791,7 +938,7 @@
     blocks = nj * h
     rows = mb * blocks
     packs = chans // PACK
-    groups = modes.shape[1]
+    groups = chans // 4
     direct = nj == 8 and n_dp == 4 and packs == 4 and all(w.shape[0] % 16 == 0 for w in weights)
     if not direct:
         weights = [lax.all_gather(w, ("dp", "chan"), axis=0, tiled=True) for w in weights]
@@ -800,43 +947,70 @@
     full = [(4, 2, 2, 2) + p for p in per]
     ff = per[1][1]
     shape = jax.ShapeDtypeStruct
-    shapes = [
-        shape((width, feats), BF16), shape((width, feats), BF16), shape((6,) + modes.shape[1:], F32), shape(vec.shape, F32),
-    ] + ([shape(p, F32) for p in per] if direct else [shape(f, BF16) for f in full])
+    shapes = [shape((width, feats), BF16)] * 2 + [shape((1, chans), F32)] * 2
+    shapes += [shape(x.shape, F32) for x in mode_parts] + [shape(x.shape, F32) for x in vectors]
+    shapes += [shape(p, F32) for p in per] if direct else [shape(f, BF16) for f in full]
     dma, vm = pltpu.SemaphoreType.DMA, pltpu.VMEM
+    sheet, grid = (32, 128), (groups, 128)
     scratch = [vm((nj, chans, width), BF16)] * 6 + [
         vm((packs, rows * PACK, 128), F32),
         vm((packs, 4, blocks * PACK, 128), F32),
-        vm((width, feats), BF16), vm((width, ff), BF16), vm((width, ff), BF16), vm((width, 2 * feats), BF16), vm((width, feats), F32),
-        vm((n_dp,) + vec.shape, F32), vm((nj,) + vec.shape, F32), vm((n_dp, 4) + modes.shape[1:], F32),
-        vm((n_dp, 5) + modes.shape[1:], F32), vm(modes.shape, F32), vm(vec.shape, F32), vm(vec.shape, F32),
-        vm((18, groups, 128), F32),
+        vm((width, feats), BF16), vm((width, ff), BF16), vm((width, ff), BF16), vm((width, 2 * feats), BF16),
+        vm((width, feats), F32), vm((width, feats), F32), vm((width, feats), F32), vm((width, ff), F32),
+        vm((n_dp,) + sheet, F32), vm((nj,) + sheet, F32), vm((n_dp,) + sheet, F32), vm((nj,) + sheet, F32),
+        vm((n_dp, 4, mode_parts[0].shape[0], 128), F32),
+        vm((n_dp, 5) + grid, F32), vm((n_dp, chans, 128), F32), vm((nj, 8, 128), F32),
+        vm((5,) + grid, F32), vm(sheet, F32), vm(sheet, F32), vm((chans, 128), F32), vm((chans, 128), F32), vm((192, 128), F32),
+        vm((18,) + grid, F32),
         vm((rows * PACK, 128), F32), vm((rows * PACK, 128), F32), vm((rows * PACK, 128), F32),
         vm((4, blocks * PACK, 128), F32),
-        dma((6, 2)), dma((2, packs)), dma((2, packs)), dma((2, mb)), dma((2, packs)),
+        dma((8, 2)), dma((2, packs)), dma((2, packs)), dma((2, mb)), dma((2, packs)),
     ]
     if direct:
+        half = [(r, k // 2) for r, k in per]
         scratch += [vm(f, BF16) for f in full] * 2
-        half = [(r, k // 2) for r, k in per]
         scratch += [vm((4, 2, 2) + p, BF16) for p in per]
         scratch += [vm((4, 2) + p, BF16) for p in half] * 2
         scratch += [vm((4,) + p, BF16) for p in half] * 2
         scratch += [vm((4,) + p, BF16) for p in per]
-        scratch += [dma((2, 36)), dma((2, 33))]
+        scratch += [dma((2, 42)), dma((2, 33))]
     vmem = pl.BlockSpec(memory_space=pltpu.VMEM)
     outs = pl.pallas_call(
         functools.partial(whole_kernel, (nj, chans, mb, h), n_dp, direct),
         out_shape=shapes,
-        in_specs=[vmem] * 9,
-        out_specs=[vmem] * 7,
+        in_specs=[vmem] * 16,
+        out_specs=[vmem] * len(shapes),
         scratch_shapes=scratch,
-        compiler_params=pltpu.CompilerParams(collective_id=0, has_side_effects=True, vmem_limit_bytes=60 << 20),
+        compiler_params=pltpu.CompilerParams(collective_id=0, has_side_effects=True, vmem_limit_bytes=62 << 20),
         name="whole",
-    )(tokens, cot, vec, modes, skip, keep, *weights)
-    grads = outs[4:]
-    if not direct:
-        grads = [lax.psum_scatter(g.reshape(-1, g.shape[-1]).astype(F32), ("dp", "chan"), scatter_dimension=0, tiled=True) for g in grads]
-    return outs[:4], grads
+    )(tokens, cot, lengths, log_step, skip, *mode_parts, *vectors, *weights)
+    if direct:
+        return deliver(outs)
+    outs, grads = outs[:12], outs[12:]
+    grads = [lax.psum_scatter(g.reshape(-1, g.shape[-1]).astype(F32), ("dp", "chan"), scatter_dimension=0, tiled=True) for g in grads]
+    return deliver(outs) + grads
+
+
+def deliver_kernel(*refs):
+    n = (len(refs) - 1) // 2
+    sems = refs[-1]
+    copies = [pltpu.make_async_copy(refs[k], refs[n + k], sems.at[k]) for k in range(n)]
+    for copy in copies:
+        copy.start()
+    for copy in copies:
+        copy.wait()
+
+
+def deliver(arrays):
+    anywhere = pl.BlockSpec(memory_space=pl.ANY)
+    return list(pl.pallas_call(
+        deliver_kernel,
+        out_shape=[jax.ShapeDtypeStruct(x.shape, x.dtype) for x in arrays],
+        in_specs=[pl.BlockSpec(memory_space=pltpu.VMEM)] * len(arrays),
+        out_specs=[anywhere] * len(arrays),
+        scratch_shapes=[pltpu.SemaphoreType.DMA((len(arrays),))],
+        name="deliver",
+    )(*arrays))
 
 
 def on_device(
@@ -844,36 +1018,16 @@
     skip_gain, out_weight, out_bias, ffn_gain, in_weight, in_bias, back_weight,
 ):
     mb, rows, feats = tokens.shape
-    chans, groups = log_decay.shape
     nj, n_dp = lax.axis_size("chan"), lax.axis_size("dp")
-    shards = n_dp * nj
-    place = lax.axis_index("dp") * nj + lax.axis_index("chan")
-    vectors = (out_bias, norm_gain, ffn_gain, in_bias)
-
-    def placed(x):
-        return lax.dynamic_update_slice(jnp.zeros((shards * x.shape[0],), F32), x.astype(F32), (place * x.shape[0],))
-    vec = jnp.concatenate([placed(x) for x in vectors]).reshape(-1, 128)
-    mine = jnp.arange(groups * n_dp) // groups == lax.axis_index("dp")
-    modes = [jnp.broadcast_to(log_step[:, None], (chans, groups * n_dp))]
-    modes += [jnp.where(mine, jnp.tile(x, (1, n_dp)), 0.0) for x in (log_decay, frequency, readout_real, readout_imaginary)]
-    modes = jnp.stack([x.reshape(-1, 128) for x in modes])
-    skip = jnp.broadcast_to(skip_gain[:, None], (chans, 128))
-    keep = keep_rows(lengths[:, 0], nj * rows // SPAN, mb)
-    (block_out, grad_tokens, mode_grads, vec), (g_out, g_in, g_back) = whole(
-        tokens.reshape(mb * rows, feats), cotangent.reshape(mb * rows, feats), vec, modes, skip, keep,
+    flat_rows = (mb * rows, feats)
+    block_out, grad_tokens, g_ls, g_skip, g_ld, g_fr, g_rr, g_ri, g_bo, g_g1, g_g2, g_bi, g_out, g_in, g_back = whole(
+        tokens.reshape(flat_rows), cotangent.reshape(flat_rows), lengths.T, log_step.reshape(1, -1), skip_gain.reshape(1, -1),
+        [x.T for x in (log_decay, frequency, readout_real, readout_imaginary)],
+        [x.reshape(1, -1) for x in (out_bias, norm_gain, ffn_gain, in_bias)],
         (out_weight, in_weight, back_weight), mb, n_dp, nj)
-    g_ls, g_ld, g_fr, g_rr, g_ri, g_skip = (x.reshape(chans, -1) for x in mode_grads)
-    first = lax.axis_index("dp") * groups
-    own = [lax.dynamic_slice_in_dim(x, first, groups, 1) for x in (g_ld, g_fr, g_rr, g_ri)]
-    vec = vec.reshape(-1)
-    cuts, start = [], 0
-    for x in vectors:
-        cuts.append(lax.dynamic_slice_in_dim(vec, start + place * x.shape[0], x.shape[0], 0))
-        start += shards * x.shape[0]
-    g_bo, g_g1, g_g2, g_bi = cuts
     return (
-        block_out.reshape(tokens.shape), grad_tokens.reshape(tokens.shape), g_g1, jnp.sum(g_ls, 1), *own, g_skip[:, 0],
-        g_out, g_bo, g_g2, g_in, g_bi, g_back,
+        block_out.reshape(tokens.shape), grad_tokens.reshape(tokens.shape), g_g1.reshape(-1), g_ls.reshape(-1),
+        g_ld.T, g_fr.T, g_rr.T, g_ri.T, g_skip.reshape(-1), g_out, g_bo.reshape(-1), g_g2.reshape(-1), g_in, g_bi.reshape(-1), g_back,
     )
 
 

time: 166 us -> 126 us (0.76)
  local copies, waits for them, and re-layouts: 22.7 us -> 0 us
  Pallas kernels: 140 us -> 125 us
  other arithmetic: 1.82 us -> 0 us
    pallas_call x1, Pallas kernels: 140 us -> 122 us  [whole(): pl.pallas_call(functools.partial(whole_kernel, (nj, chans, mb, h), n_dp,...]
    unnamed x48 -> x0, local copies, waits for them, and re-layouts: 14.2 us -> none
    dynamic_slice x5 -> x0, local copies, waits for them, and re-layouts: 4.02 us -> none  [the longest x3 3.86 us: on_device(): lax.dynamic_slice_in_dim(vec, start + place * x.shape[0], x.shape[0], 0)]
    pallas_call x0 -> x1, Pallas kernels: none -> 2.93 us  [deliver(): pl.pallas_call(deliver_kernel, out_shape=[jax.ShapeDtypeStruct(x.shape, x...]
    another operation x17 -> x0, local copies, waits for them, and re-layouts: 1.99 us -> none  [the longest x1 0.86 us: on_device(): g_ls, g_ld, g_fr, g_rr, g_ri, g_skip = (x.reshape(chans, -1) for x in mod...]
    broadcast_in_dim x10 -> x0, local copies, waits for them, and re-layouts: 1.8 us -> none  [the longest x1 0.76 us: keep_rows(): return jnp.broadcast_to(rows[:, :, None], (blocks, PACK, 128))]
where the time goes in v4:
time: 126 us; the launch traced here: 125 us
  Pallas kernels  125 us (99%)
    pallas_call x1, Pallas kernels, whole(): pl.pallas_call(functools.partial(whole_kernel, (nj, chans, mb, h), n_dp,...  122 us
    pallas_call x1, Pallas kernels, deliver(): pl.pallas_call(deliver_kernel, out_shape=[jax.ShapeDtypeStruct(x.shape, x...  2.93 us

profile of v4, /device:TPU:0, one launch (start us, length us, event | category | flops | bytes accessed | tf_op | source)
XLA Modules:
  0.0 125.4 jit_solution(1706377320474349173)
XLA Ops:
  0.7 121.6 %whole.1 = (bf16[768,512]{1,0:T(8,128)(2,1)}, bf16[768,512]{1,0:T(8,128)(2,1)}, f32[1,64]{1,0:T(1,128)}, f32[1,64]{1,0:T(1,128)}, f32[8,64]{1,0:T(8,128)}, /*ind...) custom-call(bf16[768,512]{1,0:T(8,128)(2,1)} %bitcast.25, ...), custom_call_target="tpu_custom_call" | custom-call | tf_op jit(solution)/shard_map/whole/pallas_call | solution.py:978
  122.3 2.9 %deliver.1 = (bf16[768,512]{1,0:T(8,128)(2,1)}, bf16[768,512]{1,0:T(8,128)(2,1)}, f32[1,64]{1,0:T(1,128)}, f32[1,64]{1,0:T(1,128)}, f32[8,64]{1,0:T(8,128)}, /*i...) custom-call(bf16[768,512]{1,0:T(8,128)(2,1)} %get-tuple-element.45.r, ...), custom_call_target="tpu_custom_call" | custom-call | tf_op jit(solution)/shard_map/deliver/pallas_call | solution.py:1006

commit v5 on v4

--- a/solution.py
+++ b/solution.py
@@ -1,5 +1,7 @@
 import functools
 import jax
+import ml_dtypes
+import numpy as np
 import jax.numpy as jnp
 from jax import lax
 from jax.experimental import pallas as pl
@@ -7,6 +9,8 @@
 from jax.sharding import PartitionSpec as P
 
 SPAN = 128
+FU = 2
+SU = 2
 PACK = 16
 HI = lax.Precision.HIGHEST
 
@@ -99,17 +103,39 @@
     return jnp.where(t >= s, whole, 0.0).astype(jnp.bfloat16)
 
 
-def lag_sums(g):
-    s = lax.broadcasted_iota(jnp.int32, (SPAN, 128), 0)
-    t = lax.broadcasted_iota(jnp.int32, (SPAN, 128), 1)
-    g = jnp.where(t >= s, g, 0.0)
-    n = SPAN
-    while n > 8:
-        n //= 2
-        g = g[:n] + pltpu.roll(g[n:], 128 - n, 1)
-    for n in (4, 2, 1):
-        g = g + pltpu.roll(pltpu.roll(g, 128 - n, 1), 8 - n, 0)
-    return g[0:1]
+def wave_tables():
+    angle = 2.0 * np.pi * np.outer(np.arange(SPAN), np.arange(SPAN)) / (2 * SPAN)
+    turn = np.cos(np.pi * np.arange(SPAN))
+    cosines, sines = np.cos(angle), np.sin(angle)
+    there = np.concatenate([cosines, sines], 1)
+    there[:, SPAN] = turn
+    high = there.astype(ml_dtypes.bfloat16)
+    low = (there - high.astype(np.float64)).astype(ml_dtypes.bfloat16)
+    back = np.concatenate([2.0 * cosines, -2.0 * sines], 0)
+    back[0] = 1.0
+    back[SPAN] = turn
+    return np.concatenate([high, low], 0), (back / (2 * SPAN)).astype(np.float32)
+
+
+def lag_sums(xs, gy, rows, there, back):
+    step = 8 * PACK
+    table = there[...]
+
+    def spectrum(x):
+        x = x.astype(jnp.bfloat16)
+        return nn(jnp.concatenate([x, x], 1), table)
+
+    def one(n, sums):
+        at = pl.ds(pl.multiple_of(n * step, step), step)
+        u, g = spectrum(xs[at, :]), spectrum(gy[at, :])
+        u_c, u_s, g_c, g_s = u[:, :128], u[:, 128:], g[:, :128], g[:, 128:]
+        parts = (u_c * g_c, u_s * g_s, g_c * u_s - g_s * u_c)
+        return tuple(x + jnp.sum(p.reshape(8, PACK, 128), axis=0) for x, p in zip(sums, parts))
+    even, odd, cross = lax.fori_loop(0, rows // 8, one, (jnp.zeros((PACK, 128), jnp.float32),) * 3)
+    ends = lax.broadcasted_iota(jnp.int32, (PACK, 128), 1) == 0
+    real = even + jnp.where(ends, 0.0, odd)
+    imag = jnp.where(ends, odd, cross)
+    return nn(jnp.concatenate([real, imag], 1), back[...], precision=HI)
 
 
 def lane_owner(rows):
@@ -156,24 +182,69 @@
     return jnp.concatenate(parts, 0)
 
 
-def forward_pack(dims, q, skip_ref, gain_ref, span, u_ref, act_ref, slope_ref, carry_ref, pw_ref, xs, ys, sc):
+def table_place(store, g, width, first=0):
+    per = store.shape[1] // width
+    g = g + first
+    return store.at[pl.ds(pl.multiple_of(g // per * SPAN, SPAN), SPAN), pl.ds(pl.multiple_of(lax.rem(g, per) * width, width), width)]
+
+
+def forward_tables(pw_ref, groups, early, toep):
+    def one(g, _):
+        rws = group_rows(pw_ref, g)
+        p_r, p_i = power_table(rws, True)
+        back = (SPAN - 1 - lax.broadcasted_iota(jnp.int32, (SPAN, 128), 0)).astype(jnp.float32)
+        table_place(early, g, 512)[...] = jnp.concatenate([p_r, p_i, back * p_r, back * p_i], 1).astype(jnp.bfloat16)
+        e_r, e_i = power_table(rws, False)
+        w_r, w_i = jnp.concatenate([rws[16]] * 16, 0), jnp.concatenate([rws[17]] * 16, 0)
+        r_r, r_i = cmul(e_r, e_i, w_r, w_i)
+        table_place(early, g, 256, 2 * groups)[...] = jnp.concatenate([r_r, -r_i], 1).astype(jnp.bfloat16)
+        krow = kernel_rows(r_r, rws[16])
+        for k in range(4):
+            toep[4 * g + k] = toeplitz(krow[k:k + 1])
+        return 0
+    lax.fori_loop(0, groups, one, 0, unroll=2)
+
+
+def backward_tables(pw_ref, groups, state_tab, read_tab):
+    def one(g, _):
+        rws = group_rows(pw_ref, g)
+        e_r, e_i = power_table(rws, False)
+        ahead = (1 + lax.broadcasted_iota(jnp.int32, (SPAN, 128), 0)).astype(jnp.float32)
+        state_tab[g] = jnp.concatenate([e_r, e_i, ahead * e_r, ahead * e_i], 1).astype(jnp.bfloat16)
+        p_r, p_i = power_table(rws, True)
+        w_r, w_i = jnp.concatenate([rws[16]] * 16, 0), jnp.concatenate([rws[17]] * 16, 0)
+        r_r, r_i = cmul(p_r, p_i, w_r, w_i)
+        read_tab[g] = jnp.concatenate([r_r, -r_i], 1).astype(jnp.bfloat16)
+        return 0
+    lax.fori_loop(0, groups, one, 0, unroll=2)
+
+
+def channel_rows(box, c, rows):
+    return box[pl.ds(c, rows, stride=PACK), :].astype(jnp.bfloat16)
+
+
+def put_states(sc, s, g, mb, blocks):
+    for a in range(4):
+        for m in range(mb):
+            sc[a, pl.ds(g * mb + m, blocks, stride=PACK), :] = s[m * blocks:(m + 1) * blocks, a * 128:(a + 1) * 128]
+
+
+def get_carry(ref, g, mb, blocks):
+    return jnp.concatenate([
+        jnp.concatenate([ref[a, pl.ds(g * mb + m, blocks, stride=PACK), :] for m in range(mb)], 0) for a in range(2)], 1)
+
+
+def forward_pack(dims, q, skip_ref, gain_ref, span, early, toep, u_ref, act_ref, slope_ref, carry_ref, pw_ref, xs, ys, sc, poll):
     nj, chans, mb, h = dims
     blocks = nj * h
     rows = mb * blocks
     unpack(u_ref, q, xs, nj, mb, h, blocks, gain_ref[block_rows(q), :])
 
     def states(g, _):
-        rws = group_rows(pw_ref, q * 4 + g)
-        p_r, p_i = power_table(rws, True)
-        back = (SPAN - 1 - lax.broadcasted_iota(jnp.int32, (SPAN, 128), 0)).astype(jnp.float32)
-        table = jnp.concatenate([p_r, p_i, back * p_r, back * p_i], 1).astype(jnp.bfloat16)
-        x = jnp.concatenate([xs[pl.ds(4 * g + k, rows, stride=PACK), :] for k in range(4)], 0).astype(jnp.bfloat16)
-        s = fold(nn(x, table), rows)
-        for a in range(4):
-            for m in range(mb):
-                sc[a, pl.ds(g * mb + m, blocks, stride=PACK), :] = s[m * blocks:(m + 1) * blocks, a * 128:(a + 1) * 128]
+        x = jnp.concatenate([channel_rows(xs, 4 * g + k, rows) for k in range(4)], 0)
+        put_states(sc, fold(nn(x, table_place(early, q * 4 + g, 512)[...]), rows), g, mb, blocks)
         return 0
-    lax.fori_loop(0, 4, states, 0, unroll=2)
+    lax.fori_loop(0, 4, states, 0, unroll=FU)
     h_r, h_i = rows_of(pw_ref, 14, q, mb), rows_of(pw_ref, 15, q, mb)
 
     def step(i, c):
@@ -187,25 +258,18 @@
         d_r, d_i = cmul(c[2] + SPAN * c[0], c[3] + SPAN * c[1], h_r, h_i)
         return (z_r + s[0], z_i + s[1], d_r + s[2], d_i + s[3])
     zero = jnp.zeros((PACK, 128), jnp.float32)
-    lax.fori_loop(0, blocks, step, (zero,) * 4)
+    lax.fori_loop(0, blocks, step, (zero,) * 4, unroll=SU)
+    poll(f'f{q}a')
 
     def outputs(g, _):
-        rws = group_rows(pw_ref, q * 4 + g)
-        e_r, e_i = power_table(rws, False)
-        w_r, w_i = jnp.concatenate([rws[16]] * 16, 0), jnp.concatenate([rws[17]] * 16, 0)
-        r_r, r_i = cmul(e_r, e_i, w_r, w_i)
-        krow = kernel_rows(r_r, rws[16])
-        table = jnp.concatenate([r_r, -r_i], 1).astype(jnp.bfloat16)
-        c = jnp.concatenate([
-            jnp.concatenate([carry_ref[q, a, pl.ds(g * mb + m, blocks, stride=PACK), :] for m in range(mb)], 0)
-            for a in range(2)], 1)
-        across = nt(spread(c, rows).astype(jnp.bfloat16), table)
+        c = get_carry(carry_ref.at[q], g, mb, blocks)
+        across = nt(spread(c, rows).astype(jnp.bfloat16), table_place(early, q * 4 + g, 256, 2 * (chans // 4))[...])
         for k in range(4):
-            x = xs[pl.ds(4 * g + k, rows, stride=PACK), :].astype(jnp.bfloat16)
-            y = across[k * rows:(k + 1) * rows] + nn(x, toeplitz(krow[k:k + 1]))
+            y = across[k * rows:(k + 1) * rows] + nn(channel_rows(xs, 4 * g + k, rows), toep[q * PACK + 4 * g + k])
             ys[pl.ds(4 * g + k, rows, stride=PACK), :] = y
         return 0
-    lax.fori_loop(0, 4, outputs, 0, unroll=2)
+    lax.fori_loop(0, 4, outputs, 0, unroll=FU)
+    poll(f'f{q}b')
     skip = skip_ref[block_rows(q), :]
 
     def finish(j, _):
@@ -220,11 +284,12 @@
     lax.fori_loop(0, nj, finish, 0)
 
 
-def backward_pack(dims, q, skip_ref, gain_ref, span, u_ref, ga_ref, slope_ref, carry_ref, gn_ref, zw_ref, ng_ref, pw_ref, xs, gy, gx, sc):
+def backward_pack(dims, q, skip_ref, gain_ref, span, state_tab, read_tab, toep, waves, u_ref, ga_ref, slope_ref, carry_ref, gn_ref, zw_ref, ng_ref, pw_ref, xs, gy, gx, sc, lags, poll):
     nj, chans, mb, h = dims
     blocks = nj * h
     rows = mb * blocks
     unpack(u_ref, q, xs, nj, mb, h, blocks, gain_ref[block_rows(q), :])
+
     def start(j, _):
         for m in range(mb):
             for k in range(h):
@@ -233,41 +298,29 @@
                 gy[block_rows(r), :] = x.astype(jnp.float32) * slope_ref[q, block_rows(r), :]
         return 0
     lax.fori_loop(0, nj, start, 0)
+    lags[...] = lag_sums(xs, gy, rows, *waves)
+    poll(f'b{q}a')
 
     def states(g, _):
         gg = q * 4 + g
-        rws = group_rows(pw_ref, gg)
-        e_r, e_i = power_table(rws, False)
-        ahead = (1 + lax.broadcasted_iota(jnp.int32, (SPAN, 128), 0)).astype(jnp.float32)
-        table = jnp.concatenate([e_r, e_i, ahead * e_r, ahead * e_i], 1).astype(jnp.bfloat16)
-        ups = [gy[pl.ds(4 * g + k, rows, stride=PACK), :].astype(jnp.bfloat16) for k in range(4)]
-        lag = []
-        for k in range(4):
-            x = xs[pl.ds(4 * g + k, rows, stride=PACK), :].astype(jnp.bfloat16)
-            lag.append(lag_sums(tn(x, ups[k])))
-        lag = jnp.concatenate(lag + [jnp.zeros((4, 128), jnp.float32)], 0)
+        ups = [channel_rows(gy, 4 * g + k, rows) for k in range(4)]
+        lag = jnp.concatenate([lags[pl.ds(4 * g, 4), :], jnp.zeros((4, 128), jnp.float32)], 0)
         own8 = lax.broadcasted_iota(jnp.int32, (8, 128), 1) // 32 == lax.broadcasted_iota(jnp.int32, (8, 128), 0)
         lag0 = jnp.sum(jnp.where(own8, jnp.broadcast_to(lag[:, 0:1], (8, 128)), 0.0), axis=0, keepdims=True)
         lane = lax.broadcasted_iota(jnp.int32, (8, 128), 1)
         later = jnp.where(lane == 127, 0.0, pltpu.roll(lag, 127, 1))
         top = later.astype(jnp.bfloat16)
         low = (later - top.astype(jnp.float32)).astype(jnp.bfloat16)
-        stack = jnp.concatenate(ups + [top, low], 0)
-        s = nn(stack, table)
+        s = nn(jnp.concatenate(ups + [top, low], 0), state_tab[gg])
         near = s[4 * rows:4 * rows + 8] + s[4 * rows + 8:]
-        own = jnp.concatenate([own8] * 4, 1)
-        near = jnp.sum(jnp.where(own, near, 0.0), axis=0, keepdims=True)
+        near = jnp.sum(jnp.where(jnp.concatenate([own8] * 4, 1), near, 0.0), axis=0, keepdims=True)
         zw_ref[0, pl.ds(gg, 1), :] = near[:, 0:128] + lag0
         for a in range(1, 4):
             zw_ref[a, pl.ds(gg, 1), :] = near[:, a * 128:(a + 1) * 128]
         zw_ref[4, pl.ds(gg, 1), :] = lag0
-        s = fold(s[:4 * rows], rows)
-        for a in range(4):
-            for m in range(mb):
-                sc[a, pl.ds(g * mb + m, blocks, stride=PACK), :] = s[m * blocks:(m + 1) * blocks, a * 128:(a + 1) * 128]
+        put_states(sc, fold(s[:4 * rows], rows), g, mb, blocks)
         return 0
-    lax.fori_loop(0, 4, states, 0, unroll=2)
-
+    lax.fori_loop(0, 4, states, 0, unroll=FU)
     h_r, h_i = rows_of(pw_ref, 14, q, mb), rows_of(pw_ref, 15, q, mb)
 
     def step(n, c):
@@ -285,33 +338,23 @@
         n_r, n_i = cmul(a_r, a_i, h_r, h_i)
         return ((n_r + q_[0]) * keep, (n_i + q_[1]) * keep, z_r + d[0], z_i + d[1], w_r + e1[0] + e2[0], w_i + e1[1] + e2[1])
     zero = jnp.zeros((PACK, 128), jnp.float32)
-    out = lax.fori_loop(0, blocks, step, (zero,) * 6)
+    out = lax.fori_loop(0, blocks, step, (zero,) * 6, unroll=SU)
     for a in range(4):
         for g in range(4):
             add = jnp.sum(out[2 + a][g * mb:(g + 1) * mb], axis=0, keepdims=True)
             zw_ref[a, pl.ds(q * 4 + g, 1), :] += add
+    poll(f'b{q}b')
 
     def outputs(g, _):
-        rws = group_rows(pw_ref, q * 4 + g)
-        e_r, e_i = power_table(rws, False)
-        w_r, w_i = jnp.concatenate([rws[16]] * 16, 0), jnp.concatenate([rws[17]] * 16, 0)
-        r_r = e_r * w_r - e_i * w_i
-        krow = kernel_rows(r_r, rws[16])
-        p_r, p_i = power_table(rws, True)
-        r_r, r_i = cmul(p_r, p_i, w_r, w_i)
-        table = jnp.concatenate([r_r, -r_i], 1).astype(jnp.bfloat16)
-        c = jnp.concatenate([
-            jnp.concatenate([sc[a, pl.ds(g * mb + m, blocks, stride=PACK), :] for m in range(mb)], 0)
-            for a in range(2)], 1)
-        across = nt(spread(c, rows).astype(jnp.bfloat16), table)
+        across = nt(spread(get_carry(sc, g, mb, blocks), rows).astype(jnp.bfloat16), read_tab[q * 4 + g])
         for k in range(4):
-            up = gy[pl.ds(4 * g + k, rows, stride=PACK), :].astype(jnp.bfloat16)
-            y = across[k * rows:(k + 1) * rows] + nt(up, toeplitz(krow[k:k + 1]))
+            y = across[k * rows:(k + 1) * rows] + nt(channel_rows(gy, 4 * g + k, rows), toep[q * PACK + 4 * g + k])
             gx[pl.ds(4 * g + k, rows, stride=PACK), :] = y
         return 0
-    lax.fori_loop(0, 4, outputs, 0, unroll=2)
-
+    lax.fori_loop(0, 4, outputs, 0, unroll=FU)
+    poll(f'b{q}c')
     skip = skip_ref[block_rows(q), :]
+
     def finish(j, total):
         for m in range(mb):
             for k in range(h):
@@ -379,7 +422,10 @@
         pl.semaphore_signal(barrier, inc=1, device_id=(p, c), device_id_type=MESH)
     for p in peers(n_chan, c):
         pl.semaphore_signal(barrier, inc=1, device_id=(d, p), device_id_type=MESH)
-    pl.semaphore_wait(barrier, n_dp + n_chan - 2)
+
+
+def be_greeted(n_dp, n_chan):
+    pl.semaphore_wait(pltpu.get_barrier_semaphore(), n_dp + n_chan - 2)
 
 
 def send(src, dst, send_sem, recv_sem, to):
@@ -451,127 +497,196 @@
         return self.at(self.a, self.b, 1 - self.core)
 
 
-def halves(w):
-    cols = w.shape[-1] // 2
-    return pl.ds(0, cols), pl.ds(cols, cols)
+class Part:
+    def __init__(self, rows, low, high):
+        self.rows, self.low, self.high = rows, low, high
+        self.all = pl.ds(low.start, low.size + high.size)
+
+
+def parts_of(w_out, w_in, w_back):
+    def cut(w, rows, first, cols):
+        return Part(rows, pl.ds(first, cols // 2), pl.ds(first + cols // 2, cols // 2))
+    r, k = w_out.shape[-2:]
+    some = [(0, cut(w_out, pl.ds(0, r), 0, k))]
+    r, k = w_in.shape[-2:]
+    some += [(1, cut(w_in, pl.ds(0, r), n * (k // 2), k // 2)) for n in range(2)]
+    r, k = w_back.shape[-2:]
+    some += [(2, cut(w_back, pl.ds(n * (r // 2), r // 2), 0, k)) for n in range(2)]
+    return some
 
 
 class Gather:
-    def __init__(self, owns, wholes, copies, here):
-        self.owns, self.wholes, self.copies, self.here = owns, wholes, copies, here
-        self.side = []
+    def __init__(self, w, part, dp_first, copies, here, n_dp):
+        self.w, self.part, self.copies, self.here, self.n_dp = w, part, copies, here, n_dp
+        self.step, self.side, self.at = [], [], 0
+        self.stages = [self.dp_first, self.hop] if dp_first else [self.first, self.dp_second]
+        self.stages += [self.last, self.twin, self.done]
+
+    def advance(self):
+        self.stages[self.at]()
+        self.at += 1
 
     def same(self, ref, to):
         return self.copies.put(ref, ref, to)
 
-    def along_dp(self, n_dp):
+    def low(self, d, a, b, core):
+        return self.w.at[d, a, b, core, self.part.rows, self.part.low]
+
+    def high(self, d, a, b, core):
+        return self.w.at[d, a, b, core, self.part.rows, self.part.high]
+
+    def first(self):
         i = self.here
-        self.step = []
-        for own, w in zip(self.owns, self.wholes):
-            w[i.d, i.a, i.b, i.core] = own[...]
-            ref = w.at[i.d, i.a, i.b, i.core]
-            self.step += [self.same(ref, (p, i.c)) for p in peers(n_dp, i.d)]
-
-    def first_hop(self):
+        self.step = [self.same(self.low(i.d, i.a, i.b, i.core), i.over_b), self.same(self.high(i.d, i.a, i.b, i.core), i.over_a)]
+
+    def dp_second(self):
         i = self.here
         arrive(self.step)
         self.step = []
-        for w in self.wholes:
-            low, high = halves(w)
-            self.step.append(self.same(w.at[:, i.a, i.b, i.core, :, low], i.over_b))
-            self.step.append(self.same(w.at[:, i.a, i.b, i.core, :, high], i.over_a))
-        self.side += [self.same(w.at[:, i.a, i.b, i.core], i.twin) for w in self.wholes]
-
-    def second_hop(self):
+        for p in peers(self.n_dp, i.d):
+            self.step.append(self.same(self.low(i.d, i.a, slice(None), i.core), (p, i.c)))
+            self.step.append(self.same(self.high(i.d, slice(None), i.b, i.core), (p, i.c)))
+
+    def dp_first(self):
         i = self.here
+        own = self.w.at[i.d, i.a, i.b, i.core, self.part.rows, self.part.all]
+        self.step = [self.same(own, (p, i.c)) for p in peers(self.n_dp, i.d)]
+
+    def hop(self):
+        i, every = self.here, slice(None)
+        arrive(self.step)
+        self.step = [self.same(self.low(every, i.a, i.b, i.core), i.over_b), self.same(self.high(every, i.a, i.b, i.core), i.over_a)]
+
+    def last(self):
+        i, every = self.here, slice(None)
+        arrive(self.step)
+        low, high = self.low(every, i.a, every, i.core), self.high(every, every, i.b, i.core)
+        self.step = [self.same(low, i.over_a), self.same(high, i.over_b)]
+        self.side = [self.same(low, i.twin), self.same(high, i.twin)]
+
+    def twin(self):
+        i, every = self.here, slice(None)
+        arrive(self.step)
+        self.side += [self.same(self.low(every, 1 - i.a, every, i.core), i.twin), self.same(self.high(every, every, 1 - i.b, i.core), i.twin)]
+
+    def done(self):
+        arrive(self.side)
+
+
+class Scatter:
+    def __init__(self, g, part, dp_last, boxes, out, copies, here, n_dp):
+        self.g, self.part, self.out, self.copies, self.here, self.n_dp = g, part, out, copies, here, n_dp
+        self.box, self.low_box, self.high_box, *self.more = boxes
+        self.step, self.at = [], 0
+        self.stages = [self.to_twin, self.add_twin]
+        self.stages += [self.hop, self.dp_last, self.done_last] if dp_last else [self.dp, self.hop_last, self.done]
+
+    def advance(self):
+        self.stages[self.at]()
+        self.at += 1
+
+    def put(self, src, dst, to):
+        self.step.append(self.copies.put(src, dst, to))
+
+    def arrived(self):
         arrive(self.step)
         self.step = []
-        for w in self.wholes:
-            low, high = halves(w)
-            self.step.append(self.same(w.at[:, i.a, :, i.core, :, low], i.over_a))
-            self.step.append(self.same(w.at[:, :, i.b, i.core, :, high], i.over_b))
-        for w in self.wholes:
-            low, high = halves(w)
-            self.side.append(self.same(w.at[:, i.a, 1 - i.b, i.core, :, low], i.twin))
-            self.side.append(self.same(w.at[:, 1 - i.a, i.b, i.core, :, high], i.twin))
-
-    def last_hop(self):
+
+    def to_twin(self):
+        i, every = self.here, slice(None)
+        self.put(self.g.at[every, every, every, 1 - i.core, self.part.rows, self.part.all], self.box, i.twin)
+
+    def add_twin(self):
+        i, part, box = self.here, self.part, self.box
+        self.arrived()
+        half = box.shape[-1] // 2
+
+        def add(n, _):
+            for a in range(2):
+                for b in range(2):
+                    own = self.g[n, a, b, i.core, part.rows, part.all]
+                    box[n, a, b] = (box[n, a, b].astype(F32) + own.astype(F32)).astype(BF16)
+            return 0
+        lax.fori_loop(0, box.shape[0], add, 0)
+        self.put(box.at[:, 1 - i.a, :, :, pl.ds(0, half)], self.low_box, i.over_a)
+        self.put(box.at[:, :, 1 - i.b, :, pl.ds(half, half)], self.high_box, i.over_b)
+
+    def add_hop(self):
+        i, box, low_box, high_box = self.here, self.box, self.low_box, self.high_box
+        self.arrived()
+        half = box.shape[-1] // 2
+
+        def add(n, _):
+            for k in range(2):
+                low_box[n, k] = (low_box[n, k].astype(F32) + box[n, i.a, k, :, :half].astype(F32)).astype(BF16)
+                high_box[n, k] = (high_box[n, k].astype(F32) + box[n, k, i.b, :, half:].astype(F32)).astype(BF16)
+            return 0
+        lax.fori_loop(0, box.shape[0], add, 0)
+
+    def hop(self):
         i = self.here
-        arrive(self.step)
-        for w in self.wholes:
-            low, high = halves(w)
-            self.side.append(self.same(w.at[:, 1 - i.a, :, i.core, :, low], i.twin))
-            self.side.append(self.same(w.at[:, :, 1 - i.b, i.core, :, high], i.twin))
-
-    def finish(self):
-        arrive(self.side)
-
-
-class Scatter:
-    def __init__(self, grads, boxes, copies, here):
-        self.grads, self.copies, self.here = grads, copies, here
-        self.twins, self.lows, self.highs, self.low2s, self.high2s, self.lasts = boxes
-        self.first = []
-        self.step = []
-
-    def to_twin(self, k):
+        low2, high2, _low3, _high3 = self.more
+        self.add_hop()
+        self.put(self.low_box.at[:, 1 - i.b], low2, i.over_b)
+        self.put(self.high_box.at[:, 1 - i.a], high2, i.over_a)
+
+    def dp_last(self):
         i = self.here
-        self.first.append(self.copies.put(self.grads[k].at[:, :, :, 1 - i.core], self.twins[k], i.twin))
-
-    def add_twin(self):
+        low2, high2, low3, high3 = self.more
+        self.arrived()
+        for n in range(self.n_dp):
+            low2[n] = (low2[n].astype(F32) + self.low_box[n, i.b].astype(F32)).astype(BF16)
+            high2[n] = (high2[n].astype(F32) + self.high_box[n, i.a].astype(F32)).astype(BF16)
+        for p in peers(self.n_dp, i.d):
+            self.put(low2.at[p], low3.at[i.d], (p, i.c))
+            self.put(high2.at[p], high3.at[i.d], (p, i.c))
+
+    def done_last(self):
         i = self.here
-        arrive(self.first)
-        for g, t in zip(self.grads, self.twins):
-            def add(n, _):
-                for a in range(2):
-                    for b in range(2):
-                        t[n, a, b] = (t[n, a, b].astype(F32) + g[n, a, b, i.core].astype(F32)).astype(BF16)
-                return 0
-            lax.fori_loop(0, t.shape[0], add, 0)
-        for t, low_box, high_box in zip(self.twins, self.lows, self.highs):
-            low, high = halves(t)
-            self.step.append(self.copies.put(t.at[:, 1 - i.a, :, :, low], low_box, i.over_a))
-            self.step.append(self.copies.put(t.at[:, :, 1 - i.b, :, high], high_box, i.over_b))
-
-    def add_first(self):
+        low2, high2, low3, high3 = self.more
+        self.arrived()
+        for own, box, cols in ((low2, low3, self.part.low), (high2, high3, self.part.high)):
+            total = own[i.d].astype(F32)
+            for p in peers(self.n_dp, i.d):
+                total = total + box[p].astype(F32)
+            self.out[self.part.rows, cols] = total
+
+    def dp(self):
         i = self.here
-        arrive(self.step)
-        self.step = []
-        for t, low_box, high_box in zip(self.twins, self.lows, self.highs):
-            low, high = halves(t)
-            def add(n, _):
-                for k in range(2):
-                    low_box[n, k] = (low_box[n, k].astype(F32) + t[n, i.a, k, :, low].astype(F32)).astype(BF16)
-                    high_box[n, k] = (high_box[n, k].astype(F32) + t[n, k, i.b, :, high].astype(F32)).astype(BF16)
-                return 0
-            lax.fori_loop(0, t.shape[0], add, 0)
-        for low_box, high_box, low2, high2 in zip(self.lows, self.highs, self.low2s, self.high2s):
-            self.step.append(self.copies.put(low_box.at[:, 1 - i.b], low2, i.over_b))
-            self.step.append(self.copies.put(high_box.at[:, 1 - i.a], high2, i.over_a))
-
-    def add_second(self, n_dp):
+        low2, high2, _low3, _high3 = self.more
+        self.add_hop()
+        for p in peers(self.n_dp, i.d):
+            self.put(self.low_box.at[p], low2.at[i.d], (p, i.c))
+            self.put(self.high_box.at[p], high2.at[i.d], (p, i.c))
+
+    def hop_last(self):
         i = self.here
-        arrive(self.step)
-        self.step = []
-        for low_box, high_box, low2, high2, last in zip(self.lows, self.highs, self.low2s, self.high2s, self.lasts):
-            low, high = halves(last)
-            for n in range(n_dp):
-                low2[n] = (low2[n].astype(F32) + low_box[n, i.b].astype(F32)).astype(BF16)
-                high2[n] = (high2[n].astype(F32) + high_box[n, i.a].astype(F32)).astype(BF16)
-            for p in peers(n_dp, i.d):
-                self.step.append(self.copies.put(low2.at[p], last.at[i.d, :, low], (p, i.c)))
-                self.step.append(self.copies.put(high2.at[p], last.at[i.d, :, high], (p, i.c)))
-
-    def finish(self, outs, n_dp):
-        i = self.here
-        arrive(self.step)
-        for low2, high2, last, out in zip(self.low2s, self.high2s, self.lasts, outs):
-            low, high = halves(last)
-            for cut, box in ((low, low2), (high, high2)):
-                total = box[i.d].astype(F32)
-                for p in peers(n_dp, i.d):
-                    total = total + last[p, :, cut].astype(F32)
-                out[:, cut] = total
+        low2, high2, low3, high3 = self.more
+        self.arrived()
+        for first, box, other, own, cols, to in (
+            (self.low_box, low2, low3, i.b, self.part.low, i.over_b), (self.high_box, high2, high3, i.a, self.part.high, i.over_a),
+        ):
+            def total(k):
+                x = first[i.d, k].astype(F32)
+                for p in peers(self.n_dp, i.d):
+                    x = x + box[p, k].astype(F32)
+                return x
+            self.out[self.part.rows, cols] = total(own)
+            other[0] = total(1 - own).astype(BF16)
+            self.put(other.at[0], other.at[1], to)
+
+    def done(self):
+        _low2, _high2, low3, high3 = self.more
+        self.arrived()
+        for box, cols in ((low3, self.part.low), (high3, self.part.high)):
+            self.out[self.part.rows, cols] += box[1].astype(F32)
+
+
+def scatter_boxes(size, dp_last):
+    r, k = size
+    half = (r, k // 2)
+    boxes = [(4, 2, 2, r, k), (4, 2) + half, (4, 2) + half]
+    return boxes + ([(4,) + half] * 4 if dp_last else [(4, 2) + half] * 2 + [(2,) + half] * 2)
 
 
 def wide(vec_ref, first, count):
@@ -642,10 +757,9 @@
 
 
 def dense_up(m, t, tokens, act, w_out, w_in, vec, keeps):
-    middle, gate_ref, gated_ref, second, hidden, slopes = keeps
+    middle, gate_ref, gated_ref, second, _hidden, _slopes = keeps
     at = row_block(m, t)
     feats = tokens.shape[1]
-    tile = w_in.shape[-1] // 4
     project = tn(act[:, :, at].reshape(feats, t), flat(w_out[...])) + wide(vec, 0, 2 * feats // 128)
     gate = jax.nn.sigmoid(project[:, feats:])
     gated = project[:, :feats] * gate
@@ -656,7 +770,15 @@
     n, _scale = layer_stats(total)
     after = (n * wide(vec, 12, feats // 128)).astype(BF16)
     second[at, :] = after
-    for f in range(4):
+    dense_hidden(m, t, (0, 1), w_in, vec, keeps)
+
+
+def dense_hidden(m, t, tiles, w_in, vec, keeps):
+    _middle, _gate_ref, _gated_ref, second, hidden, slopes = keeps
+    at = row_block(m, t)
+    tile = w_in.shape[-1] // 4
+    after = second[at, :]
+    for f in tiles:
         cols = slice(f * tile, (f + 1) * tile)
         before = nn(after, flat(w_in[:, :, :, :, :, cols])) + wide(vec, 16 + f * tile // 128, tile // 128)
         high, slope = gelu_pair(before)
@@ -710,6 +832,35 @@
     lax.fori_loop(0, 4, one, 0)
 
 
+PART_NAMES = ("o", "i", "j", "b", "c")
+GATHER_DP_FIRST = (False, False, False, False, True)
+SCATTER_DP_LAST = (True, False, True, False, False)
+SCHEDULE = {
+    "greeted": "gc go gi gj gb",
+    "sent": "go gi gc",
+    "tables": "go gj",
+    "f0c": "gb",
+    "f1b": "gi",
+    "f1c": "go",
+    "f3c": "gj gc gi",
+    "act": "go gi",
+    "up0": "gb",
+    "up2": "gj gj",
+    "hid1": "gc",
+    "g_back": "sb sc gb gc gb",
+    "pre0": "sb sc",
+    "g_in": "si sj sb",
+    "g_out": "so sc si sj so",
+    "b0d": "si sb sc",
+    "b1a": "sj",
+    "b1d": "so",
+    "b2d": "sj si",
+    "b3b": "so",
+    "tail": "sb sc si",
+    "rows": "sj so",
+}
+
+
 def whole_kernel(dims, n_dp, direct, *refs):
     nj, chans, mb, h = dims
     refs = list(refs)
@@ -717,13 +868,15 @@
         out = refs[:n]
         del refs[:n]
         return out
-    tokens, cot, lengths, log_step, skip_row, *mode_parts = take(9)
+    tokens_in, cot_in, lengths, log_step, skip_row, *mode_parts = take(9)
     vectors = take(4)
+    waves = take(2)
     given = take(3)
-    block_out, grad_tokens = take(2)
+    block_out_to, grad_tokens_to = take(2)
     g_step, g_skip, *g_modes = take(6)
     g_vectors = take(4)
-    results = take(3)
+    results_to = take(3)
+    tokens, cot, block_out, grad_tokens = take(4)
     u, snd, act, out, ga, gn, slope, carry = take(8)
     second, hidden, gb, gp = take(4)
     keeps = take(4)
@@ -731,8 +884,8 @@
     keeps = keeps[:3] + [second, hidden] + keeps[3:]
     vec_dp, vec_chan, vec2_dp, vec2_chan, modes_dp, zw_dp, ng_dp, ng_chan = take(8)
     modes, vec, sums, skip, gain, mode_rows_box = take(6)
-    pw, xs, ys, gy, sc = take(5)
-    box_sems, in_sems, out_sems, back_sems, gn_sems = take(5)
+    pw, xs, ys, gy, sc, lags, toep, state_tab, read_tab = take(9)
+    box_sems, in_sems, out_sems, back_sems, gn_sems, own_sems = take(6)
     d, c = lax.axis_index("dp"), lax.axis_index("chan")
     here = (d, c)
     shards, shard = n_dp * nj, d * nj + c
@@ -754,27 +907,39 @@
     zw_all, ng_first, ng_second = along_dp(zw_dp, 5), along_dp(ng_dp, 6), along_chan(ng_chan, 7)
     if direct:
         wholes, grads = take(3), take(3)
-        boxes = [take(3) for _ in range(6)]
+        results = take(3)
+        places = parts_of(*wholes)
+        boxes = [take(7) for _ in places]
         place = Place(d, c)
         gather_copies, scatter_copies = Copies(refs[0]), Copies(refs[1])
-        early = Gather(given[:2], wholes[:2], gather_copies, place)
-        late = Gather(given[2:], wholes[2:], gather_copies, place)
-        rest = Scatter(grads[:2], [b[:2] for b in boxes], scatter_copies, place)
-        ahead = Scatter(grads[2:], [b[2:] for b in boxes], scatter_copies, place)
+        parts = {}
+        for (k, part), dp_first, dp_last, name, each in zip(places, GATHER_DP_FIRST, SCATTER_DP_LAST, PART_NAMES, boxes):
+            parts["g" + name] = Gather(wholes[k], part, dp_first, gather_copies, place, n_dp)
+            parts["s" + name] = Scatter(grads[k], part, dp_last, each, results[k], scatter_copies, place, n_dp)
     else:
-        wholes, grads = given, results
+        wholes, grads = given, results_to
     g_out, g_in, g_back = grads
+
+    def poll(point):
+        if direct:
+            for name in SCHEDULE.get(point, "").split():
+                parts[name].advance()
+
+    def fetch(src, dst, n):
+        copy = pltpu.make_async_copy(src, dst, own_sems.at[n])
+        copy.start()
+        return copy
+    fetched = [fetch(tokens_in, tokens, 0)]
+    if direct:
+        fetched += [fetch(own, w.at[d, place.a, place.b, place.core], 2 + k) for k, (own, w) in enumerate(zip(given, wholes))]
+    fetched.append(fetch(cot_in, cot, 1))
 
     for k, (own, first) in enumerate(zip(vectors, (0, 8, 12, 16))):
         put_own(vec_dp.at[d], first, own[...].astype(F32), shard, shards)
     for a in range(4):
         modes_dp[d, a] = padded(mode_parts[a][...])
     greet(n_dp, nj, d, c)
-    vec_first.start()
-    modes_all.start()
-    if direct:
-        early.along_dp(n_dp)
-        late.along_dp(n_dp)
+    fetched[0].wait()
 
     def normalize(m, _):
         at = row_block(m, t)
@@ -782,6 +947,13 @@
         snd[:, :, at] = n.T.astype(BF16).reshape(nj, chans, t)
         return 0
     lax.fori_loop(0, mb, normalize, 0)
+    be_greeted(n_dp, nj)
+    vec_first.start()
+    modes_all.start()
+    if direct:
+        for copy in fetched[1:4]:
+            copy.wait()
+    poll("greeted")
 
     def share(box, where, sems, q):
         for p in peers(nj, c):
@@ -793,6 +965,7 @@
 
     for q in range(packs):
         share(snd, u, in_sems, q)
+    poll("sent")
     sums[...] = jnp.zeros(sums.shape, F32)
     sc[...] = jnp.zeros(sc.shape, F32)
     skip[...] = to_column(skip_row[...])
@@ -809,6 +982,9 @@
     kinds += [jnp.concatenate([modes_dp[p, a] for p in range(n_dp)], 0) for a in range(4)]
     spread_modes(jnp.concatenate(kinds, 0), modes)
     mode_prelude(modes, pw)
+    forward_tables(pw, groups, gb, toep)
+    poll("tables")
+    backward_tables(pw, groups, state_tab, read_tab)
     vec_second.wait()
     vec[...] = vec_second.total()
     for k in range(nj):
@@ -817,89 +993,70 @@
             first = k * chans
             row = vec[8 + first // 128:9 + first // 128, :]
             gain[...] = to_column(row[:, first % 128:first % 128 + chans])
-    if direct:
-        early.first_hop()
 
     for q in range(packs):
         shared(u, in_sems, q)
-        forward_pack(dims, q, skip, gain, span, u, out, slope, carry, pw, xs, ys, sc)
+        forward_pack(dims, q, skip, gain, span, gb, toep, u, out, slope, carry, pw, xs, ys, sc, poll)
         share(out, act, out_sems, q)
-        if direct:
-            if q == 0:
-                early.second_hop()
-                late.first_hop()
-            if q == 2:
-                early.last_hop()
-            if q == 3:
-                late.second_hop()
+        poll(f'f{q}c')
     for q in range(packs):
         shared(act, out_sems, q)
-    if direct:
-        early.finish()
-
-    def rows_up(m, _):
+    poll("act")
+    for m in range(mb):
         dense_up(m, t, tokens, act, wholes[0], wholes[1], vec, keeps)
-        return 0
-    lax.fori_loop(0, mb, rows_up, 0)
-    if direct:
-        late.last_hop()
+        poll(f"up{m}")
+    for m in range(mb):
+        dense_hidden(m, t, (2, 3), wholes[1], vec, keeps)
+        poll(f"hid{m}")
+    fetched[-1].wait()
     outer_products(hidden, cot, g_back)
-    if direct:
-        ahead.to_twin(0)
-        late.finish()
+    poll("g_back")
     for m in range(mb):
         dense_down(m, t, cot, wholes, vec, block_out, keeps, gb, gp, snd, sums)
+        poll(f"pre{m}")
         at = pl.ds(m * t, t)
         for p in peers(nj, c):
             send(snd.at[p, :, at], ga.at[c, :, at], back_sems.at[0, m], back_sems.at[1, m], (d, p))
         ga[c, :, at] = snd[c, :, at]
-        if direct and m == 0:
-            ahead.add_twin()
+        poll(f"down{m}")
+    written = [fetch(block_out, block_out_to, 5)]
     vec2_chan[c] = sums[...]
     sums_first.start()
     outer_products(second, gb, g_in)
-    if direct:
-        rest.to_twin(1)
+    poll("g_in")
     def outer(n, _):
         g_out[n] = shaped(nn(flat(act[pl.ds(n * (nj // 4), nj // 4)]), gp[...]), g_out)
         return 0
     lax.fori_loop(0, 4, outer, 0)
-    if direct:
-        rest.to_twin(0)
-        ahead.add_first()
+    poll("g_out")
     for m in range(mb):
         settle(ga.at[pl.ds(0, nj - 1), :, pl.ds(m * t, t)], back_sems.at[0, m], back_sems.at[1, m], here)
-    if direct:
-        rest.add_twin()
-
+    poll("ga")
     for q in range(packs):
-        backward_pack(dims, q, skip, gain, span, u, ga, slope, carry, out, zw_dp.at[d], ng_dp.at[d], pw, xs, gy, ys, sc)
+        backward_pack(dims, q, skip, gain, span, state_tab, read_tab, toep, waves, u, ga, slope, carry, out, zw_dp.at[d], ng_dp.at[d], pw, xs, gy, ys, sc, lags, poll)
         share(out, gn, gn_sems, q)
-        if q == 0:
+        poll(f'b{q}d')
+        if q == packs // 2:
             sums_first.wait()
             vec2_dp[d] = sums_first.total()
             sums_second.start()
-        if direct:
-            if q == 0:
-                ahead.add_second(n_dp)
-            if q == 1:
-                rest.add_first()
-            if q == 2:
-                rest.add_second(n_dp)
     zw_all.start()
     ng_first.start()
-    sums_second.wait()
-    sums[...] = sums_second.total()
-    for k, (first, own) in enumerate(zip((0, 8, 12, 16), g_vectors)):
-        if k != 1:
-            own[...] = pick_own(sums, first, own.shape[1], shard)
-    ng_first.wait()
-    ng_chan[c, 0:1, :] = padded(column_sum(ng_first.total().T))
-    ng_chan[c, 1:8, :] = jnp.zeros((7, 128), F32)
-    ng_second.start()
-    if direct:
-        ahead.finish(results[2:], n_dp)
-        rest.finish(results[:2], n_dp)
+    for q in range(packs):
+        shared(gn, gn_sems, q)
+    poll("tail")
+    wide_gain = wide(vec, 8, feats // 128)
+    for m in range(mb):
+        at = row_block(m, t)
+        n, scale = layer_stats(tokens[at, :].astype(F32))
+        grad = gn[:, :, at].reshape(feats, t).astype(F32).T
+        grad_tokens[at, :] = (middle[at, :] + layer_back(grad * wide_gain, n, scale)).astype(BF16)
+        if m == 0:
+            ng_first.wait()
+            ng_chan[c, 0:1, :] = padded(column_sum(ng_first.total().T))
+            ng_chan[c, 1:8, :] = jnp.zeros((7, 128), F32)
+            ng_second.start()
+    written.append(fetch(grad_tokens, grad_tokens_to, 6))
     zw_all.wait()
     zw = [sum(zw_dp[k, a] for k in range(n_dp)) for a in range(5)]
     found = list(mode_gradients([modes[a] for a in range(5)], zw)) + [zw[4]]
@@ -909,17 +1066,14 @@
     for a in range(4):
         each = g_modes[a].shape[0]
         g_modes[a][...] = mode_rows_box[pl.ds(32 * (a + 1) + d * each, each), :chans]
-    for q in range(packs):
-        shared(gn, gn_sems, q)
-    wide_gain = wide(vec, 8, feats // 128)
-
-    def finish_rows(m, _):
-        at = row_block(m, t)
-        n, scale = layer_stats(tokens[at, :].astype(F32))
-        grad = gn[:, :, at].reshape(feats, t).astype(F32).T
-        grad_tokens[at, :] = (middle[at, :] + layer_back(grad * wide_gain, n, scale)).astype(BF16)
-        return 0
-    lax.fori_loop(0, mb, finish_rows, 0)
+    sums_second.wait()
+    sums[...] = sums_second.total()
+    for k, (first, own) in enumerate(zip((0, 8, 12, 16), g_vectors)):
+        if k != 1:
+            own[...] = pick_own(sums, first, own.shape[1], shard)
+    poll("rows")
+    if direct:
+        written += [fetch(x, to, 7 + k) for k, (x, to) in enumerate(zip(results, results_to))]
     ng_second.wait()
     size = g_vectors[1].shape[1]
     start = shard * size
@@ -928,6 +1082,9 @@
     if direct:
         gather_copies.finish()
         scatter_copies.finish()
+        assert all(x.at == len(x.stages) for x in parts.values())
+    for copy in written:
+        copy.wait()
 
 
 def whole(tokens, cot, lengths, log_step, skip, mode_parts, vectors, weights, mb, n_dp, nj):
@@ -952,7 +1109,7 @@
     shapes += [shape(p, F32) for p in per] if direct else [shape(f, BF16) for f in full]
     dma, vm = pltpu.SemaphoreType.DMA, pltpu.VMEM
     sheet, grid = (32, 128), (groups, 128)
-    scratch = [vm((nj, chans, width), BF16)] * 6 + [
+    scratch = [vm((width, feats), BF16)] * 4 + [vm((nj, chans, width), BF16)] * 6 + [
         vm((packs, rows * PACK, 128), F32),
         vm((packs, 4, blocks * PACK, 128), F32),
         vm((width, feats), BF16), vm((width, ff), BF16), vm((width, ff), BF16), vm((width, 2 * feats), BF16),
@@ -964,26 +1121,26 @@
         vm((18,) + grid, F32),
         vm((rows * PACK, 128), F32), vm((rows * PACK, 128), F32), vm((rows * PACK, 128), F32),
         vm((4, blocks * PACK, 128), F32),
-        dma((8, 2)), dma((2, packs)), dma((2, packs)), dma((2, mb)), dma((2, packs)),
+        vm((PACK, 128), F32), vm((chans, SPAN, 128), BF16), vm((groups, SPAN, 512), BF16), vm((groups, SPAN, 256), BF16),
+        dma((8, 2)), dma((2, packs)), dma((2, packs)), dma((2, mb)), dma((2, packs)), dma((10,)),
     ]
     if direct:
-        half = [(r, k // 2) for r, k in per]
-        scratch += [vm(f, BF16) for f in full] * 2
-        scratch += [vm((4, 2, 2) + p, BF16) for p in per]
-        scratch += [vm((4, 2) + p, BF16) for p in half] * 2
-        scratch += [vm((4,) + p, BF16) for p in half] * 2
-        scratch += [vm((4,) + p, BF16) for p in per]
-        scratch += [dma((2, 42)), dma((2, 33))]
-    vmem = pl.BlockSpec(memory_space=pltpu.VMEM)
+        scratch += [vm(f, BF16) for f in full] * 2 + [vm(p, F32) for p in per]
+        (r0, k0), (r1, k1), (r2, k2) = per
+        sizes = [(r0, k0), (r1, k1 // 2), (r1, k1 // 2), (r2 // 2, k2), (r2 // 2, k2)]
+        for size, dp_last in zip(sizes, SCATTER_DP_LAST):
+            scratch += [vm(x, BF16) for x in scatter_boxes(size, dp_last)]
+        scratch += [dma((2, 70)), dma((2, 55))]
+    vmem, anywhere = pl.BlockSpec(memory_space=pltpu.VMEM), pl.BlockSpec(memory_space=pl.ANY)
     outs = pl.pallas_call(
         functools.partial(whole_kernel, (nj, chans, mb, h), n_dp, direct),
         out_shape=shapes,
-        in_specs=[vmem] * 16,
-        out_specs=[vmem] * len(shapes),
+        in_specs=[anywhere] * 2 + [vmem] * 13 + [anywhere if direct else vmem] * 3,
+        out_specs=[anywhere] * 2 + [vmem] * 10 + [anywhere if direct else vmem] * 3,
         scratch_shapes=scratch,
-        compiler_params=pltpu.CompilerParams(collective_id=0, has_side_effects=True, vmem_limit_bytes=62 << 20),
+        compiler_params=pltpu.CompilerParams(collective_id=0, has_side_effects=True, vmem_limit_bytes=63 << 20),
         name="whole",
-    )(tokens, cot, lengths, log_step, skip, *mode_parts, *vectors, *weights)
+    )(tokens, cot, lengths, log_step, skip, *mode_parts, *vectors, *(jnp.asarray(x) for x in wave_tables()), *weights)
     if direct:
         return deliver(outs)
     outs, grads = outs[:12], outs[12:]
@@ -992,12 +1149,16 @@
 
 
 def deliver_kernel(*refs):
-    n = (len(refs) - 1) // 2
+    n = (len(refs) - 1) // 3
     sems = refs[-1]
-    copies = [pltpu.make_async_copy(refs[k], refs[n + k], sems.at[k]) for k in range(n)]
-    for copy in copies:
+    first = [pltpu.make_async_copy(refs[k], refs[2 * n + k], sems.at[0, k]) for k in range(n)]
+    last = [pltpu.make_async_copy(refs[2 * n + k], refs[n + k], sems.at[1, k]) for k in range(n)]
+    for copy in first:
         copy.start()
-    for copy in copies:
+    for one, two in zip(first[::-1], last[::-1]):
+        one.wait()
+        two.start()
+    for copy in last:
         copy.wait()
 
 
@@ -1006,9 +1167,9 @@
     return list(pl.pallas_call(
         deliver_kernel,
         out_shape=[jax.ShapeDtypeStruct(x.shape, x.dtype) for x in arrays],
-        in_specs=[pl.BlockSpec(memory_space=pltpu.VMEM)] * len(arrays),
+        in_specs=[anywhere] * len(arrays),
         out_specs=[anywhere] * len(arrays),
-        scratch_shapes=[pltpu.SemaphoreType.DMA((len(arrays),))],
+        scratch_shapes=[pltpu.VMEM(x.shape, x.dtype) for x in arrays] + [pltpu.SemaphoreType.DMA((2, len(arrays)))],
         name="deliver",
     )(*arrays))
 

time: 126 us -> 112 us (0.89)
  Pallas kernels: 125 us -> 111 us
    pallas_call x1, Pallas kernels: 122 us -> 107 us  [whole(): pl.pallas_call(functools.partial(whole_kernel, (nj, chans, mb, h), n_dp,...]
where the time goes in v5:
time: 112 us; the launch traced here: 111 us
  Pallas kernels  111 us (99%)
    pallas_call x1, Pallas kernels, whole(): pl.pallas_call(functools.partial(whole_kernel, (nj, chans, mb, h), n_dp,...  107 us
    pallas_call x1, Pallas kernels, deliver(): pl.pallas_call(deliver_kernel, out_shape=[jax.ShapeDtypeStruct(x.shape, x...  3.07 us

profile of v5, /device:TPU:0, one launch (start us, length us, event | category | flops | bytes accessed | tf_op | source)
XLA Modules:
  0.0 111.3 jit_solution(7350968124612025669)
XLA Ops:
  0.7 107.4 %whole.1 = (bf16[768,512]{1,0:T(8,128)(2,1)}, bf16[768,512]{1,0:T(8,128)(2,1)}, f32[1,64]{1,0:T(1,128)}, f32[1,64]{1,0:T(1,128)}, f32[8,64]{1,0:T(8,128)}, /*ind...) custom-call(bf16[768,512]{1,0:T(8,128)(2,1)} %bitcast.25, ...), custom_call_target="tpu_custom_call" | custom-call | tf_op jit(solution)/shard_map/whole/pallas_call | solution.py:1135
  108.1 3.1 %deliver.1 = (bf16[768,512]{1,0:T(8,128)(2,1)}, bf16[768,512]{1,0:T(8,128)(2,1)}, f32[1,64]{1,0:T(1,128)}, f32[1,64]{1,0:T(1,128)}, f32[8,64]{1,0:T(8,128)}, /*i...) custom-call(bf16[768,512]{1,0:T(8,128)(2,1)} %get-tuple-element.45.r, ...), custom_call_target="tpu_custom_call" | custom-call | tf_op jit(solution)/shard_map/deliver/pallas_call | solution.py:1167

commit v6 on v5

--- a/solution.py
+++ b/solution.py
@@ -796,15 +796,13 @@
     total = middle[at, :]
     n, scale = layer_stats(total)
     gain = wide(vec, 12, feats // 128)
-    back = jnp.zeros((t, feats), F32)
     for f in range(4):
         cols = slice(f * tile, (f + 1) * tile)
-        wb = flat(w_back[f])
-        low = (slopes[at, cols] * nt(up, wb)).astype(BF16)
+        low = (slopes[at, cols] * nt(up, flat(w_back[f]))).astype(BF16)
         gb[at, cols] = low
         add_wide(sums, 16 + f * tile // 128, column_sum(low.astype(F32)))
-        total = total + nn(hidden[at, cols], wb)
-        back = back + nt(low, flat(w_in[:, :, :, :, :, cols]))
+    total = total + nn(hidden[at, :], flat(w_back[...]))
+    back = nt(gb[at, :], flat(w_in[...]))
     block_out[at, :] = total.astype(BF16)
     add_wide(sums, 12, column_sum(back * n))
     grad = up.astype(F32) + layer_back(back * gain, n, scale)
@@ -836,28 +834,29 @@
 GATHER_DP_FIRST = (False, False, False, False, True)
 SCATTER_DP_LAST = (True, False, True, False, False)
 SCHEDULE = {
-    "greeted": "gc go gi gj gb",
-    "sent": "go gi gc",
-    "tables": "go gj",
-    "f0c": "gb",
-    "f1b": "gi",
-    "f1c": "go",
-    "f3c": "gj gc gi",
-    "act": "go gi",
-    "up0": "gb",
-    "up2": "gj gj",
-    "hid1": "gc",
-    "g_back": "sb sc gb gc gb",
-    "pre0": "sb sc",
-    "g_in": "si sj sb",
-    "g_out": "so sc si sj so",
-    "b0d": "si sb sc",
-    "b1a": "sj",
-    "b1d": "so",
-    "b2d": "sj si",
-    "b3b": "so",
-    "tail": "sb sc si",
-    "rows": "sj so",
+    "greeted": ("gc", "go", "gi", "gj", "gb"),
+    "sent": ("go", "gi", "gc"),
+    "tables": ("go", "gj"),
+    "f0c": ("gb",),
+    "f1b": ("gi",),
+    "f1c": ("go",),
+    "f3c": ("gj", "gc", "gi"),
+    "act": ("go", "gi"),
+    "up0": ("gb",),
+    "up2": ("gj", "gj"),
+    "hid1": ("gc",),
+    "g_back": ("sb", "sc", "sb", "sc", "gb", "gc", "gb"),
+    "g_in": ("si", "sj"),
+    "g_out": ("si", "so", "sj", "so"),
+    "b0d": ("si", "sb", "sc"),
+    "b1a": ("sj",),
+    "b1d": ("so",),
+    "b2d": ("sj", "si"),
+    "zw": ("so",),
+    "tail": ("sb", "sc", "si"),
+    "rows": ("sj", "so"),
+    "down0": ("sb",),
+    "down1": ("sc",),
 }
 
 
@@ -922,7 +921,7 @@
 
     def poll(point):
         if direct:
-            for name in SCHEDULE.get(point, "").split():
+            for name in SCHEDULE.get(point, ()):
                 parts[name].advance()
 
     def fetch(src, dst, n):
@@ -1042,21 +1041,7 @@
             sums_second.start()
     zw_all.start()
     ng_first.start()
-    for q in range(packs):
-        shared(gn, gn_sems, q)
-    poll("tail")
-    wide_gain = wide(vec, 8, feats // 128)
-    for m in range(mb):
-        at = row_block(m, t)
-        n, scale = layer_stats(tokens[at, :].astype(F32))
-        grad = gn[:, :, at].reshape(feats, t).astype(F32).T
-        grad_tokens[at, :] = (middle[at, :] + layer_back(grad * wide_gain, n, scale)).astype(BF16)
-        if m == 0:
-            ng_first.wait()
-            ng_chan[c, 0:1, :] = padded(column_sum(ng_first.total().T))
-            ng_chan[c, 1:8, :] = jnp.zeros((7, 128), F32)
-            ng_second.start()
-    written.append(fetch(grad_tokens, grad_tokens_to, 6))
+    poll("zw")
     zw_all.wait()
     zw = [sum(zw_dp[k, a] for k in range(n_dp)) for a in range(5)]
     found = list(mode_gradients([modes[a] for a in range(5)], zw)) + [zw[4]]
@@ -1066,6 +1051,22 @@
     for a in range(4):
         each = g_modes[a].shape[0]
         g_modes[a][...] = mode_rows_box[pl.ds(32 * (a + 1) + d * each, each), :chans]
+    ng_first.wait()
+    ng_chan[c, 0:1, :] = padded(column_sum(ng_first.total().T))
+    ng_chan[c, 1:8, :] = jnp.zeros((7, 128), F32)
+    ng_second.start()
+    for q in range(packs):
+        shared(gn, gn_sems, q)
+    poll("tail")
+    if direct:
+        written.append(fetch(results[2], results_to[2], 9))
+    wide_gain = wide(vec, 8, feats // 128)
+    for m in range(mb):
+        at = row_block(m, t)
+        n, scale = layer_stats(tokens[at, :].astype(F32))
+        grad = gn[:, :, at].reshape(feats, t).astype(F32).T
+        grad_tokens[at, :] = (middle[at, :] + layer_back(grad * wide_gain, n, scale)).astype(BF16)
+    written.append(fetch(grad_tokens, grad_tokens_to, 6))
     sums_second.wait()
     sums[...] = sums_second.total()
     for k, (first, own) in enumerate(zip((0, 8, 12, 16), g_vectors)):
@@ -1073,7 +1074,7 @@
             own[...] = pick_own(sums, first, own.shape[1], shard)
     poll("rows")
     if direct:
-        written += [fetch(x, to, 7 + k) for k, (x, to) in enumerate(zip(results, results_to))]
+        written += [fetch(x, to, 7 + k) for k, (x, to) in enumerate(zip(results[:2], results_to))]
     ng_second.wait()
     size = g_vectors[1].shape[1]
     start = shard * size
@@ -1149,27 +1150,22 @@
 
 
 def deliver_kernel(*refs):
-    n = (len(refs) - 1) // 3
+    n = (len(refs) - 1) // 2
     sems = refs[-1]
-    first = [pltpu.make_async_copy(refs[k], refs[2 * n + k], sems.at[0, k]) for k in range(n)]
-    last = [pltpu.make_async_copy(refs[2 * n + k], refs[n + k], sems.at[1, k]) for k in range(n)]
-    for copy in first:
+    copies = [pltpu.make_async_copy(refs[k], refs[n + k], sems.at[k]) for k in range(n)]
+    for copy in copies:
         copy.start()
-    for one, two in zip(first[::-1], last[::-1]):
-        one.wait()
-        two.start()
-    for copy in last:
+    for copy in copies:
         copy.wait()
 
 
 def deliver(arrays):
-    anywhere = pl.BlockSpec(memory_space=pl.ANY)
     return list(pl.pallas_call(
         deliver_kernel,
         out_shape=[jax.ShapeDtypeStruct(x.shape, x.dtype) for x in arrays],
-        in_specs=[anywhere] * len(arrays),
-        out_specs=[anywhere] * len(arrays),
-        scratch_shapes=[pltpu.VMEM(x.shape, x.dtype) for x in arrays] + [pltpu.SemaphoreType.DMA((2, len(arrays)))],
+        in_specs=[pl.BlockSpec(memory_space=pltpu.VMEM)] * len(arrays),
+        out_specs=[pl.BlockSpec(memory_space=pl.ANY)] * len(arrays),
+        scratch_shapes=[pltpu.SemaphoreType.DMA((len(arrays),))],
         name="deliver",
     )(*arrays))
 

time: 112 us -> 107 us (0.955)
  Pallas kernels: 111 us -> 106 us
    pallas_call x1, Pallas kernels: 107 us -> 103 us  [whole(): pl.pallas_call(functools.partial(whole_kernel, (nj, chans, mb, h), n_dp,...]
where the time goes in v6:
time: 107 us; the launch traced here: 106 us
  Pallas kernels  106 us (99%)
    pallas_call x1, Pallas kernels, whole(): pl.pallas_call(functools.partial(whole_kernel, (nj, chans, mb, h), n_dp,...  103 us
    pallas_call x1, Pallas kernels, deliver(): pl.pallas_call(deliver_kernel, out_shape=[jax.ShapeDtypeStruct(x.shape, x...  2.93 us

profile of v6, /device:TPU:0, one launch (start us, length us, event | category | flops | bytes accessed | tf_op | source)
XLA Modules:
  0.0 106.4 jit_solution(15856146595560361377)
XLA Ops:
  0.7 102.6 %whole.1 = (bf16[768,512]{1,0:T(8,128)(2,1)}, bf16[768,512]{1,0:T(8,128)(2,1)}, f32[1,64]{1,0:T(1,128)}, f32[1,64]{1,0:T(1,128)}, f32[8,64]{1,0:T(8,128)}, /*ind...) custom-call(bf16[768,512]{1,0:T(8,128)(2,1)} %bitcast.25, ...), custom_call_target="tpu_custom_call" | custom-call | tf_op jit(solution)/shard_map/whole/pallas_call | solution.py:1136
  103.3 2.9 %deliver.1 = (bf16[768,512]{1,0:T(8,128)(2,1)}, bf16[768,512]{1,0:T(8,128)(2,1)}, f32[1,64]{1,0:T(1,128)}, f32[1,64]{1,0:T(1,128)}, f32[8,64]{1,0:T(8,128)}, /*i...) custom-call(bf16[768,512]{1,0:T(8,128)(2,1)} %get-tuple-element.45.r, ...), custom_call_target="tpu_custom_call" | custom-call | tf_op jit(solution)/shard_map/deliver/pallas_call | solution.py:1163
